TPU v7x, 128 devices: a whole 4x4x4 slice. The times are simulated.
128 devices in a mesh: lat: 4 (over z_hi, core), lon: 32 (over x, y, z_lo).
Axes of the slice: x: 4, y: 4, z: 4 (z_hi: 2, z_lo: 2; z = z_hi * 2 + z_lo), core: 2. Of those that a mesh axis runs over, the one named last changes fastest.
Arguments:
- pixels: bfloat16 [4, 24, 768, 500], P(None, 'lat', 'lon'), may hold values from -6 to 6
- land_patch_mask: int32 [24, 768], P('lat', 'lon'), may hold values 0 or 1
- region: int32 [2, 4, 64], P(None, 'lat', 'lon'), may hold values from 0 to 31
- patch_embed_weight: bfloat16 [500, 512], replicated, may hold values from -0.25 to 0.25
- patch_embed_bias: float32 [512], replicated, may hold values from -4 to 4
- land_embedding_vector: float32 [512], replicated, may hold values from -4 to 4
- attention_norm_gain: float32 [512], replicated, may hold values from 0.1 to 1.9
- query_key_value_weight: bfloat16 [512, 1536], replicated, may hold values from -0.25 to 0.25
- region_down_factor: bfloat16 [32, 8, 512], replicated, may hold values from -0.25 to 0.25
- region_up_factor: bfloat16 [32, 8, 1536], replicated, may hold values from -2 to 2
- head_logit_scale: float32 [16], replicated, may hold values from 1 to 10
- attention_output_weight: bfloat16 [512, 512], replicated, may hold values from -0.25 to 0.25
- feedforward_gain: float32 [512], replicated, may hold values from 0.1 to 1.9
- feedforward_up_weight: bfloat16 [512, 2048], replicated, may hold values from -0.25 to 0.25
- feedforward_down_weight: bfloat16 [2048, 512], replicated, may hold values from -0.125 to 0.125
- cotangent: float32 [4, 24, 768, 512], P(None, 'lat', 'lon'), may hold values from -6 to 6
Outputs:
- mixed_state: float32 [4, 24, 768, 512], P(None, 'lat', 'lon')
- step_down: float32 [32, 8, 512], replicated
- step_up: float32 [32, 8, 1536], replicated
All inputs are finite; a program needn't handle non-finite values. No bound on the sum of `land_patch_mask` on one device may be relied on, other than what follows from the above.
Results may differ from a plain program's by a relative error of at most 0.015.
Values may be sent and summed in bfloat16 or wider, within the bound.
No kernel may reach another device: no remote copies, remote signals or barrier semaphores. Data moves between devices by JAX's collectives and lax.ppermute only.
A program may use at most 128 MiB of HBM per device.

v0:
```python
import jax
import jax.numpy as jnp
from jax import lax
from jax.sharding import PartitionSpec as P

WLEV = 2
WLAT = 6
WLON = 12


HIGH = lax.Precision.HIGHEST


def shifted(array, axis, by):
    size = lax.axis_size(axis)
    return lax.ppermute(array, axis, [(i, (i + by) % size) for i in range(size)])


def layer_norm(field, gain):
    mean = jnp.mean(field, axis=-1, keepdims=True)
    centred = field - mean
    spread = jnp.mean(centred * centred, axis=-1, keepdims=True)
    return (centred * lax.rsqrt(spread + 1e-05) * gain).astype(jnp.bfloat16)


def embed(pixels, land_patch_mask, patch_embed_weight, patch_embed_bias, land_embedding_vector):
    levels, rows, cols, patch_len = pixels.shape
    flat = jnp.dot(
        pixels.reshape(-1, patch_len), patch_embed_weight, preferred_element_type=jnp.float32
    )
    land = land_patch_mask.astype(jnp.float32)[None, :, :, None] * land_embedding_vector
    return flat.reshape(levels, rows, cols, -1) + patch_embed_bias + land


def to_windows(field):
    levels, rows, cols, width = field.shape
    field = field.reshape(levels // WLEV, WLEV, rows // WLAT, WLAT, cols // WLON, WLON, width)
    field = field.transpose(0, 2, 4, 1, 3, 5, 6)
    return field.reshape(-1, WLEV * WLAT * WLON, width)


def from_windows(window_tokens, levels, rows, cols):
    width = window_tokens.shape[-1]
    field = window_tokens.reshape(
        levels // WLEV, rows // WLAT, cols // WLON, WLEV, WLAT, WLON, width
    )
    field = field.transpose(0, 3, 1, 4, 2, 5, 6)
    return field.reshape(levels, rows, cols, width)


def roll_forward(field):
    field = jnp.roll(field, -(WLEV // 2), axis=0)
    upper_bound = shifted(field[:, : WLAT // 2], "lat", -1)
    field = jnp.concatenate((field[:, WLAT // 2 :], upper_bound), axis=1)
    eastern = shifted(field[:, :, : WLON // 2], "lon", -1)
    return jnp.concatenate((field[:, :, WLON // 2 :], eastern), axis=2)


def roll_backward(field):
    western = shifted(field[:, :, -(WLON // 2) :], "lon", 1)
    field = jnp.concatenate((western, field[:, :, : -(WLON // 2)]), axis=2)
    lower = shifted(field[:, -(WLAT // 2) :], "lat", 1)
    field = jnp.concatenate((lower, field[:, : -(WLAT // 2)]), axis=1)
    return jnp.roll(field, WLEV // 2, axis=0)


def apply_projection(
    window_tokens, region_index, query_key_value_weight, region_down_factor, region_up_factor
):
    count, tokens, width = window_tokens.shape
    base = jnp.dot(
        window_tokens.reshape(-1, width), query_key_value_weight, preferred_element_type=jnp.float32
    )
    down_factor = jnp.take(region_down_factor, region_index, axis=0)
    upper_bound = jnp.take(region_up_factor, region_index, axis=0).astype(jnp.float32)
    low_rank_state = jnp.einsum(
        "wtd,wrd->wtr", window_tokens, down_factor, preferred_element_type=jnp.float32
    ).astype(jnp.bfloat16)
    extra = jnp.einsum(
        "wtr,wrc->wtc", low_rank_state.astype(jnp.float32), upper_bound, precision=HIGH
    )
    return (base.reshape(count, tokens, -1) + extra, low_rank_state)


def attend(query_key_value, groups, head_logit_scale, attention_output_weight):
    count, tokens, triple = query_key_value.shape
    heads = head_logit_scale.shape[0]
    size = triple // (3 * heads)
    parts = query_key_value.reshape(count, tokens, 3, heads, size)
    query = parts[:, :, 0]
    key = parts[:, :, 1]
    value = parts[:, :, 2].astype(jnp.bfloat16).astype(jnp.float32)
    query = query * lax.rsqrt(jnp.mean(query * query, axis=-1, keepdims=True) + 1e-06)
    key = key * lax.rsqrt(jnp.mean(key * key, axis=-1, keepdims=True) + 1e-06)
    scores = jnp.einsum("wqhe,wkhe->whqk", query, key, precision=HIGH)
    scores = scores * (head_logit_scale / size)[None, :, None, None]
    same = (groups[:, :, None] == groups[:, None, :])[:, None]
    weights = jnp.where(same, jnp.exp(scores), 0.0)
    probs = (weights / jnp.sum(weights, axis=-1, keepdims=True)).astype(jnp.bfloat16)
    mixed = jnp.einsum("whqk,wkhe->wqhe", probs.astype(jnp.float32), value, precision=HIGH)
    mixed = mixed.reshape(count * tokens, heads * size).astype(jnp.bfloat16)
    out = jnp.dot(mixed, attention_output_weight, preferred_element_type=jnp.float32).astype(
        jnp.bfloat16
    )
    return out.reshape(count, tokens, -1)


def adapter_pieces(
    window_tokens, low_rank_state, grad_query_key_value, region_index, region_up_factor
):
    total_sum = region_up_factor.shape[0]
    upper_bound = jnp.take(region_up_factor, region_index, axis=0).astype(jnp.float32)
    grad_up = jnp.einsum(
        "wtr,wtc->wrc", low_rank_state.astype(jnp.float32), grad_query_key_value, precision=HIGH
    )
    back = jnp.einsum("wtc,wrc->wtr", grad_query_key_value, upper_bound, precision=HIGH)
    grad_down = jnp.einsum("wtr,wtd->wrd", back, window_tokens.astype(jnp.float32), precision=HIGH)
    onehot = (region_index[:, None] == jnp.arange(total_sum, dtype=jnp.int32)[None, :]).astype(
        jnp.float32
    )
    sum_down = jnp.einsum("wg,wrd->grd", onehot, grad_down, precision=HIGH)
    sum_up = jnp.einsum("wg,wrc->grc", onehot, grad_up, precision=HIGH)
    return (sum_down, sum_up)


def feed(state, gain, feedforward_up_weight, feedforward_down_weight):
    array_shape = state.shape
    normed = layer_norm(state, gain).reshape(-1, array_shape[-1])
    inner = jax.nn.gelu(
        jnp.dot(normed, feedforward_up_weight, preferred_element_type=jnp.float32),
        approximate=False,
    )
    inner = inner.astype(jnp.bfloat16)
    return state + jnp.dot(
        inner, feedforward_down_weight, preferred_element_type=jnp.float32
    ).reshape(array_shape)


def window_groups(levels, rows, cols):
    level_flag = (jnp.arange(levels) == levels - 1).astype(jnp.int32)
    lat_global = lax.axis_index("lat") * rows + jnp.arange(rows, dtype=jnp.int32)
    lat_flag = (lat_global >= rows * lax.axis_size("lat") - WLAT // 2).astype(jnp.int32)
    marks = jnp.broadcast_to(
        level_flag[:, None, None] * 2 + lat_flag[None, :, None], (levels, rows, cols)
    )
    return to_windows(marks[..., None])[..., 0]


def local(
    pixels,
    land_patch_mask,
    region,
    patch_embed_weight,
    patch_embed_bias,
    land_embedding_vector,
    attention_norm_gain,
    query_key_value_weight,
    region_down_factor,
    region_up_factor,
    head_logit_scale,
    attention_output_weight,
    feedforward_gain,
    feedforward_up_weight,
    feedforward_down_weight,
    cotangent,
):
    levels, rows, cols, patch_len = pixels.shape
    region_index = region.reshape(-1)
    marks = window_groups(levels, rows, cols)
    state = embed(
        pixels, land_patch_mask, patch_embed_weight, patch_embed_bias, land_embedding_vector
    )

    def attention_pass(rolled):
        window_tokens = to_windows(rolled)
        query_key_value, low_rank_state = apply_projection(
            window_tokens,
            region_index,
            query_key_value_weight,
            region_down_factor,
            region_up_factor,
        )
        z_win, pull = jax.vjp(
            lambda q: attend(q, marks, head_logit_scale, attention_output_weight), query_key_value
        )
        return (from_windows(z_win, levels, rows, cols), pull, window_tokens, low_rank_state)

    rolled = roll_forward(layer_norm(state, attention_norm_gain))
    z_field, pull, window_tokens, low_rank_state = attention_pass(rolled)
    hidden = state + roll_backward(z_field).astype(jnp.float32)
    mixed_state, mlp_pull = jax.vjp(
        lambda v: feed(v, feedforward_gain, feedforward_up_weight, feedforward_down_weight), hidden
    )
    d_hidden = mlp_pull(cotangent)[0].astype(jnp.bfloat16)
    d_rolled = roll_forward(d_hidden)
    grad_query_key_value = pull(to_windows(d_rolled))[0]
    partial_down_grad, partial_up_grad = adapter_pieces(
        window_tokens, low_rank_state, grad_query_key_value, region_index, region_up_factor
    )
    grad_down, grad_up = lax.psum((partial_down_grad, partial_up_grad), ("lat", "lon"))
    squares = jnp.sum(grad_down * grad_down) + jnp.sum(grad_up * grad_up)
    factor = lax.rsqrt(squares / (grad_down.size + grad_up.size) + 1e-06)
    return (mixed_state, grad_down * factor, grad_up * factor)


def solution(mesh):
    placed = (
        P(None, "lat", "lon", None),
        P("lat", "lon"),
        P(None, "lat", "lon"),
        P(),
        P(),
        P(),
        P(),
        P(),
        P(),
        P(),
        P(),
        P(),
        P(),
        P(),
        P(),
        P(None, "lat", "lon", None),
    )
    return jax.shard_map(
        local,
        mesh=mesh,
        in_specs=placed,
        out_specs=(P(None, "lat", "lon", None), P(), P()),
        check_vma=False,
    )
```

profile of v0, /device:TPU:1, one launch (start us, length us, event | category | flops | bytes accessed | tf_op | source)
XLA Modules:
  0.0 367.7 jit_solution(8580001922563521561)
XLA Ops:
  8.8 1.8 fusion.93
  11.7 1.4 collective-permute-start
  16.6 4.5 %collective-permute-done = bf16[4,3,24,512]{3,2,1,0:T(8,128)(2,1)S(1)} collective-permute-done((bf16[4,3,24,512]{3,2,1,0:T(8,128)(2,1)S(1)}, bf16[4,3,24,512]{3,2,1,0:T(8,128)(2,1)S(1)}, u32[]{:S(2)}, u32[]{:S(2)}) %collective-permute-start) | collective-permute-done | bytes 294944 | tf_op jit(solution)/shard_map/ppermute | solution.py:16
  21.1 5.5 %collective-permute-start.1 = (bf16[4,6,6,512]{3,2,1,0:T(8,128)(2,1)S(1)}, bf16[4,6,6,512]{3,2,1,0:T(8,128)(2,1)S(1)}, u32[]{:S(2)}, u32[]{:S(2)}) collective-permute-start(bf16[4,6,6,512]{3,2,1,0:T(8,128)(2,1)S(1)} %pad_maximum_fusion.9), channel_id=1, source_target_pairs={{0,31},{1,0},{2,1},{3,2},{4,3},{5,4},{6,5},{7,6},{8,7},{9,8},{10,9... | collective-permute-start | bytes 442376 | tf_op jit(solution)/shard_map/ppermute | solution.py:16
  26.5 1.5 gather_fusion
  28.0 2.3 gather_fusion.1
  32.7 1.2 copy.62
  34.1 2.7 fusion.41
  37.7 2.4 convolution_add_fusion
  40.2 6.3 %copy.35 = f32[4,144,1536]{1,2,0:T(8,128)} copy(f32[4,144,1536]{2,1,0:T(8,128)} %convolution_add_fusion) | data formatting | bytes 7077888 | tf_op jit(solution)/shard_map/add | solution.py:82
  46.5 2.5 fusion.92
  51.1 10.9 %fusion.7 = (f32[4,16,144]{2,1,0:T(8,128)S(1)}, f32[4,16,144,144]{2,3,1,0:T(8,128)S(1)}) fusion(f32[16]{0:T(128)S(1)} %copy-done.39, pred[4,144,144]{1,2,0:T(8,128)(4,1)S(1)} %copy-done.17, f32[4,144,1,16,32]{1,4,3,2,0:T(8,128)S(1)} %get-tuple-element.14, f32[4,144,16]{1,2,0:T(8,128)S(1)} %fusion.72, f32[4,144,1,16,32]{1,4,3,2,0:T(8,128)S(1)} %get-tuple-element.15, ...), kind=kOutput, calls=%fused_computation.15 | convolution fusion | flops 514169856 | bytes 7861312 | tf_op jit(solution)/shard_map/jvp(wqhe,wkhe->whqk)/dot_general | solution.py:95
  62.0 2.4 divide_convert_fusion
  64.4 1.3 copy-done.2
  65.8 3.9 %fusion.44 = bf16[4,144,16,32]{1,3,2,0:T(8,128)(2,1)S(1)} fusion(bf16[4,16,144,144]{2,3,1,0:T(8,128)(2,1)S(1)} %divide_convert_fusion, f32[4,144,3,16,32]{1,4,3,2,0:T(8,128)} %bitcast.139), kind=kOutput, calls=%fused_computation.80 | convolution fusion | flops 85229568 | bytes 4292608 | tf_op jit(solution)/shard_map/jvp(whqk,wkhe->wqhe)/dot_general | solution.py:100
  70.6 1.5 convert_element_type.99
  72.1 2.6 convolution_convert_fusion.5
  74.7 1.2 reshape.247
  76.8 1.3 reshape.279
  78.2 11.2 %collective-permute-done.2 = bf16[4,6,6,512]{3,2,1,0:T(8,128)(2,1)S(1)} collective-permute-done((bf16[4,6,6,512]{3,2,1,0:T(8,128)(2,1)S(1)}, bf16[4,6,6,512]{3,2,1,0:T(8,128)(2,1)S(1)}, u32[]{:S(2)}, u32[]{:S(2)}) %collective-permute-start.2) | collective-permute-done | bytes 147488 | tf_op jit(solution)/shard_map/ppermute | solution.py:16
  89.6 3.7 collective-permute-done.3
  93.3 1.6 fusion.91
  96.4 12.7 %fusion.17 = (f32[576,2048]{1,0:T(8,128)S(1)}, f32[576,2048]{1,0:T(8,128)S(1)}) fusion(bf16[576,512]{1,0:T(8,128)(2,1)S(1)} %bitcast.153, bf16[512,2048]{1,0:T(8,128)(2,1)S(1)} %copy-done), kind=kOutput, calls=%fused_computation.25 | convolution fusion | flops 1281097728 | bytes 12124160 | tf_op jit(solution)/shard_map/jvp()/dot_general | solution.py:130
  109.1 3.0 fusion.25
  113.1 8.7 %fusion.46 = bf16[576,512]{1,0:T(8,128)(2,1)} fusion(bf16[512,2048]{1,0:T(8,128)(2,1)S(1)} %copy-done, f32[576,2048]{1,0:T(8,128)} %copy-done.8, f32[576,2048]{1,0:T(8,128)} %copy-done.9, f32[576,512]{1,0:T(8,128)} %bitcast.152, bf16[2048,512]{1,0:T(8,128)(2,1)} %param.32), kind=kOutput, calls=%fused_computation.82 | convolution fusion | flops 2433613824 | bytes 15400960 | tf_op jit(solution)/shard_map/transpose(jvp())/dot_general | solution.py:130
  121.8 1.6 fusion.51
  124.1 1.6 fusion.61
  125.8 1.5 add_convert_fusion
  127.4 5.2 %collective-permute-start.4 = (bf16[4,3,24,512]{3,2,1,0:T(8,128)(2,1)S(1)}, bf16[4,3,24,512]{3,2,1,0:T(8,128)(2,1)S(1)}, u32[]{:S(2)}, u32[]{:S(2)}) collective-permute-start(bf16[4,3,24,512]{3,2,1,0:T(8,128)(2,1)S(1)} %get-tuple-element.19), channel_id=1, source_target_pairs={{0,96},{32,0},{64,32},{96,64},{1,97},{33,1},{65,33},{97,65},{2,98}... | collective-permute-start | bytes 884744 | tf_op jit(solution)/shard_map/ppermute | solution.py:16
  132.6 3.3 collective-permute-done.4
  135.9 1.2 collective-permute-start.5
  137.3 3.2 collective-permute-done.5
  143.2 4.0 %fusion.45 = bf16[4,144,1,16,32]{1,4,3,0,2:T(8,128)(2,1)S(1)} fusion(bf16[4,16,144,144]{2,3,1,0:T(8,128)(2,1)} %copy-done.7, bf16[4,16,32,144]{3,0,2,1:T(4,128)(2,1)S(1)} %bitcast.147), kind=kOutput, calls=%fused_computation.81 | convolution fusion | flops 85229568 | bytes 3833856 | tf_op jit(solution)/shard_map/transpose(jvp(whqk,wkhe->wqhe))/dot_general | solution.py:100
  147.2 8.4 %fusion.5 = (f32[4,16,144]{2,1,0:T(8,128)S(1)}, bf16[4,16,144,144]{2,3,1,0:T(8,128)(2,1)}) fusion(f32[4,16,144,144]{2,3,1,0:T(8,128)} %copy-done.2, f32[4,16,144]{2,1,0:T(8,128)S(1)} %multiply_divide_fusion, f32[16]{0:T(128)S(1)} %copy-done.40, pred[4,144,144]{1,2,0:T(8,128)(4,1)S(1)} %copy-done.17, bf16[4,16,32,144]{3,0,2,1:T(4,128)(2,1)S(1)} %bitcast.148, ...), kind=kOutput, calls=%fused_computation.9 | convolution fusion | flops 94215168 | bytes 13886528 | tf_op jit(solution)/shard_map/transpose(jvp(whqk,wkhe->wqhe))/dot_general | solution.py:100
  155.7 5.4 %fusion.3 = f32[4,16,144,144]{2,3,1,0:T(8,128)S(1)} fusion(bf16[4,16,144,144]{2,3,1,0:T(8,128)(2,1)} %get-tuple-element.29, f32[4,16,144,144]{2,3,1,0:T(8,128)S(1)} %bitcast.135, f32[4,16,144]{2,1,0:T(8,128)S(1)} %neg.19, f32[4,16,144]{2,1,0:T(8,128)S(1)} %copy-done.22, f32[16]{0:T(128)S(1)} %copy-done.40, pred[4,144,144]{1,2,0:T(8,128)(4,1)S(1)} %copy-done.17), kind=kLoop, calls=%fused_computation.7 | loop fusion | flops 9289728 | bytes 13427776 | tf_op jit(solution)/shard_map/transpose(jvp())/mul | solution.py:96
  161.1 7.3 %fusion.32 = (f32[4,144,16]{1,2,0:T(8,128)S(1)}, f32[4,16,144,32]{2,3,1,0:T(8,128)S(1)}) fusion(f32[4,144,1,16,32]{1,4,3,2,0:T(8,128)} %copy-done.5, f32[4,16,144,144]{2,3,1,0:T(8,128)S(1)} %fusion.3, f32[4,144,1,16,32]{1,4,3,2,0:T(8,128)S(1)} %copy-done.4, f32[4,144,16]{1,2,0:T(8,128)S(1)} %fusion.72), kind=kOutput, calls=%fused_computation.59 | convolution fusion | flops 510483456 | bytes 8921088 | tf_op jit(solution)/shard_map/transpose(jvp(wqhe,wkhe->whqk))/dot_general | solution.py:95
  168.5 11.1 %fusion.33 = (f32[4,144,16]{1,2,0:T(8,128)S(1)}, f32[4,16,144,32]{2,3,1,0:T(8,128)}) fusion(f32[4,144,1,16,32]{1,4,3,2,0:T(8,128)S(1)} %copy-done.4, f32[4,16,144,144]{2,3,1,0:T(8,128)S(1)} %fusion.3, f32[4,144,1,16,32]{1,4,3,2,0:T(8,128)S(1)} %copy-done.6, f32[4,144,16]{1,2,0:T(8,128)S(1)} %fusion.71), kind=kOutput, calls=%fused_computation.62 | convolution fusion | flops 510483456 | bytes 8921088 | tf_op jit(solution)/shard_map/transpose(jvp(wqhe,wkhe->whqk))/dot_general | solution.py:95
  179.7 3.0 fusion.30
  183.5 1.1 copy.52
  184.6 3.0 fusion.95
  187.7 5.2 %fusion.73 = f32[4,144,8]{2,1,0:T(8,128)S(1)} fusion(f32[4,144,1536]{1,2,0:T(8,128)S(1)} %bitcast.137, bf16[4,8,1536]{2,1,0:T(8,128)(2,1)S(1)} %copy-done.24, pred[4]{0:T(512)(128)(4,1)S(1)} %copy-done.42), kind=kOutput, calls=%fused_computation.144 | convolution fusion | flops 84983808 | bytes 3655684 | tf_op jit(solution)/shard_map/wtc,wrc->wtr/dot_general | solution.py:116
  192.9 2.1 fusion.67
  195.3 1.3 fusion.69
  196.6 155.0 %all-reduce.6.cloned.1.call-done = (f32[32,8,512]{2,0,1:T(8,128)}, f32[32,8,1536]{2,0,1:T(8,128)}) async-done(((f32[32,8,512]{2,0,1:T(8,128)}, f32[32,8,1536]{2,0,1:T(8,128)}), (f32[32,8,512]{2,0,1:T(8,128)}, f32[32,8,1536]{2,0,1:T(8,128)})) %all-reduce.6.cloned.1.call-update) | async-done | bytes 2097168 | tf_op jit(solution)/shard_map/psum | solution.py:200
  351.6 2.6 multiply_reduce_fusion.2
  354.2 1.8 multiply_reduce_fusion.5
  357.5 2.1 copy.54
  359.6 1.1 copy.53
  (174 shorter events, 21.3 us)
Async XLA Ops:
  7.2 89.2 %copy-start = (bf16[512,2048]{1,0:T(8,128)(2,1)S(1)}, bf16[512,2048]{1,0:T(8,128)(2,1)}, u32[]{:S(2)}) copy-start(bf16[512,2048]{1,0:T(8,128)(2,1)} %param.31) | copy-start | bytes 6291460
  7.2 3.8 %copy-start.43 = (f32[512]{0:T(512)S(1)}, f32[512]{0:T(512)}, u32[]{:S(2)}) copy-start(f32[512]{0:T(512)} %param.24) | copy-start | bytes 6148
  7.2 344.4 %all-reduce.6.cloned.1.call-start = ((), (), s32[]{:S(2)}) async-start(), calls=%async_computation | async-start | bytes 4194304 | tf_op jit(solution)/shard_map/psum | solution.py:200
  11.0 2.6 copy-start.46
  11.0 4.2 %copy-start.47 = (f32[16]{0:T(128)S(1)}, f32[16]{0:T(128)}, u32[]{:S(2)}) copy-start(f32[16]{0:T(128)} %param.28) | copy-start | bytes 196
  11.7 9.4 %collective-permute-start = (bf16[4,3,24,512]{3,2,1,0:T(8,128)(2,1)S(1)}, bf16[4,3,24,512]{3,2,1,0:T(8,128)(2,1)S(1)}, u32[]{:S(2)}, u32[]{:S(2)}) collective-permute-start(bf16[4,3,24,512]{3,2,1,0:T(8,128)(2,1)S(1)} %get-tuple-element.21), channel_id=1, source_target_pairs={{0,96},{32,0},{64,32},{96,64},{1,97},{33,1},{65,33},{97,65},{2,98}... | collective-permute-start | bytes 884744 | tf_op jit(solution)/shard_map/ppermute | solution.py:16
  14.4 22.8 %copy-start.41 = (pred[4]{0:T(512)(128)(4,1)}, pred[4]{0:T(512)(128)(4,1)S(1)}, u32[]{:S(2)}) copy-start(pred[4]{0:T(512)(128)(4,1)S(1)} %compare_and_fusion) | copy-start | bytes 16
  21.1 10.0 %collective-permute-start.1 = (bf16[4,6,6,512]{3,2,1,0:T(8,128)(2,1)S(1)}, bf16[4,6,6,512]{3,2,1,0:T(8,128)(2,1)S(1)}, u32[]{:S(2)}, u32[]{:S(2)}) collective-permute-start(bf16[4,6,6,512]{3,2,1,0:T(8,128)(2,1)S(1)} %pad_maximum_fusion.9), channel_id=1, source_target_pairs={{0,31},{1,0},{2,1},{3,2},{4,3},{5,4},{6,5},{7,6},{8,7},{9,8},{10,9... | collective-permute-start | bytes 442376 | tf_op jit(solution)/shard_map/ppermute | solution.py:16
  34.1 2.7 copy-start.10
  34.1 3.7 copy-start.23
  49.1 12.9 %copy-start.3 = (f32[4,144,1,16,32]{1,4,3,2,0:T(8,128)}, f32[4,144,1,16,32]{1,4,3,2,0:T(8,128)S(1)}, u32[]{:S(2)}) copy-start(f32[4,144,1,16,32]{1,4,3,2,0:T(8,128)S(1)} %get-tuple-element.14) | copy-start | bytes 3538948
  49.1 12.9 %copy-start.5 = (f32[4,144,1,16,32]{1,4,3,2,0:T(8,128)}, f32[4,144,1,16,32]{1,4,3,2,0:T(8,128)S(1)}, u32[]{:S(2)}) copy-start(f32[4,144,1,16,32]{1,4,3,2,0:T(8,128)S(1)} %get-tuple-element.15) | copy-start | bytes 3538948
  49.1 2.0 copy-start.17
  49.1 2.0 copy-start.39
  62.0 3.7 copy-start.2
  62.0 3.7 %copy-start.21 = (f32[4,16,144]{2,1,0:T(8,128)}, f32[4,16,144]{2,1,0:T(8,128)S(1)}, u32[]{:S(2)}) copy-start(f32[4,16,144]{2,1,0:T(8,128)S(1)} %get-tuple-element.24) | copy-start | bytes 110596
  65.8 3.9 %copy-start.7 = (bf16[4,16,144,144]{2,3,1,0:T(8,128)(2,1)}, bf16[4,16,144,144]{2,3,1,0:T(8,128)(2,1)S(1)}, u32[]{:S(2)}) copy-start(bf16[4,16,144,144]{2,3,1,0:T(8,128)(2,1)S(1)} %divide_convert_fusion) | copy-start | bytes 7962628
  78.1 11.6 %copy-start.14 = (bf16[4,6,24,512]{3,2,1,0:T(8,128)(2,1)}, bf16[4,6,24,512]{3,2,1,0:T(8,128)(2,1)S(1)}, u32[]{:S(2)}) copy-start(bf16[4,6,24,512]{3,2,1,0:T(8,128)(2,1)S(1)} %reshape.279) | copy-start | bytes 1769476
  78.1 11.3 %collective-permute-start.2 = (bf16[4,6,6,512]{3,2,1,0:T(8,128)(2,1)S(1)}, bf16[4,6,6,512]{3,2,1,0:T(8,128)(2,1)S(1)}, u32[]{:S(2)}, u32[]{:S(2)}) collective-permute-start(bf16[4,6,6,512]{3,2,1,0:T(8,128)(2,1)S(1)} %slice.102), channel_id=1, source_target_pairs={{0,1},{1,2},{2,3},{3,4},{4,5},{5,6},{6,7},{7,8},{8,9},{9,10},{10,1... | collective-permute-start | bytes 442376 | tf_op jit(solution)/shard_map/ppermute | solution.py:16
  89.5 6.3 %copy-start.37 = (f32[512]{0:T(512)S(1)}, f32[512]{0:T(512)}, u32[]{:S(2)}) copy-start(f32[512]{0:T(512)} %param.30) | copy-start | bytes 6148
  89.5 3.7 %collective-permute-start.3 = (bf16[4,3,24,512]{3,2,1,0:T(8,128)(2,1)S(1)}, bf16[4,3,24,512]{3,2,1,0:T(8,128)(2,1)S(1)}, u32[]{:S(2)}, u32[]{:S(2)}) collective-permute-start(bf16[4,3,24,512]{3,2,1,0:T(8,128)(2,1)S(1)} %fusion.65), channel_id=1, source_target_pairs={{0,32},{32,64},{64,96},{96,0},{1,33},{33,65},{65,97},{97,1},{2,34}... | collective-permute-start | bytes 884744 | tf_op jit(solution)/shard_map/ppermute | solution.py:16
  96.4 12.7 %copy-start.18 = (bf16[2048,512]{1,0:T(8,128)(2,1)S(1)}, bf16[2048,512]{1,0:T(8,128)(2,1)}, u32[]{:S(2)}) copy-start(bf16[2048,512]{1,0:T(8,128)(2,1)} %param.32) | copy-start | bytes 6291460
  109.1 3.0 copy-start.8
  109.1 4.0 %copy-start.9 = (f32[576,2048]{1,0:T(8,128)}, f32[576,2048]{1,0:T(8,128)S(1)}, u32[]{:S(2)}) copy-start(f32[576,2048]{1,0:T(8,128)S(1)} %get-tuple-element.27) | copy-start | bytes 14155780
  121.8 4.0 %copy-start.13 = (f32[576,512]{1,0:T(8,128)S(1)}, f32[576,512]{1,0:T(8,128)}, u32[]{:S(2)}) copy-start(f32[576,512]{1,0:T(8,128)} %fusion.25) | copy-start | bytes 3538948
  121.8 4.0 %copy-start.16 = (bf16[576,512]{1,0:T(8,128)(2,1)S(1)}, bf16[576,512]{1,0:T(8,128)(2,1)}, u32[]{:S(2)}) copy-start(bf16[576,512]{1,0:T(8,128)(2,1)} %fusion.46) | copy-start | bytes 1769476
  121.8 4.0 %copy-start.20 = (f32[4,6,24,512]{3,2,1,0:T(8,128)S(1)}, f32[4,6,24,512]{3,2,1,0:T(8,128)}, u32[]{:S(2)}) copy-start(f32[4,6,24,512]{3,2,1,0:T(8,128)} %param.33) | copy-start | bytes 3538948
  121.8 4.0 %copy-start.26 = (f32[4,6,24]{2,1,0:T(8,128)S(1)}, f32[4,6,24]{2,1,0:T(8,128)}, u32[]{:S(2)}) copy-start(f32[4,6,24]{2,1,0:T(8,128)} %copy-done.25) | copy-start | bytes 6916
  121.8 4.0 %copy-start.33 = (f32[4,6,24]{2,1,0:T(8,128)S(1)}, f32[4,6,24]{2,1,0:T(8,128)}, u32[]{:S(2)}) copy-start(f32[4,6,24]{2,1,0:T(8,128)} %copy-done.32) | copy-start | bytes 6916
  121.8 4.0 %copy-start.38 = (f32[512]{0:T(512)S(1)}, f32[512]{0:T(512)}, u32[]{:S(2)}) copy-start(f32[512]{0:T(512)} %param.30) | copy-start | bytes 6148
  127.3 9.8 %copy-start.22 = (f32[4,16,144]{2,1,0:T(8,128)S(1)}, f32[4,16,144]{2,1,0:T(8,128)}, u32[]{:S(2)}) copy-start(f32[4,16,144]{2,1,0:T(8,128)} %copy-done.21) | copy-start | bytes 110596
  127.4 8.5 %collective-permute-start.4 = (bf16[4,3,24,512]{3,2,1,0:T(8,128)(2,1)S(1)}, bf16[4,3,24,512]{3,2,1,0:T(8,128)(2,1)S(1)}, u32[]{:S(2)}, u32[]{:S(2)}) collective-permute-start(bf16[4,3,24,512]{3,2,1,0:T(8,128)(2,1)S(1)} %get-tuple-element.19), channel_id=1, source_target_pairs={{0,96},{32,0},{64,32},{96,64},{1,97},{33,1},{65,33},{97,65},{2,98}... | collective-permute-start | bytes 884744 | tf_op jit(solution)/shard_map/ppermute | solution.py:16
  135.9 4.6 %collective-permute-start.5 = (bf16[4,6,6,512]{3,2,1,0:T(8,128)(2,1)S(1)}, bf16[4,6,6,512]{3,2,1,0:T(8,128)(2,1)S(1)}, u32[]{:S(2)}, u32[]{:S(2)}) collective-permute-start(bf16[4,6,6,512]{3,2,1,0:T(8,128)(2,1)S(1)} %pad_maximum_fusion.8), channel_id=1, source_target_pairs={{0,31},{1,0},{2,1},{3,2},{4,3},{5,4},{6,5},{7,6},{8,7},{9,8},{10,9... | collective-permute-start | bytes 442376 | tf_op jit(solution)/shard_map/ppermute | solution.py:16
  143.1 4.1 %copy-start.40 = (f32[16]{0:T(128)S(1)}, f32[16]{0:T(128)}, u32[]{:S(2)}) copy-start(f32[16]{0:T(128)} %broadcast_multiply_fusion.5) | copy-start | bytes 196
  143.2 12.5 %slice-start = ((s8[9437184]{0:T(1024)(128)(4,1)}), s8[4194304]{0:T(1024)(128)(4,1)S(1)}, s32[]{:S(2)}) async-start(s8[9437184]{0:T(1024)(128)(4,1)} %bitcast.134), calls=%async_computation.1 | async-start | bytes 8388608
  147.2 8.4 %slice-start.1 = ((s8[9437184]{0:T(1024)(128)(4,1)}), s8[4194304]{0:T(1024)(128)(4,1)S(1)}, s32[]{:S(2)}) async-start(s8[9437184]{0:T(1024)(128)(4,1)} %bitcast.134), calls=%async_computation.2 | async-start | bytes 8388608
  147.2 8.4 %slice-start.2 = ((s8[9437184]{0:T(1024)(128)(4,1)}), s8[1048576]{0:T(1024)(128)(4,1)S(1)}, s32[]{:S(2)}) async-start(s8[9437184]{0:T(1024)(128)(4,1)} %bitcast.134), calls=%async_computation.3 | async-start | bytes 2097152
  155.7 5.4 %copy-start.4 = (f32[4,144,1,16,32]{1,4,3,2,0:T(8,128)S(1)}, f32[4,144,1,16,32]{1,4,3,2,0:T(8,128)}, u32[]{:S(2)}) copy-start(f32[4,144,1,16,32]{1,4,3,2,0:T(8,128)} %copy-done.3) | copy-start | bytes 3538948
  161.1 7.4 %copy-start.6 = (f32[4,144,1,16,32]{1,4,3,2,0:T(8,128)S(1)}, f32[4,144,1,16,32]{1,4,3,2,0:T(8,128)}, u32[]{:S(2)}) copy-start(f32[4,144,1,16,32]{1,4,3,2,0:T(8,128)} %copy-done.5) | copy-start | bytes 3538948
  168.5 11.2 %copy-start.28 = (f32[4,144,16]{1,2,0:T(8,128)S(1)}, f32[4,144,16]{1,2,0:T(8,128)}, u32[]{:S(2)}) copy-start(f32[4,144,16]{1,2,0:T(8,128)} %copy-done.27) | copy-start | bytes 110596
  168.5 11.2 %copy-start.30 = (f32[4,144,16]{1,2,0:T(8,128)S(1)}, f32[4,144,16]{1,2,0:T(8,128)}, u32[]{:S(2)}) copy-start(f32[4,144,16]{1,2,0:T(8,128)} %copy-done.29) | copy-start | bytes 110596
  184.6 3.0 copy-start.24
  184.6 3.0 copy-start.42
  187.7 5.2 %copy-start.45 = (s32[4]{0:T(128)S(1)}, s32[4]{0:T(128)}, u32[]{:S(2)}) copy-start(s32[4]{0:T(128)} %copy-done.44) | copy-start | bytes 52
  187.7 7.2 %copy-start.11 = (bf16[4,144,512]{2,1,0:T(8,128)(2,1)S(1)}, bf16[4,144,512]{2,1,0:T(8,128)(2,1)}, u32[]{:S(2)}) copy-start(bf16[4,144,512]{2,1,0:T(8,128)(2,1)} %copy-done.10) | copy-start | bytes 1769476
  351.6 5.7 %copy-start.15 = (f32[32,8,1536]{2,0,1:T(8,128)S(1)}, f32[32,8,1536]{2,0,1:T(8,128)}, u32[]{:S(2)}) copy-start(f32[32,8,1536]{2,0,1:T(8,128)} %get-tuple-element.11) | copy-start | bytes 4718596
  351.6 5.8 %copy-start.19 = (f32[32,8,512]{2,0,1:T(8,128)S(1)}, f32[32,8,512]{2,0,1:T(8,128)}, u32[]{:S(2)}) copy-start(f32[32,8,512]{2,0,1:T(8,128)} %get-tuple-element.10) | copy-start | bytes 1572868
  357.5 3.2 copy-start.1
  (10 other events, 8.4 us)
Sparse Core Ops, SparseCore 0:
  196.8 154.8 all-reduce.5
where the time goes:
time: 373 us; the launch traced here: 368 us
  waiting for transfers between devices  181 us (49%)
  matrix products  92.2 us (25%)
  local copies, waits for them, and re-layouts  34.6 us (9%)
  other arithmetic  29.5 us (8%)
  between operations  16.6 us (4%)
  starting transfers between devices  13.5 us (4%)
    psum x1, waiting for transfers between devices, local(): lax.psum((partial_down_grad, partial_up_grad), ('lat', 'lon'))  155 us
    dot_general x3, matrix products, attend(): scores = jnp.einsum('wqhe,wkhe->whqk', query, key, precision=HIGH)  29.4 us
    ppermute x6, waiting for transfers between devices, shifted(): lax.ppermute(array, axis, [(i, (i + by) % size) for i in range(size)])  26.4 us
    dot_general x2, matrix products, feed(): jnp.dot(normed, feedforward_up_weight, preferred_element_type=jnp.float32)  21.4 us
    dot_general x3, matrix products, attend(): jnp.einsum('whqk,wkhe->wqhe', probs.astype(jnp.float32), value, precision...  16.3 us
    ppermute x6, starting transfers between devices, shifted(): lax.ppermute(array, axis, [(i, (i + by) % size) for i in range(size)])  13.4 us
    unnamed x105, local copies, waits for them, and re-layouts  9.72 us
  transfers between devices with their start and end apart: 7, of which 7 were waited for; matrix products, arithmetic and copies ran while one was open for 2% of the time, Pallas kernels for 0%

commit v1 on v0

v1 whole, which is shorter than its diff:
```python
import jax
import jax.numpy as jnp
from jax import lax
from jax.experimental import pallas as pl
from jax.experimental.pallas import tpu as pltpu
from jax.sharding import PartitionSpec as P

WLEV = 2
WLAT = 6
WLON = 12
TOKENS = WLEV * WLAT * WLON
HALF_LAT = WLAT // 2
HALF_LON = WLON // 2
LANES = 128
HEAD = 32
PER_GROUP = LANES // HEAD

F32 = jnp.float32
BF16 = jnp.bfloat16
VMEM_LIMIT = 56 * 1024 * 1024


def mm(a, b):
    return lax.dot_general(a, b, (((1,), (0,)), ((), ())), preferred_element_type=F32)


def mm_nt(a, b):
    return lax.dot_general(a, b, (((1,), (1,)), ((), ())), preferred_element_type=F32)


def mm_tn(a, b):
    return lax.dot_general(a, b, (((0,), (0,)), ((), ())), preferred_element_type=F32)


def head_mean(squares):
    rows = lax.broadcasted_iota(jnp.int32, (LANES, LANES), 0) // HEAD
    cols = lax.broadcasted_iota(jnp.int32, (LANES, LANES), 1) // HEAD
    block = jnp.where(rows == cols, 1.0 / HEAD, 0.0).astype(BF16)
    parts = []
    for g in range(squares.shape[1] // LANES):
        part = squares[:, g * LANES : (g + 1) * LANES]
        top = part.astype(BF16)
        rest = (part - top.astype(F32)).astype(BF16)
        parts.append(mm(top, block) + mm(rest, block))
    return jnp.concatenate(parts, axis=1)


def head_masks():
    lane = lax.broadcasted_iota(jnp.int32, (1, LANES), 1) // HEAD
    return [jnp.where(lane == h, 1.0, 0.0).astype(F32) for h in range(PER_GROUP)]


def stack_heads(x, masks):
    return jnp.concatenate([(x * m).astype(BF16) for m in masks], axis=0)


def unstack_heads(x, masks):
    tokens = x.shape[0] // PER_GROUP
    return sum(x[h * tokens : (h + 1) * tokens] * m for h, m in enumerate(masks))


def window_columns(tokens, columns):
    count = tokens // TOKENS
    rows = lax.broadcasted_iota(jnp.int32, (tokens, columns), 0)
    cols = lax.broadcasted_iota(jnp.int32, (tokens, columns), 1) % count
    own = jnp.zeros((tokens, columns), F32)
    for w in range(count):
        inside = (rows >= w * TOKENS) & (rows < (w + 1) * TOKENS) & (cols == w)
        own = jnp.where(inside, 1.0, own)
    return own


def norm_stats(x):
    width = x.shape[1]
    mean = jnp.sum(x, axis=1, keepdims=True) * (1.0 / width)
    centred = x - mean
    spread = jnp.sum(centred * centred, axis=1, keepdims=True) * (1.0 / width)
    return centred, lax.rsqrt(spread + 1e-05)


def gelu_and_slope(u):
    x = jnp.abs(u) * 0.7071067811865476
    t = 1.0 / (1.0 + 0.3275911 * x)
    e = jnp.exp(-0.5 * u * u)
    poly = 1.061405429
    for c in (-1.453152027, 1.421413741, -0.284496736, 0.254829592):
        poly = poly * t + c
    tail = 0.5 * poly * t * e
    phi = jnp.where(u < 0, tail, 1.0 - tail)
    return u * phi, phi + u * (0.3989422804014327 * e)


def forward_kernel(
    pix_ref, wp_ref, bias_ref, land_ref, gain1_ref, wqkv_ref, down_ref, up_ref, scale_ref,
    same_ref, wo_ref, gain2_ref, wup_ref, wdn_ref, cot_ref,
    mixed_ref, normed_ref, low_ref, qk_ref, v_ref, probs_ref, datt_ref,
    state_ref, qs_ref, kn_ref, att_ref,
):
    tokens, width = state_ref.shape
    count = tokens // TOKENS
    groups = width // LANES
    masks = head_masks()
    pix = pix_ref[...]
    patch_len = wp_ref.shape[0]
    land = pix[:, 500:501].astype(F32)
    state = mm(pix, wp_ref[...]) + bias_ref[...] + land * land_ref[...]
    state_ref[...] = state
    centred, inv = norm_stats(state)
    normed = (centred * inv * gain1_ref[...]).astype(BF16)
    normed_ref[...] = normed
    low = (mm_nt(normed, down_ref[...]) * window_columns(tokens, down_ref.shape[0])).astype(BF16)
    low_ref[...] = low
    for part in range(3):
        cols = slice(part * width, (part + 1) * width)
        qkv = mm(normed, wqkv_ref[:, cols]) + mm(low, up_ref[:, cols])
        if part == 2:
            v_ref[...] = qkv.astype(BF16)
        else:
            qk_ref[:, cols] = qkv
            unit = qkv * lax.rsqrt(head_mean(qkv * qkv) + 1e-06)
            if part == 0:
                qs_ref[...] = unit * scale_ref[...]
            else:
                kn_ref[...] = unit.astype(BF16)

    def window(w, carry):
        rows = pl.ds(pl.multiple_of(w * TOKENS, TOKENS), TOKENS)
        same = same_ref[w // (count // WLEV)]
        for g in range(groups):
            cols = slice(g * LANES, (g + 1) * LANES)
            stack = stack_heads(qs_ref[rows, cols], masks)
            weights = jnp.exp(mm_nt(kn_ref[rows, cols], stack)) * same
            total = jnp.sum(weights, axis=0, keepdims=True)
            probs = (weights * (1.0 / total)).astype(BF16)
            probs_ref[w * groups + g] = probs
            mixed = mm_tn(probs, v_ref[rows, cols])
            att_ref[rows, cols] = unstack_heads(mixed, masks).astype(BF16)
        return carry

    lax.fori_loop(0, count, window, 0)
    z = mm(att_ref[...], wo_ref[...]).astype(BF16)
    hidden = state_ref[...] + z.astype(F32)
    centred, inv = norm_stats(hidden)
    unit = centred * inv
    normed2 = (unit * gain2_ref[...]).astype(BF16)
    cot = cot_ref[...]
    mixed_ref[...] = hidden
    state_ref[...] = unit
    d_normed = jnp.zeros((tokens, width), F32)
    chunk = 512
    for c in range(wup_ref.shape[1] // chunk):
        cols = slice(c * chunk, (c + 1) * chunk)
        act, slope = gelu_and_slope(mm(normed2, wup_ref[:, cols]))
        mixed_ref[...] += mm(act.astype(BF16), wdn_ref[cols, :])
        d_up = mm_nt(cot, wdn_ref[cols, :]) * slope
        d_normed += mm_nt(d_up.astype(BF16), wup_ref[:, cols])
    d_unit = d_normed * gain2_ref[...]
    unit = state_ref[...]
    first = jnp.sum(d_unit, axis=1, keepdims=True) * (1.0 / width)
    second = jnp.sum(d_unit * unit, axis=1, keepdims=True) * (1.0 / width)
    d_hidden = cot.astype(F32) + inv * (d_unit - first - unit * second)
    datt_ref[...] = mm_nt(d_hidden.astype(BF16), wo_ref[...]).astype(BF16)


def backward_kernel(
    normed_ref, low_ref, qk_ref, v_ref, probs_ref, datt_ref, up_ref, scale_ref, ids_ref,
    terms_ref,
    qs_ref, kn_ref, dq_ref, dk_ref, dqkv_ref,
):
    tokens, width = normed_ref.shape
    count = tokens // TOKENS
    groups = width // LANES
    masks = head_masks()
    scale = scale_ref[...]
    inv = []
    for part in range(2):
        raw = qk_ref[:, part * width : (part + 1) * width]
        inv.append(lax.rsqrt(head_mean(raw * raw) + 1e-06))
        if part == 0:
            qs_ref[...] = raw * inv[0] * scale
        else:
            kn_ref[...] = (raw * inv[1]).astype(BF16)

    def window(w, carry):
        rows = pl.ds(pl.multiple_of(w * TOKENS, TOKENS), TOKENS)
        for g in range(groups):
            cols = slice(g * LANES, (g + 1) * LANES)
            d_stack = stack_heads(datt_ref[rows, cols].astype(F32), masks)
            q_stack = stack_heads(qs_ref[rows, cols], masks)
            probs = probs_ref[w * groups + g]
            d_probs = mm_nt(v_ref[rows, cols], d_stack)
            wide = probs.astype(F32)
            prod = wide * d_probs
            d_scores = (prod - wide * jnp.sum(prod, axis=0, keepdims=True)).astype(BF16)
            dqkv_ref[rows, slice(2 * width + g * LANES, 2 * width + (g + 1) * LANES)] = mm(
                probs, d_stack
            ).astype(BF16)
            dk_ref[rows, cols] = mm(d_scores, q_stack)
            dq_ref[rows, cols] = unstack_heads(mm_tn(d_scores, kn_ref[rows, cols]), masks)
        return carry

    lax.fori_loop(0, count, window, 0)
    for part, grad_ref in enumerate((dq_ref, dk_ref)):
        cols = slice(part * width, (part + 1) * width)
        unit = qk_ref[:, cols] * inv[part]
        grad = grad_ref[...] * scale if part == 0 else grad_ref[...]
        dqkv_ref[:, cols] = (inv[part] * (grad - unit * head_mean(grad * unit))).astype(BF16)
    low = low_ref[...]
    d_qkv = dqkv_ref[...]
    own = window_columns(tokens, up_ref.shape[0])
    back = (mm_nt(d_qkv, up_ref[...]) * own).astype(BF16)
    grads = jnp.concatenate([mm_tn(back, normed_ref[...]), mm_tn(low, d_qkv)], axis=1)
    blocks = grads.shape[1] // LANES
    for r in range(grads.shape[0] // count):
        for b in range(blocks):
            terms_ref[r * blocks + b, :count, :] = grads[
                r * count : (r + 1) * count, b * LANES : (b + 1) * LANES
            ]
            terms_ref[r * blocks + b, count:, :] = ids_ref[...]


def reduce_kernel(terms_ref, sums_ref):
    pieces, regions = sums_ref.shape[:2]
    half = terms_ref.shape[2] // 2
    for p in range(pieces):
        tile = terms_ref[:, p]
        ids = pltpu.roll(tile, half, 1)
        row = lax.broadcasted_iota(jnp.int32, tile.shape, 1)
        value = jnp.where(row < half, tile, 0.0)
        for g in range(regions):
            part = jnp.sum(jnp.where(ids == g, value, 0.0), axis=0)
            sums_ref[p, g : g + 1, :] = jnp.sum(part, axis=0, keepdims=True).astype(sums_ref.dtype)


def scale_kernel(sums_ref, down_ref, up_ref):
    regions, rank, width = down_ref.shape
    blocks = sums_ref.shape[0] // rank
    total = jnp.zeros((regions, LANES), F32)
    for p in range(sums_ref.shape[0]):
        part = sums_ref[p].astype(F32)
        total += part * part
    size = sums_ref.shape[0] * regions * LANES
    total = jnp.sum(jnp.sum(total, axis=0, keepdims=True), axis=1, keepdims=True)
    factor = lax.rsqrt(total * (1.0 / size) + 1e-06)
    for b in range(blocks):
        part = jnp.stack([sums_ref[r * blocks + b].astype(F32) * factor for r in range(rank)])
        part = jnp.swapaxes(part, 0, 1)
        start = b * LANES
        if start < width:
            down_ref[:, :, start : start + LANES] = part
        else:
            up_ref[:, :, start - width : start - width + LANES] = part


def call(kernel, outs, scratch=(), flops=0, moved=0, name=None):
    return pl.pallas_call(
        kernel,
        out_shape=outs,
        scratch_shapes=list(scratch),
        compiler_params=pltpu.CompilerParams(vmem_limit_bytes=VMEM_LIMIT),
        cost_estimate=pl.CostEstimate(flops=flops, bytes_accessed=moved, transcendentals=0),
        name=name,
    )


def shape(*dims, dtype=F32):
    return jax.ShapeDtypeStruct(dims, dtype)


def halo_pairs(step):
    lats, lons = lax.axis_size("lat"), lax.axis_size("lon")

    def index(a, b):
        return (a % lats) * lons + b % lons

    return [
        (index(a, b), index(a + step[0], b + step[1])) for a in range(lats) for b in range(lons)
    ]


def move(array, step):
    return lax.ppermute(array, ("lat", "lon"), halo_pairs(step))


def to_windows(field):
    levels, rows, cols, width = field.shape
    field = jnp.roll(field, -(WLEV // 2), axis=0)
    field = field.reshape(levels // WLEV, WLEV, rows // WLAT, WLAT, cols // WLON, WLON, width)
    return field.transpose(0, 2, 4, 1, 3, 5, 6).reshape(-1, width)


def from_windows(tokens, levels, rows, cols):
    width = tokens.shape[-1]
    field = tokens.reshape(levels // WLEV, rows // WLAT, cols // WLON, WLEV, WLAT, WLON, width)
    field = field.transpose(0, 3, 1, 4, 2, 5, 6).reshape(levels, rows, cols, width)
    return jnp.roll(field, WLEV // 2, axis=0)


def shifted_windows(field):
    south = move(field[:, :HALF_LAT, HALF_LON:], (-1, 0))
    east = move(field[:, HALF_LAT:, :HALF_LON], (0, -1))
    corner = move(field[:, :HALF_LAT, :HALF_LON], (-1, -1))
    upper = jnp.concatenate((field[:, HALF_LAT:, HALF_LON:], east), axis=2)
    lower = jnp.concatenate((south, corner), axis=2)
    return to_windows(jnp.concatenate((upper, lower), axis=1))


def home_field(tokens, levels, rows, cols):
    field = from_windows(tokens, levels, rows, cols)
    edge = cols - HALF_LON
    north = move(field[:, HALF_LAT:, :edge].astype(BF16), (1, 0)).astype(F32)
    west = move(field[:, :HALF_LAT, edge:].astype(BF16), (0, 1)).astype(F32)
    corner = move(field[:, HALF_LAT:, edge:].astype(BF16), (1, 1)).astype(F32)
    upper = jnp.concatenate((corner, north), axis=2)
    lower = jnp.concatenate((west, field[:, :HALF_LAT, :edge]), axis=2)
    return jnp.concatenate((upper, lower), axis=1)


def same_group(levels, rows):
    level = jnp.arange(levels).reshape(levels // WLEV, WLEV, 1, 1) == levels - 1
    row = jnp.arange(rows).reshape(1, 1, rows, 1) >= rows - HALF_LAT
    row = row & (lax.axis_index("lat") == lax.axis_size("lat") - 1)
    group = jnp.broadcast_to(2 * level + row, (levels // WLEV, WLEV, rows, WLON))
    group = group.reshape(levels // WLEV, TOKENS)
    same = (group[:, :, None] == group[:, None, :]).astype(F32)
    return jnp.tile(same, (1, 1, PER_GROUP))


def local(
    pixels,
    land_patch_mask,
    region,
    patch_embed_weight,
    patch_embed_bias,
    land_embedding_vector,
    attention_norm_gain,
    query_key_value_weight,
    region_down_factor,
    region_up_factor,
    head_logit_scale,
    attention_output_weight,
    feedforward_gain,
    feedforward_up_weight,
    feedforward_down_weight,
    cotangent,
):
    levels, rows, cols, patch_len = pixels.shape
    width = patch_embed_weight.shape[1]
    inner = feedforward_up_weight.shape[1]
    regions, rank, _ = region_down_factor.shape
    region_index = region.reshape(-1)
    count = region_index.shape[0]
    tokens = count * TOKENS
    groups = width // LANES
    devices = lax.axis_size("lat") * lax.axis_size("lon")
    padded = -(-patch_len // LANES) * LANES

    land = jnp.broadcast_to(land_patch_mask.astype(BF16)[None, :, :, None], (levels, rows, cols, 1))
    spare = jnp.zeros((levels, rows, cols, padded - patch_len - 1), BF16)
    pix = shifted_windows(jnp.concatenate((pixels, land, spare), axis=3))
    cot = shifted_windows(cotangent.astype(BF16))
    embed_weight = jnp.pad(patch_embed_weight, ((0, padded - patch_len), (0, 0)))
    down = jnp.take(region_down_factor, region_index, axis=0).swapaxes(0, 1).reshape(-1, width)
    up = jnp.take(region_up_factor, region_index, axis=0).swapaxes(0, 1).reshape(-1, 3 * width)
    scale = jnp.repeat(head_logit_scale / HEAD, HEAD)[None]
    ids = jnp.broadcast_to(region_index.astype(F32)[:, None], (count, LANES))

    mixed, normed, low, qk, v, probs, d_att = call(
        forward_kernel,
        (
            shape(tokens, width),
            shape(tokens, width, dtype=BF16),
            shape(tokens, rank * count, dtype=BF16),
            shape(tokens, 2 * width),
            shape(tokens, width, dtype=BF16),
            shape(count * groups, TOKENS, PER_GROUP * TOKENS, dtype=BF16),
            shape(tokens, width, dtype=BF16),
        ),
        (
            pltpu.VMEM((tokens, width), F32),
            pltpu.VMEM((tokens, width), F32),
            pltpu.VMEM((tokens, width), BF16),
            pltpu.VMEM((tokens, width), BF16),
        ),
        flops=2 * tokens * width * (6 * width + 4 * inner),
        moved=20_000_000,
        name="layer_forward",
    )(
        pix, embed_weight, patch_embed_bias[None], land_embedding_vector[None],
        attention_norm_gain[None], query_key_value_weight, down, up, scale,
        same_group(levels, rows), attention_output_weight, feedforward_gain[None],
        feedforward_up_weight, feedforward_down_weight, cot,
    )
    pieces = rank * 4 * width // LANES
    terms = call(
        backward_kernel,
        shape(pieces, 2 * count, LANES),
        (
            pltpu.VMEM((tokens, width), F32),
            pltpu.VMEM((tokens, width), BF16),
            pltpu.VMEM((tokens, width), F32),
            pltpu.VMEM((tokens, width), F32),
            pltpu.VMEM((tokens, 3 * width), BF16),
        ),
        flops=2 * tokens * width * 4 * width,
        moved=12_000_000,
        name="attention_backward",
    )(normed, low, qk, v, probs, d_att, up, scale, ids)
    mixed_state = home_field(mixed, levels, rows, cols)

    each = pieces // devices
    terms = lax.all_to_all(terms, ("lat", "lon"), 0, 0, tiled=True)
    terms = terms.reshape(devices, each, 2 * count, LANES)
    sums = call(reduce_kernel, shape(each, regions, LANES, dtype=BF16), name="sum_by_region")(terms)
    sums = jnp.broadcast_to(sums[None], (devices, each, regions, LANES))
    sums = lax.all_to_all(sums, ("lat", "lon"), 0, 0, tiled=True)
    step_down, step_up = call(
        scale_kernel,
        (shape(regions, rank, width), shape(regions, rank, 3 * width)),
        name="scale_steps",
    )(sums.reshape(pieces, regions, LANES))
    return (mixed_state, step_down, step_up)


def solution(mesh):
    field = P(None, "lat", "lon", None)
    placed = (field, P("lat", "lon"), P(None, "lat", "lon")) + (P(),) * 12 + (field,)
    return jax.shard_map(
        local, mesh=mesh, in_specs=placed, out_specs=(field, P(), P()), check_vma=False
    )
```

time: 373 us -> 131 us (0.35); the launches traced: 368 us -> 130 us
  waiting for transfers between devices: 181 us -> 12.5 us
  matrix products: 92.2 us -> 0 us
  Pallas kernels: 0 us -> 41.9 us
  blocking collectives: 0 us -> 22.2 us
  other arithmetic: 29.5 us -> 7.46 us
  between operations: 16.6 us -> 0.99 us
  local copies, waits for them, and re-layouts: 34.6 us -> 22 us
  starting transfers between devices: 13.5 us -> 23.5 us
    psum x1 -> x0, waiting for transfers between devices: 155 us -> none  [local(): lax.psum((partial_down_grad, partial_up_grad), ('lat', 'lon'))]
    dot_general x20 -> x0, matrix products: 92.2 us -> none  [the longest x3 29.4 us: attend(): scores = jnp.einsum('wqhe,wkhe->whqk', query, key, precision=HIGH)]
    pallas_call x0 -> x4, Pallas kernels: none -> 41.9 us  [the longest x1 21.9 us: local(): call(forward_kernel, (shape(tokens, width), shape(tokens, width, dtype=BF...]
    all_to_all x0 -> x1, blocking collectives: none -> 22.2 us  [local(): terms = lax.all_to_all(terms, ('lat', 'lon'), 0, 0, tiled=True)]
    ppermute x6 -> x9, waiting for transfers between devices: 26.4 us -> 12.5 us  [move(): return lax.ppermute(array, ('lat', 'lon'), halo_pairs(step))]
    reduce_sum x9 -> x0, other arithmetic: 10.4 us -> none  [the longest x2 4.34 us: local(): squares = jnp.sum(grad_down * grad_down) + jnp.sum(grad_up * grad_up)]
    unnamed x105 -> x16, local copies, waits for them, and re-layouts: 9.72 us -> 1.93 us
    add x1 -> x0, local copies, waits for them, and re-layouts: 6.34 us -> none  [apply_projection(): return (base.reshape(count, tokens, -1) + extra, low_rank_state)]
  transfers between devices with their start and end apart: 7 -> 10, of which waited for: 7 -> 1; matrix products, arithmetic and copies ran while one was open for 2% -> 16% of each run, Pallas kernels for 0% -> 0%
where the time goes in v1:
time: 131 us; the launch traced here: 130 us
  Pallas kernels  41.9 us (32%)
  starting transfers between devices  23.5 us (18%)
  blocking collectives  22.2 us (17%)
  local copies, waits for them, and re-layouts  22 us (17%)
  waiting for transfers between devices  12.5 us (10%)
  other arithmetic  7.46 us (6%)
    all_to_all x1, blocking collectives, local(): terms = lax.all_to_all(terms, ('lat', 'lon'), 0, 0, tiled=True)  22.2 us
    pallas_call x1, Pallas kernels, local(): call(forward_kernel, (shape(tokens, width), shape(tokens, width, dtype=BF...  21.9 us
    ppermute x9, starting transfers between devices, move(): return lax.ppermute(array, ('lat', 'lon'), halo_pairs(step))  18.2 us
    pallas_call x1, Pallas kernels, local(): call(backward_kernel, shape(pieces, 2 * count, LANES), (pltpu.VMEM((token...  13.6 us
    ppermute x9, waiting for transfers between devices, move(): return lax.ppermute(array, ('lat', 'lon'), halo_pairs(step))  12.5 us
    all_to_all x1, starting transfers between devices, local(): sums = lax.all_to_all(sums, ('lat', 'lon'), 0, 0, tiled=True)  5.3 us
    pallas_call x1, Pallas kernels, local(): call(reduce_kernel, shape(each, regions, LANES, dtype=BF16), name='sum_by...  3.46 us
    pallas_call x1, Pallas kernels, local(): call(scale_kernel, (shape(regions, rank, width), shape(regions, rank, 3 *...  3.05 us
  transfers between devices with their start and end apart: 10, of which 1 were waited for; matrix products, arithmetic and copies ran while one was open for 16% of the time, Pallas kernels for 0%

profile of v1, /device:TPU:1, one launch (start us, length us, event | category | flops | bytes accessed | tf_op | source)
XLA Modules:
  0.0 130.5 jit_solution(1272121705416822902)
XLA Ops:
  0.6 1.4 %convert_element_type.42 = bf16[4,6,24,512]{3,2,1,0:T(8,128)(2,1)S(1)} convert(f32[4,6,24,512]{3,2,1,0:T(8,128)} %param.31) | non-fusion elementwise | flops 294912 | bytes 1769472 | tf_op jit(solution)/shard_map/convert_element_type | solution.py:361
  2.1 0.9 fusion.8
  3.0 1.4 %collective-permute-start.4 = (bf16[4,3,18,512]{3,2,1,0:T(8,128)(2,1)}, bf16[4,3,18,512]{3,2,1,0:T(8,128)(2,1)S(1)}, u32[]{:S(2)}, u32[]{:S(2)}) collective-permute-start(bf16[4,3,18,512]{3,2,1,0:T(8,128)(2,1)} %get-tuple-element.30), channel_id=1, source_target_pairs={{0,96},{1,97},{2,98},{3,99},{4,100},{5,101},{6,102},{7,103},{8,104... | collective-permute-start | bytes 663560 | tf_op jit(solution)/shard_map/ppermute | solution.py:282
  4.4 0.7 fusion.9
  5.1 6.4 %collective-permute-start.3 = (bf16[4,3,6,512]{3,2,1,0:T(8,128)(2,1)}, bf16[4,3,6,512]{3,2,1,0:T(8,128)(2,1)S(1)}, u32[]{:S(2)}, u32[]{:S(2)}) collective-permute-start(bf16[4,3,6,512]{3,2,1,0:T(8,128)(2,1)} %get-tuple-element.31), channel_id=1, source_target_pairs={{0,31},{1,0},{2,1},{3,2},{4,3},{5,4},{6,5},{7,6},{8,7},{9,8},{10,9... | collective-permute-start | bytes 221192 | tf_op jit(solution)/shard_map/ppermute | solution.py:282
  11.5 3.3 %collective-permute-start.5 = (bf16[4,3,6,512]{3,2,1,0:T(8,128)(2,1)}, bf16[4,3,6,512]{3,2,1,0:T(8,128)(2,1)}, u32[]{:S(2)}, u32[]{:S(2)}) collective-permute-start(bf16[4,3,6,512]{3,2,1,0:T(8,128)(2,1)} %get-tuple-element.32), channel_id=1, source_target_pairs={{0,127},{1,96},{2,97},{3,98},{4,99},{5,100},{6,101},{7,102},{8,103... | collective-permute-start | bytes 221192 | tf_op jit(solution)/shard_map/ppermute | solution.py:282
  15.2 0.9 fusion.10
  16.0 0.7 fusion.11
  16.7 0.9 collective-permute-start
  17.7 0.5 broadcast.143
  18.2 0.7 reduce.5
  19.0 0.6 gather_fusion.1
  19.6 1.5 %gather_fusion = bf16[4,8,512]{2,1,0:T(8,128)(2,1)S(1)} fusion(bf16[32,8,512]{2,1,0:T(8,128)(2,1)} %param.24, s32[1024]{0:T(1024)S(1)} %pad_clamp_fusion), kind=kCustom, calls=%fused_computation | custom fusion | bytes 65552 | tf_op jit(solution)/shard_map/jit(_take)/gather | solution.py:363
  21.7 0.7 reshape.135.up_ref
  22.4 0.6 reshape.134.down_ref
  23.1 0.7 broadcast_in_dim_reshape.2.scale_ref
  23.7 0.2 tile.4
  24.0 1.6 %tile.10.same_ref = f32[2,144,576]{2,1,0:T(8,128)} reshape(f32[2,144,4,144]{3,2,1,0:T(4,128)S(1)} %tile.4) | data formatting | bytes 1327104 | tf_op jit(solution)/shard_map/tile | solution.py:326
  25.6 1.9 %pad.4.wp_ref = bf16[512,512]{1,0:T(8,128)(2,1)} pad(bf16[500,512]{1,0:T(8,128)(2,1)} %param.19, bf16[]{:T(256)} %constant.24.clone.1), padding=0_12x0_0 | pad | bytes 1036290 | tf_op jit(solution)/shard_map/jit(_pad)/pad | solution.py:362
  27.4 1.6 %collective-permute-start.2 = (bf16[4,3,6,512]{3,2,1,0:T(8,128)(2,1)S(1)}, bf16[4,3,6,512]{3,2,1,0:T(8,128)(2,1)S(1)}, u32[]{:S(2)}, u32[]{:S(2)}) collective-permute-start(bf16[4,3,6,512]{3,2,1,0:T(8,128)(2,1)S(1)} %copy-done.3), channel_id=1, source_target_pairs={{0,127},{1,96},{2,97},{3,98},{4,99},{5,100},{6,101},{7,102},{8,103... | collective-permute-start | bytes 221192 | tf_op jit(solution)/shard_map/ppermute | solution.py:282
  29.0 1.0 maximum_maximum_fusion.3
  30.1 0.8 fusion.2
  30.9 0.5 copy.36
  31.3 0.2 reshape.139
  31.7 1.0 reshape.140.cot_ref
  32.7 1.0 maximum_maximum_fusion.2
  33.7 0.8 fusion.4
  34.5 0.5 copy.32
  35.0 0.2 reshape.130
  35.4 1.0 reshape.131.pix_ref
  36.4 21.9 %layer_forward.1 = (f32[576,512]{1,0:T(8,128)}, bf16[576,512]{1,0:T(8,128)(2,1)}, bf16[576,32]{1,0:T(8,128)(2,1)}, f32[576,1024]{1,0:T(8,128)}, bf16[576,512]{1,...) custom-call(bf16[576,512]{1,0:T(8,128)(2,1)} %reshape.131.pix_ref, bf16[512,512]{1,0:T(8,128)(2,1)} %pad.4.wp_ref, ...), custom_call_target="tpu_custom_call" | custom-call | flops 6643777536 | bytes 20000000 | tf_op jit(solution)/shard_map/layer_forward/pallas_call | solution.py:368
  58.2 0.6 broadcast_in_dim.75.ids_ref
  58.9 13.6 %attention_backward.1 = f32[128,8,128]{2,1,0:T(8,128)} custom-call(bf16[576,512]{1,0:T(8,128)(2,1)} %get-tuple-element.13.normed_ref, bf16[576,32]{1,0:T(8,128)(2,1)} %get-tuple-element.14.low_ref, f32[576,1024]{1,0:T(8,128)} %get-tuple-element.15.qk_ref, bf16[576,512]{1,0:T(8,128)(2,1)} %get-tuple-element.16.v_ref, ...), custom_call_target="tpu_custom_call" | custom-call | flops 1207959552 | bytes 12000000 | tf_op jit(solution)/shard_map/attention_backward/pallas_call | solution.py:395
  72.4 22.2 %all_to_all.10 = f32[128,8,128]{2,1,0:T(8,128)} all-to-all(f32[128,8,128]{2,1,0:T(8,128)} %attention_backward.1), channel_id=1, replica_groups=mesh['lat'=4,'lon'=32] {'lat','lon'}, dimensions={0} | all-to-all | bytes 1048576 | tf_op jit(solution)/shard_map/all_to_all | solution.py:412
  94.7 3.5 %sum_by_region.1 = bf16[1,32,128]{2,1,0:T(8,128)(2,1)} custom-call(f32[128,1,8,128]{3,2,1,0:T(8,128)} %bitcast.33), custom_call_target="tpu_custom_call" | custom-call | tf_op jit(solution)/shard_map/sum_by_region/pallas_call | solution.py:414
  98.1 1.8 %broadcast_in_dim.77 = bf16[128,1,32,128]{3,2,1,0:T(8,128)(2,1)} broadcast(bf16[32,128]{1,0:T(8,128)(2,1)} %bitcast.34), dimensions={2,3} | broadcast | bytes 1056768 | tf_op jit(solution)/shard_map/broadcast_in_dim | solution.py:415
  99.9 5.3 %all-to-all-start.1 = ((bf16[128,1,32,128]{3,2,1,0:T(8,128)(2,1)}), bf16[128,1,32,128]{3,2,1,0:T(8,128)(2,1)}, u32[]{:S(2)}, u32[]{:S(2)}) async-start(bf16[128,1,32,128]{3,2,1,0:T(8,128)(2,1)} %broadcast_in_dim.77), calls=%async_computation.1 | async-start | bytes 2097152 | tf_op jit(solution)/shard_map/all_to_all | solution.py:416
  105.4 0.9 copy.38
  106.3 1.0 reshape.142
  107.3 0.3 slice.93
  107.6 0.6 fusion
  108.3 3.7 %collective-permute-start.7 = (bf16[4,3,18,512]{3,0,2,1:T(4,128)(2,1)S(1)}, bf16[4,3,18,512]{3,0,2,1:T(4,128)(2,1)S(1)}, u32[]{:S(2)}, u32[]{:S(2)}) collective-permute-start(bf16[4,3,18,512]{3,0,2,1:T(4,128)(2,1)S(1)} %slice.96), channel_id=1, source_target_pairs={{0,32},{1,33},{2,34},{3,35},{4,36},{5,37},{6,38},{7,39},{8,40},{9,... | collective-permute-start | bytes 663560 | tf_op jit(solution)/shard_map/ppermute | solution.py:282
  112.3 0.7 collective-permute-start.8
  112.9 0.2 fusion.5
  113.1 12.4 %collective-permute-done.8 = bf16[4,3,6,512]{3,0,2,1:T(4,128)(2,1)S(1)} collective-permute-done((bf16[4,3,6,512]{3,0,2,1:T(4,128)(2,1)S(1)}, bf16[4,3,6,512]{3,0,2,1:T(4,128)(2,1)S(1)}, u32[]{:S(2)}, u32[]{:S(2)}) %collective-permute-start.8) | collective-permute-done | bytes 73760 | tf_op jit(solution)/shard_map/ppermute | solution.py:282
  125.8 0.3 maximum_maximum_fusion
  126.1 1.4 %copy.39 = f32[4,6,24,512]{3,2,1,0:T(8,128)} copy(f32[4,6,24,512]{3,0,2,1:T(4,128)S(1)} %maximum_maximum_fusion) | data formatting | bytes 2359296
  127.4 3.0 %scale_steps.1 = (f32[32,8,512]{2,1,0:T(8,128)}, f32[32,8,1536]{2,1,0:T(8,128)}) custom-call(bf16[128,32,128]{2,1,0:T(8,128)(2,1)} %bitcast.12.sums_ref), custom_call_target="tpu_custom_call" | custom-call | tf_op jit(solution)/shard_map/scale_steps/pallas_call | solution.py:417
  (57 shorter events, 2.3 us)
Async XLA Ops:
  0.6 18.4 %copy-start = (bf16[32,8,1536]{2,1,0:T(8,128)(2,1)S(1)}, bf16[32,8,1536]{2,1,0:T(8,128)(2,1)}, u32[]{:S(2)}) copy-start(bf16[32,8,1536]{2,1,0:T(8,128)(2,1)} %param.25) | copy-start | bytes 2359300
  2.1 12.7 %copy-start.4 = (s32[6,24]{1,0:T(8,128)S(1)}, s32[6,24]{1,0:T(8,128)}, u32[]{:S(2)}) copy-start(s32[6,24]{1,0:T(8,128)} %param.17) | copy-start | bytes 1732
  2.1 12.9 %copy-start.2 = (bf16[4,6,24,500]{3,2,1,0:T(8,128)(2,1)S(1)}, bf16[4,6,24,500]{3,2,1,0:T(8,128)(2,1)}, u32[]{:S(2)}) copy-start(bf16[4,6,24,500]{3,2,1,0:T(8,128)(2,1)} %param.16) | copy-start | bytes 1728004
  3.0 26.0 %collective-permute-start.4 = (bf16[4,3,18,512]{3,2,1,0:T(8,128)(2,1)}, bf16[4,3,18,512]{3,2,1,0:T(8,128)(2,1)S(1)}, u32[]{:S(2)}, u32[]{:S(2)}) collective-permute-start(bf16[4,3,18,512]{3,2,1,0:T(8,128)(2,1)} %get-tuple-element.30), channel_id=1, source_target_pairs={{0,96},{1,97},{2,98},{3,99},{4,100},{5,101},{6,102},{7,103},{8,104... | collective-permute-start | bytes 663560 | tf_op jit(solution)/shard_map/ppermute | solution.py:282
  5.1 22.4 %collective-permute-start.3 = (bf16[4,3,6,512]{3,2,1,0:T(8,128)(2,1)}, bf16[4,3,6,512]{3,2,1,0:T(8,128)(2,1)S(1)}, u32[]{:S(2)}, u32[]{:S(2)}) collective-permute-start(bf16[4,3,6,512]{3,2,1,0:T(8,128)(2,1)} %get-tuple-element.31), channel_id=1, source_target_pairs={{0,31},{1,0},{2,1},{3,2},{4,3},{5,4},{6,5},{7,6},{8,7},{9,8},{10,9... | collective-permute-start | bytes 221192 | tf_op jit(solution)/shard_map/ppermute | solution.py:282
  11.5 17.6 %collective-permute-start.5 = (bf16[4,3,6,512]{3,2,1,0:T(8,128)(2,1)}, bf16[4,3,6,512]{3,2,1,0:T(8,128)(2,1)}, u32[]{:S(2)}, u32[]{:S(2)}) collective-permute-start(bf16[4,3,6,512]{3,2,1,0:T(8,128)(2,1)} %get-tuple-element.32), channel_id=1, source_target_pairs={{0,127},{1,96},{2,97},{3,98},{4,99},{5,100},{6,101},{7,102},{8,103... | collective-permute-start | bytes 221192 | tf_op jit(solution)/shard_map/ppermute | solution.py:282
  15.0 3.2 %copy-start.5 = (s32[2,1,2]{2,1,0:T(1,128)S(1)}, s32[2,1,2]{2,1,0:T(1,128)}, u32[]{:S(2)}) copy-start(s32[2,1,2]{2,1,0:T(1,128)} %param.18) | copy-start | bytes 52
  15.2 6.5 %copy-start.6 = (f32[16]{0:T(128)S(1)}, f32[16]{0:T(128)}, u32[]{:S(2)}) copy-start(f32[16]{0:T(128)} %param.26) | copy-start | bytes 196
  16.0 16.7 %collective-permute-start.1 = (bf16[4,3,18,512]{3,2,1,0:T(8,128)(2,1)}, bf16[4,3,18,512]{3,2,1,0:T(8,128)(2,1)S(1)}, u32[]{:S(2)}, u32[]{:S(2)}) collective-permute-start(bf16[4,3,18,512]{3,2,1,0:T(8,128)(2,1)} %get-tuple-element.34), channel_id=1, source_target_pairs={{0,96},{1,97},{2,98},{3,99},{4,100},{5,101},{6,102},{7,103},{8,104... | collective-permute-start | bytes 663560 | tf_op jit(solution)/shard_map/ppermute | solution.py:282
  16.7 15.9 %collective-permute-start = (bf16[4,3,6,512]{3,2,1,0:T(8,128)(2,1)}, bf16[4,3,6,512]{3,2,1,0:T(8,128)(2,1)}, u32[]{:S(2)}, u32[]{:S(2)}) collective-permute-start(bf16[4,3,6,512]{3,2,1,0:T(8,128)(2,1)} %get-tuple-element.35), channel_id=1, source_target_pairs={{0,31},{1,0},{2,1},{3,2},{4,3},{5,4},{6,5},{7,6},{8,7},{9,8},{10,9... | collective-permute-start | bytes 221192 | tf_op jit(solution)/shard_map/ppermute | solution.py:282
  24.0 3.5 %copy-start.3 = (bf16[4,3,6,512]{3,2,1,0:T(8,128)(2,1)S(1)}, bf16[4,3,6,512]{3,2,1,0:T(8,128)(2,1)}, u32[]{:S(2)}) copy-start(bf16[4,3,6,512]{3,2,1,0:T(8,128)(2,1)} %get-tuple-element.36) | copy-start | bytes 221188
  27.4 5.3 %collective-permute-start.2 = (bf16[4,3,6,512]{3,2,1,0:T(8,128)(2,1)S(1)}, bf16[4,3,6,512]{3,2,1,0:T(8,128)(2,1)S(1)}, u32[]{:S(2)}, u32[]{:S(2)}) collective-permute-start(bf16[4,3,6,512]{3,2,1,0:T(8,128)(2,1)S(1)} %copy-done.3), channel_id=1, source_target_pairs={{0,127},{1,96},{2,97},{3,98},{4,99},{5,100},{6,101},{7,102},{8,103... | collective-permute-start | bytes 221192 | tf_op jit(solution)/shard_map/ppermute | solution.py:282
  99.9 5.3 %copy-start.1 = (f32[576,512]{1,0:T(8,128)S(1)}, f32[576,512]{1,0:T(8,128)}, u32[]{:S(2)}) copy-start(f32[576,512]{1,0:T(8,128)} %get-tuple-element.12) | copy-start | bytes 3538948
  99.9 27.5 %all-to-all-start.1 = ((bf16[128,1,32,128]{3,2,1,0:T(8,128)(2,1)}), bf16[128,1,32,128]{3,2,1,0:T(8,128)(2,1)}, u32[]{:S(2)}, u32[]{:S(2)}) async-start(bf16[128,1,32,128]{3,2,1,0:T(8,128)(2,1)} %broadcast_in_dim.77), calls=%async_computation.1 | async-start | bytes 2097152 | tf_op jit(solution)/shard_map/all_to_all | solution.py:416
  108.3 17.3 %collective-permute-start.7 = (bf16[4,3,18,512]{3,0,2,1:T(4,128)(2,1)S(1)}, bf16[4,3,18,512]{3,0,2,1:T(4,128)(2,1)S(1)}, u32[]{:S(2)}, u32[]{:S(2)}) collective-permute-start(bf16[4,3,18,512]{3,0,2,1:T(4,128)(2,1)S(1)} %slice.96), channel_id=1, source_target_pairs={{0,32},{1,33},{2,34},{3,35},{4,36},{5,37},{6,38},{7,39},{8,40},{9,... | collective-permute-start | bytes 663560 | tf_op jit(solution)/shard_map/ppermute | solution.py:282
  112.1 13.5 %collective-permute-start.6 = (bf16[4,3,6,512]{3,0,2,1:T(4,128)(2,1)S(1)}, bf16[4,3,6,512]{3,0,2,1:T(4,128)(2,1)S(1)}, u32[]{:S(2)}, u32[]{:S(2)}) collective-permute-start(bf16[4,3,6,512]{3,0,2,1:T(4,128)(2,1)S(1)} %get-tuple-element.27), channel_id=1, source_target_pairs={{0,33},{1,34},{2,35},{3,36},{4,37},{5,38},{6,39},{7,40},{8,41},{9,... | collective-permute-start | bytes 221192 | tf_op jit(solution)/shard_map/ppermute | solution.py:282
  112.3 13.3 %collective-permute-start.8 = (bf16[4,3,6,512]{3,0,2,1:T(4,128)(2,1)S(1)}, bf16[4,3,6,512]{3,0,2,1:T(4,128)(2,1)S(1)}, u32[]{:S(2)}, u32[]{:S(2)}) collective-permute-start(bf16[4,3,6,512]{3,0,2,1:T(4,128)(2,1)S(1)} %get-tuple-element.28), channel_id=1, source_target_pairs={{0,1},{1,2},{2,3},{3,4},{4,5},{5,6},{6,7},{7,8},{8,9},{9,10},{10,1... | collective-permute-start | bytes 221192 | tf_op jit(solution)/shard_map/ppermute | solution.py:282

commit v2 on v1

v2 whole, which is shorter than its diff:
```python
import jax
import jax.numpy as jnp
from jax import lax
from jax.experimental import pallas as pl
from jax.experimental.pallas import tpu as pltpu
from jax.sharding import PartitionSpec as P

WLEV = 2
WLAT = 6
WLON = 12
TOKENS = WLEV * WLAT * WLON
HALF_LAT = WLAT // 2
HALF_LON = WLON // 2
LANES = 128
HEAD = 32
PER_GROUP = LANES // HEAD

AXES = ("lat", "lon")
F32 = jnp.float32
BF16 = jnp.bfloat16


def mm(a, b):
    return lax.dot_general(a, b, (((1,), (0,)), ((), ())), preferred_element_type=F32)


def mm_nt(a, b):
    return lax.dot_general(a, b, (((1,), (1,)), ((), ())), preferred_element_type=F32)


def mm_tn(a, b):
    return lax.dot_general(a, b, (((0,), (0,)), ((), ())), preferred_element_type=F32)


def head_mean(squares):
    rows = lax.broadcasted_iota(jnp.int32, (LANES, LANES), 0) // HEAD
    cols = lax.broadcasted_iota(jnp.int32, (LANES, LANES), 1) // HEAD
    block = jnp.where(rows == cols, 1.0 / HEAD, 0.0).astype(BF16)
    parts = []
    for g in range(squares.shape[1] // LANES):
        part = squares[:, g * LANES : (g + 1) * LANES]
        top = part.astype(BF16)
        rest = (part - top.astype(F32)).astype(BF16)
        parts.append(mm(top, block) + mm(rest, block))
    return jnp.concatenate(parts, axis=1)


def head_masks():
    lane = lax.broadcasted_iota(jnp.int32, (1, LANES), 1) // HEAD
    return [jnp.where(lane == h, 1.0, 0.0).astype(F32) for h in range(PER_GROUP)]


def stack_heads(x, masks):
    return jnp.concatenate([(x * m).astype(BF16) for m in masks], axis=0)


def unstack_heads(x, masks):
    tokens = x.shape[0] // PER_GROUP
    return sum(x[h * tokens : (h + 1) * tokens] * m for h, m in enumerate(masks))


def adapter_columns(tokens, columns):
    rank = columns // (tokens // TOKENS)
    own = lax.broadcasted_iota(jnp.int32, (tokens, columns), 0)
    first = lax.broadcasted_iota(jnp.int32, (tokens, columns), 1) // rank * TOKENS
    return jnp.where((own >= first) & (own < first + TOKENS), 1.0, 0.0)


def factors(region_ref, factor_ref, all_ref):
    rank = factor_ref.shape[1]
    ids = [region_ref[a, 0, b] for a in range(region_ref.shape[0]) for b in range(region_ref.shape[2])]
    for w, r in enumerate(ids):
        all_ref[w * rank : (w + 1) * rank, :] = factor_ref[r].astype(F32)
    return all_ref[...].astype(BF16)


def scale_row(scale_ref, width):
    head = lax.broadcasted_iota(jnp.int32, (1, width), 1) // HEAD
    row = jnp.zeros((1, width), F32)
    for h in range(width // HEAD):
        row = jnp.where(head == h, scale_ref[h] / HEAD, row)
    return row


def same_group(level, south):
    def group(token):
        late = jnp.where(token >= TOKENS // WLEV, 1, 0) * level
        low = jnp.where(token // WLON % WLAT >= HALF_LAT, 1, 0) * south
        return 2 * late + low

    keys = lax.broadcasted_iota(jnp.int32, (TOKENS, 1), 0)
    queries = lax.broadcasted_iota(jnp.int32, (1, PER_GROUP * TOKENS), 1) % TOKENS
    return jnp.where(group(keys) == group(queries), 1.0, 0.0)


def pieces_of(shape):
    levels, _, cols, _ = shape
    across = (cols + HALF_LON) // WLON
    for level in range(levels):
        for row in range(WLAT):
            within = level % WLEV * WLAT * WLON + row * WLON
            starts = [((level // WLEV) * across + b) * TOKENS + within for b in range(across)]
            yield (level + WLEV // 2) % levels, row // HALF_LAT, row % HALF_LAT, starts


def into_windows(stage_ref, own_ref, south_ref, east_ref, corner_ref):
    for level, half, row, starts in pieces_of(own_ref.shape):
        wide = (south_ref if half else own_ref)[level, row].astype(F32)
        narrow = (corner_ref if half else east_ref)[level, row].astype(F32)
        for b, start in enumerate(starts[:-1]):
            stage_ref[start : start + WLON, :] = wide[b * WLON : (b + 1) * WLON]
        start = starts[-1]
        stage_ref[start : start + HALF_LON, :] = wide[-HALF_LON:]
        stage_ref[start + HALF_LON : start + WLON, :] = narrow


def out_of_windows(stage_ref, own_ref, north_ref, west_ref, corner_ref):
    for level, half, row, starts in pieces_of(own_ref.shape):
        wide = [stage_ref[start : start + WLON, :] for start in starts[:-1]]
        start = starts[-1]
        wide.append(stage_ref[start : start + HALF_LON, :])
        narrow = stage_ref[start + HALF_LON : start + WLON, :]
        wide_ref, narrow_ref = (north_ref, corner_ref) if half else (own_ref, west_ref)
        wide_ref[level, row] = jnp.concatenate(wide, axis=0).astype(wide_ref.dtype)
        narrow_ref[level, row] = narrow.astype(narrow_ref.dtype)


def norm_stats(x):
    width = x.shape[1]
    mean = jnp.sum(x, axis=1, keepdims=True) * (1.0 / width)
    centred = x - mean
    spread = jnp.sum(centred * centred, axis=1, keepdims=True) * (1.0 / width)
    return centred, lax.rsqrt(spread + 1e-05)


def gelu_and_slope(u):
    x = jnp.abs(u) * 0.7071067811865476
    t = 1.0 / (1.0 + 0.3275911 * x)
    e = jnp.exp(-0.5 * u * u)
    poly = 1.061405429
    for c in (-1.453152027, 1.421413741, -0.284496736, 0.254829592):
        poly = poly * t + c
    tail = 0.5 * poly * t * e
    phi = jnp.where(u < 0, tail, 1.0 - tail)
    return u * phi, phi + u * (0.3989422804014327 * e)


def attention_kernel(
    region_ref, temper_ref, own_ref, south_ref, east_ref, corner_ref, wp_ref, bias_ref, land_ref,
    gain_ref, wqkv_ref, down_ref, up_ref, wo_ref,
    hidden_ref, normed_ref, low_ref, qk_ref, v_ref, probs_ref,
    state_ref, qs_ref, kn_ref, att_ref, downs_ref, ups_ref, same_ref,
):
    tokens, width = state_ref.shape
    count = tokens // TOKENS
    groups = width // LANES
    masks = head_masks()
    patch_len = wp_ref.shape[0]
    into_windows(state_ref, own_ref, south_ref, east_ref, corner_ref)
    pix = state_ref[:, :patch_len].astype(BF16)
    land = state_ref[:, patch_len : patch_len + 1]
    state = mm(pix, wp_ref[...]) + bias_ref[...] + land * land_ref[...]
    state_ref[...] = state
    centred, inv = norm_stats(state)
    normed = (centred * inv * gain_ref[...]).astype(BF16)
    normed_ref[...] = normed
    downs = factors(region_ref, down_ref, downs_ref)
    ups = factors(region_ref, up_ref, ups_ref)
    low = (mm_nt(normed, downs) * adapter_columns(tokens, downs.shape[0])).astype(BF16)
    low_ref[...] = low
    scale = scale_row(temper_ref, width)
    for part in range(3):
        cols = slice(part * width, (part + 1) * width)
        qkv = mm(normed, wqkv_ref[:, cols]) + mm(low, ups[:, cols])
        if part == 2:
            v_ref[...] = qkv.astype(BF16)
        else:
            qk_ref[:, cols] = qkv
            unit = qkv * lax.rsqrt(head_mean(qkv * qkv) + 1e-06)
            if part == 0:
                qs_ref[...] = unit * scale
            else:
                kn_ref[...] = unit.astype(BF16)
    last_band = lax.axis_index("lat") == lax.axis_size("lat") - 1
    south = jnp.where(last_band, 1, 0).astype(jnp.int32)
    parts = same_ref.shape[0]
    for part in range(parts):
        same_ref[part] = same_group(1 if part == parts - 1 else 0, south)

    def window(w, carry):
        rows = pl.ds(pl.multiple_of(w * TOKENS, TOKENS), TOKENS)
        same = same_ref[w // (count // parts)]
        for g in range(groups):
            cols = slice(g * LANES, (g + 1) * LANES)
            stack = stack_heads(qs_ref[rows, cols], masks)
            weights = jnp.exp(mm_nt(kn_ref[rows, cols], stack)) * same
            total = jnp.sum(weights, axis=0, keepdims=True)
            probs = (weights * (1.0 / total)).astype(BF16)
            probs_ref[w * groups + g] = probs
            mixed = mm_tn(probs, v_ref[rows, cols])
            att_ref[rows, cols] = unstack_heads(mixed, masks).astype(BF16)
        return carry

    lax.fori_loop(0, count, window, 0)
    z = mm(att_ref[...], wo_ref[...]).astype(BF16)
    hidden_ref[...] = state_ref[...] + z.astype(F32)


def feed_kernel(
    hidden_ref, own_ref, south_ref, east_ref, corner_ref, gain_ref, wup_ref, wdn_ref, wo_ref,
    home_ref, north_ref, west_ref, diagonal_ref, datt_ref,
    cot_ref, mixed_ref, unit_ref,
):
    tokens, width = hidden_ref.shape
    into_windows(cot_ref, own_ref, south_ref, east_ref, corner_ref)
    hidden = hidden_ref[...]
    centred, inv = norm_stats(hidden)
    unit = centred * inv
    normed = (unit * gain_ref[...]).astype(BF16)
    cot = cot_ref[...].astype(BF16)
    mixed_ref[...] = hidden
    unit_ref[...] = unit
    d_normed = jnp.zeros((tokens, width), F32)
    chunk = 512
    for c in range(wup_ref.shape[1] // chunk):
        cols = slice(c * chunk, (c + 1) * chunk)
        act, slope = gelu_and_slope(mm(normed, wup_ref[:, cols]))
        mixed_ref[...] += mm(act.astype(BF16), wdn_ref[cols, :])
        d_up = mm_nt(cot, wdn_ref[cols, :]) * slope
        d_normed += mm_nt(d_up.astype(BF16), wup_ref[:, cols])
    out_of_windows(mixed_ref, home_ref, north_ref, west_ref, diagonal_ref)
    d_unit = d_normed * gain_ref[...]
    unit = unit_ref[...]
    first = jnp.sum(d_unit, axis=1, keepdims=True) * (1.0 / width)
    second = jnp.sum(d_unit * unit, axis=1, keepdims=True) * (1.0 / width)
    d_hidden = cot_ref[...] + inv * (d_unit - first - unit * second)
    datt_ref[...] = mm_nt(d_hidden.astype(BF16), wo_ref[...]).astype(BF16)


def backward_kernel(
    region_ref, temper_ref, normed_ref, low_ref, qk_ref, v_ref, probs_ref, datt_ref, up_ref,
    terms_ref,
    qs_ref, kn_ref, dq_ref, dk_ref, dqkv_ref, ups_ref, grads_ref,
):
    tokens, width = normed_ref.shape
    count = tokens // TOKENS
    groups = width // LANES
    masks = head_masks()
    scale = scale_row(temper_ref, width)
    inv = []
    for part in range(2):
        raw = qk_ref[:, part * width : (part + 1) * width]
        inv.append(lax.rsqrt(head_mean(raw * raw) + 1e-06))
        if part == 0:
            qs_ref[...] = raw * inv[0] * scale
        else:
            kn_ref[...] = (raw * inv[1]).astype(BF16)

    def window(w, carry):
        rows = pl.ds(pl.multiple_of(w * TOKENS, TOKENS), TOKENS)
        for g in range(groups):
            cols = slice(g * LANES, (g + 1) * LANES)
            d_stack = stack_heads(datt_ref[rows, cols].astype(F32), masks)
            q_stack = stack_heads(qs_ref[rows, cols], masks)
            probs = probs_ref[w * groups + g]
            d_probs = mm_nt(v_ref[rows, cols], d_stack)
            wide = probs.astype(F32)
            prod = wide * d_probs
            d_scores = (prod - wide * jnp.sum(prod, axis=0, keepdims=True)).astype(BF16)
            dqkv_ref[rows, slice(2 * width + g * LANES, 2 * width + (g + 1) * LANES)] = mm(
                probs, d_stack
            ).astype(BF16)
            dk_ref[rows, cols] = mm(d_scores, q_stack)
            dq_ref[rows, cols] = unstack_heads(mm_tn(d_scores, kn_ref[rows, cols]), masks)
        return carry

    lax.fori_loop(0, count, window, 0)
    for part, grad_ref in enumerate((dq_ref, dk_ref)):
        cols = slice(part * width, (part + 1) * width)
        unit = qk_ref[:, cols] * inv[part]
        grad = grad_ref[...] * scale if part == 0 else grad_ref[...]
        dqkv_ref[:, cols] = (inv[part] * (grad - unit * head_mean(grad * unit))).astype(BF16)
    ups = factors(region_ref, up_ref, ups_ref)
    d_qkv = dqkv_ref[...]
    back = (mm_nt(d_qkv, ups) * adapter_columns(tokens, ups.shape[0])).astype(BF16)
    grads_ref[:, :width] = mm_tn(back, normed_ref[...])
    grads_ref[:, width:] = mm_tn(low_ref[...], d_qkv)
    blocks = grads_ref.shape[1] // LANES
    rank = grads_ref.shape[0] // count
    row = lax.broadcasted_iota(jnp.int32, (count, LANES), 0)
    ids = jnp.zeros((count, LANES), F32)
    per = region_ref.shape[2]
    for w in range(count):
        ids = jnp.where(row == w, region_ref[w // per, 0, w % per].astype(F32), ids)
    for b in range(blocks):
        cols = slice(b * LANES, (b + 1) * LANES)
        for r in range(rank):
            own = [grads_ref[w * rank + r : w * rank + r + 1, cols] for w in range(count)]
            tile = jnp.concatenate(own + [ids], axis=0)
            terms_ref[r * blocks + b] = tile.astype(terms_ref.dtype)


def reduce_kernel(terms_ref, sums_ref):
    _, pieces, regions, _ = sums_ref.shape
    devices, _, height, _ = terms_ref.shape
    for p in range(pieces):
        tile = terms_ref[:, p].astype(F32).reshape(devices * height, LANES)
        ids = pltpu.roll(tile, devices * height - height // 2, 0)
        row = lax.broadcasted_iota(jnp.int32, tile.shape, 0) % height
        lane = lax.broadcasted_iota(jnp.int32, tile.shape, 1).astype(F32)
        hot = jnp.where((ids == lane) & (row < height // 2), 1.0, 0.0).astype(BF16)
        sums = mm_tn(hot, tile.astype(BF16))[:regions].astype(sums_ref.dtype)
        for d in range(sums_ref.shape[0]):
            sums_ref[d, p] = sums


def scale_kernel(near_ref, far_ref, down_ref, up_ref, all_ref):
    regions, _, width = down_ref.shape
    rank, blocks = all_ref.shape[:2]
    outer, inner = near_ref.shape[:2]
    core = lax.axis_index("lat") % 2
    total = jnp.zeros((regions, LANES), F32)
    for side, ref in enumerate((near_ref, far_ref)):
        which = core if side == 0 else 1 - core
        for a in range(outer):
            for r in range(inner):
                for b in range(blocks):
                    part = ref[a, r, b].astype(F32)
                    total += part * part
                    all_ref[(a * 2 + which) * inner + r, b] = part
    size = rank * blocks * regions * LANES
    total = jnp.sum(jnp.sum(total, axis=0, keepdims=True), axis=1, keepdims=True)
    factor = lax.rsqrt(total * (1.0 / size) + 1e-06)
    for b in range(blocks):
        part = jnp.swapaxes(all_ref[:, b] * factor, 0, 1)
        start = b * LANES
        if start < width:
            down_ref[:, :, start : start + LANES] = part
        else:
            up_ref[:, :, start - width : start - width + LANES] = part


SMEM = pl.BlockSpec(memory_space=pltpu.SMEM)
VMEM = pl.BlockSpec(memory_space=pltpu.VMEM)


def call(kernel, places, outs, scratch=(), flops=0, moved=0, mib=32, name=None):
    return pl.pallas_call(
        kernel,
        in_specs=places,
        out_shape=outs,
        scratch_shapes=[pltpu.VMEM(dims, dtype) for dims, dtype in scratch],
        compiler_params=pltpu.CompilerParams(vmem_limit_bytes=mib * 1024 * 1024),
        cost_estimate=pl.CostEstimate(flops=flops, bytes_accessed=moved, transcendentals=0),
        name=name,
    )


def shape(*dims, dtype=F32):
    return jax.ShapeDtypeStruct(dims, dtype)


def move(array, step):
    lats, lons = lax.axis_size("lat"), lax.axis_size("lon")

    def index(a, b):
        return (a % lats) * lons + b % lons

    pairs = [
        (index(a, b), index(a + step[0], b + step[1])) for a in range(lats) for b in range(lons)
    ]
    return lax.ppermute(array, ("lat", "lon"), pairs)


def halves(field):
    south = move(field[:, :HALF_LAT, HALF_LON:], (-1, 0))
    east = move(field[:, HALF_LAT:, :HALF_LON], (0, -1))
    corner = move(field[:, :HALF_LAT, :HALF_LON], (-1, -1))
    return field[:, HALF_LAT:, HALF_LON:], south, east, corner


def local(
    pixels,
    land_patch_mask,
    region,
    patch_embed_weight,
    patch_embed_bias,
    land_embedding_vector,
    attention_norm_gain,
    query_key_value_weight,
    region_down_factor,
    region_up_factor,
    head_logit_scale,
    attention_output_weight,
    feedforward_gain,
    feedforward_up_weight,
    feedforward_down_weight,
    cotangent,
):
    levels, rows, cols, patch_len = pixels.shape
    width = patch_embed_weight.shape[1]
    inner = feedforward_up_weight.shape[1]
    regions, rank, _ = region_down_factor.shape
    count = region.size
    tokens = count * TOKENS
    groups = width // LANES
    devices = lax.axis_size("lat") * lax.axis_size("lon")
    spare = width - patch_len - 1

    land = jnp.broadcast_to(land_patch_mask.astype(BF16)[None, :, :, None], (levels, rows, cols, 1))
    blank = jnp.zeros((levels, rows, cols, spare), BF16)
    pix = halves(jnp.concatenate((pixels, land, blank), axis=3))
    cot = halves(cotangent.astype(BF16))

    wide = (levels, HALF_LAT, cols - HALF_LON, width)
    narrow = (levels, HALF_LAT, HALF_LON, width)
    hidden, normed, low, qk, v, probs = call(
        attention_kernel,
        [SMEM] * 2 + [VMEM] * 12,
        (
            shape(tokens, width),
            shape(tokens, width, dtype=BF16),
            shape(tokens, rank * count, dtype=BF16),
            shape(tokens, 2 * width),
            shape(tokens, width, dtype=BF16),
            shape(count * groups, TOKENS, PER_GROUP * TOKENS, dtype=BF16),
        ),
        (
            ((tokens, width), F32),
            ((tokens, width), F32),
            ((tokens, width), BF16),
            ((tokens, width), BF16),
            ((rank * count, width), F32),
            ((rank * count, 3 * width), F32),
            ((levels // WLEV, TOKENS, PER_GROUP * TOKENS), F32),
        ),
        flops=2 * tokens * width * 6 * width,
        moved=20_000_000,
        name="attention_forward",
    )(
        region, head_logit_scale, *pix, patch_embed_weight, patch_embed_bias[None],
        land_embedding_vector[None], attention_norm_gain[None], query_key_value_weight,
        region_down_factor, region_up_factor, attention_output_weight,
    )
    home, north, west, diagonal, d_att = call(
        feed_kernel,
        [VMEM] * 9,
        (
            shape(*wide),
            shape(*wide, dtype=BF16),
            shape(*narrow, dtype=BF16),
            shape(*narrow, dtype=BF16),
            shape(tokens, width, dtype=BF16),
        ),
        (((tokens, width), F32),) * 3,
        flops=2 * tokens * width * 4 * inner,
        moved=20_000_000,
        name="feed_forward",
    )(
        hidden, *cot, feedforward_gain[None], feedforward_up_weight, feedforward_down_weight,
        attention_output_weight,
    )
    north = move(north, (1, 0)).astype(F32)
    west = move(west, (0, 1)).astype(F32)
    diagonal = move(diagonal, (1, 1)).astype(F32)
    pieces = rank * 4 * width // LANES
    terms = call(
        backward_kernel,
        [SMEM] * 2 + [VMEM] * 7,
        shape(pieces, 2 * count, LANES, dtype=BF16),
        (
            ((tokens, width), F32),
            ((tokens, width), BF16),
            ((tokens, width), F32),
            ((tokens, width), F32),
            ((tokens, 3 * width), BF16),
            ((rank * count, 3 * width), F32),
            ((rank * count, 4 * width), F32),
        ),
        flops=2 * tokens * width * 4 * width,
        moved=12_000_000,
        name="attention_backward",
    )(region, head_logit_scale, normed, low, qk, v, probs, d_att, region_up_factor)
    upper = jnp.concatenate((diagonal, north), axis=2)
    lower = jnp.concatenate((west, home), axis=2)
    mixed_state = jnp.concatenate((upper, lower), axis=1)

    each = pieces // devices
    terms = lax.all_to_all(terms, AXES, 0, 0, tiled=True)
    sums = call(
        reduce_kernel,
        [VMEM],
        shape(devices // 2, each, regions, LANES, dtype=BF16),
        name="sum_by_region",
    )(terms.reshape(devices, each, 2 * count, LANES))
    lats, lons = lax.axis_size("lat"), lax.axis_size("lon")
    cores = [[a * lons + b for a in range(c, lats, 2) for b in range(lons)] for c in range(2)]
    near = lax.all_to_all(sums, AXES, 0, 0, axis_index_groups=cores, tiled=True)
    far = lax.ppermute(near, "lat", [(a, a ^ 1) for a in range(lats)])
    blocks = 4 * width // LANES
    order = (lats // 2, rank // lats, blocks, regions, LANES)
    step_down, step_up = call(
        scale_kernel,
        [VMEM] * 2,
        (shape(regions, rank, width), shape(regions, rank, 3 * width)),
        (((rank, blocks, regions, LANES), F32),),
        name="scale_steps",
    )(near.reshape(order), far.reshape(order))
    return (mixed_state, step_down, step_up)


def solution(mesh):
    field = P(None, "lat", "lon", None)
    placed = (field, P("lat", "lon"), P(None, "lat", "lon")) + (P(),) * 12 + (field,)
    return jax.shard_map(
        local, mesh=mesh, in_specs=placed, out_specs=(field, P(), P()), check_vma=False
    )
```

time: 131 us -> 101 us (0.77)
  local copies, waits for them, and re-layouts: 22 us -> 0.6 us
  blocking collectives: 22.2 us -> 34.4 us
  Pallas kernels: 41.9 us -> 31 us
  other arithmetic: 7.46 us -> 3.41 us
  waiting for transfers between devices: 12.5 us -> 8.68 us
  starting transfers between devices: 23.5 us -> 21.5 us
    all_to_all x1 -> x2, blocking collectives: 22.2 us -> 34.4 us  [the longest x1 19.7 us: local(): terms = lax.all_to_all(terms, AXES, 0, 0, tiled=True)]
    pallas_call x4 -> x5, Pallas kernels: 41.9 us -> 31 us  [the longest x1 10.3 us: local(): call(backward_kernel, [SMEM] * 2 + [VMEM] * 7, shape(pieces, 2 * count, L...]
    all_to_all x1 -> x0, starting transfers between devices: 5.3 us -> none  [local(): sums = lax.all_to_all(sums, ('lat', 'lon'), 0, 0, tiled=True)]
    reshape x10 -> x0, local copies, waits for them, and re-layouts: 4.97 us -> none  [the longest x2 1.94 us: to_windows(): return field.transpose(0, 2, 4, 1, 3, 5, 6).reshape(-1, width)]
    ppermute x9 -> x10, waiting for transfers between devices: 12.5 us -> 8.68 us  [the longest x9 8.68 us: move(): return lax.ppermute(array, ('lat', 'lon'), pairs)]
    slice x9 -> x4, local copies, waits for them, and re-layouts: 3.64 us -> 0.35 us  [the longest x2 0.32 us: halves(): south = move(field[:, :HALF_LAT, HALF_LON:], (-1, 0))]
    ppermute x9 -> x10, starting transfers between devices: 18.2 us -> 21.5 us  [the longest x9 18.4 us: move(): return lax.ppermute(array, ('lat', 'lon'), pairs)]
    broadcast_in_dim x5 -> x1, local copies, waits for them, and re-layouts: 2.59 us -> 0.01 us  [local(): blank = jnp.zeros((levels, rows, cols, spare), BF16)]
  transfers between devices with their start and end apart: 10 -> 10, of which waited for: 1 -> 2; matrix products, arithmetic and copies ran while one was open for 16% -> 2% of each run, Pallas kernels for 0% -> 9%
where the time goes in v2:
time: 101 us
  blocking collectives  34.4 us (34%)
  Pallas kernels  31 us (31%)
  starting transfers between devices  21.5 us (21%)
  waiting for transfers between devices  8.68 us (9%)
  other arithmetic  3.41 us (3%)
    all_to_all x1, blocking collectives, local(): terms = lax.all_to_all(terms, AXES, 0, 0, tiled=True)  19.7 us
    ppermute x9, starting transfers between devices, move(): return lax.ppermute(array, ('lat', 'lon'), pairs)  18.4 us
    all_to_all x1, blocking collectives, local(): near = lax.all_to_all(sums, AXES, 0, 0, axis_index_groups=cores, tiled=True)  14.7 us
    pallas_call x1, Pallas kernels, local(): call(backward_kernel, [SMEM] * 2 + [VMEM] * 7, shape(pieces, 2 * count, L...  10.3 us
    pallas_call x1, Pallas kernels, local(): call(attention_kernel, [SMEM] * 2 + [VMEM] * 12, (shape(tokens, width), s...  9.25 us
    pallas_call x1, Pallas kernels, local(): call(feed_kernel, [VMEM] * 9, (shape(*wide), shape(*wide, dtype=BF16), sh...  9.13 us
    ppermute x9, waiting for transfers between devices, move(): return lax.ppermute(array, ('lat', 'lon'), pairs)  8.68 us
    ppermute x1, starting transfers between devices, local(): far = lax.ppermute(near, 'lat', [(a, a ^ 1) for a in range(lats)])  3.04 us
  transfers between devices with their start and end apart: 10, of which 2 were waited for; matrix products, arithmetic and copies ran while one was open for 2% of the time, Pallas kernels for 9%

profile of v2, /device:TPU:1, one launch (start us, length us, event | category | flops | bytes accessed | tf_op | source)
XLA Modules:
  0.0 100.5 jit_solution(9803685615924969538)
XLA Ops:
  0.6 0.7 convert_element_type.11
  1.3 0.1 pad.7.clone
  1.4 0.1 broadcast_in_dim.21
  1.5 0.0 copy-start.13
  1.5 1.3 %maximum_maximum_fusion.1 = bf16[4,6,24,512]{3,2,1,0:T(8,128)(2,1)S(1)} fusion(bf16[4,6,24,1]{3,2,1,0:T(8,128)(2,1)S(1)} %broadcast_in_dim.21, bf16[4,6,24,500]{3,2,1,0:T(8,128)(2,1)} %param.16, bf16[512]{0:T(512)(128)(2,1)S(1)} %pad.7.clone), kind=kLoop, calls=%fused_computation.1 | loop fusion | flops 1769472 | bytes 1168000 | tf_op jit(solution)/shard_map/concatenate | solution.py:412
  2.9 7.7 %collective-permute-start.2 = (bf16[4,3,6,512]{3,2,1,0:T(8,128)(2,1)S(1)}, bf16[4,3,6,512]{3,2,1,0:T(8,128)(2,1)S(1)}, u32[]{:S(2)}, u32[]{:S(2)}) collective-permute-start(bf16[4,3,6,512]{3,2,1,0:T(8,128)(2,1)S(1)} %get-tuple-element.33), channel_id=1, source_target_pairs={{0,127},{1,96},{2,97},{3,98},{4,99},{5,100},{6,101},{7,102},{8,103... | collective-permute-start | bytes 221192 | tf_op jit(solution)/shard_map/ppermute | solution.py:372
  10.6 0.0 collective-permute-start.1
  10.6 0.2 fusion.3
  10.8 2.0 %collective-permute-start = (bf16[4,3,18,512]{3,2,1,0:T(8,128)(2,1)S(1)}, bf16[4,3,18,512]{3,2,1,0:T(8,128)(2,1)S(1)}, u32[]{:S(2)}, u32[]{:S(2)}) collective-permute-start(bf16[4,3,18,512]{3,2,1,0:T(8,128)(2,1)S(1)} %get-tuple-element.35), channel_id=1, source_target_pairs={{0,96},{1,97},{2,98},{3,99},{4,100},{5,101},{6,102},{7,103},{8,104... | collective-permute-start | bytes 663560 | tf_op jit(solution)/shard_map/ppermute | solution.py:372
  12.8 0.1 convert_element_type.12
  12.9 0.0 copy-start
  12.9 0.0 copy-start.1
  12.9 0.0 copy-start.2
  12.9 0.0 copy-start.6
  13.0 0.0 copy-start.8
  13.0 0.0 copy-start.9
  13.0 0.0 copy-start.10
  13.0 0.0 copy-start.11
  13.0 0.2 fusion.1
  13.2 1.9 %collective-permute-start.3 = (bf16[4,3,18,512]{3,2,1,0:T(8,128)(2,1)S(1)}, bf16[4,3,18,512]{3,2,1,0:T(8,128)(2,1)S(1)}, u32[]{:S(2)}, u32[]{:S(2)}) collective-permute-start(bf16[4,3,18,512]{3,2,1,0:T(8,128)(2,1)S(1)} %get-tuple-element.31), channel_id=1, source_target_pairs={{0,96},{1,97},{2,98},{3,99},{4,100},{5,101},{6,102},{7,103},{8,104... | collective-permute-start | bytes 663560 | tf_op jit(solution)/shard_map/ppermute | solution.py:372
  15.1 0.9 collective-permute-start.5
  16.0 0.0 collective-permute-done.2.corner_ref
  16.0 3.0 %collective-permute-start.4 = (bf16[4,3,6,512]{3,2,1,0:T(8,128)(2,1)S(1)}, bf16[4,3,6,512]{3,2,1,0:T(8,128)(2,1)S(1)}, u32[]{:S(2)}, u32[]{:S(2)}) collective-permute-start(bf16[4,3,6,512]{3,2,1,0:T(8,128)(2,1)S(1)} %get-tuple-element.30), channel_id=1, source_target_pairs={{0,31},{1,0},{2,1},{3,2},{4,3},{5,4},{6,5},{7,6},{8,7},{9,8},{10,9... | collective-permute-start | bytes 221192 | tf_op jit(solution)/shard_map/ppermute | solution.py:372
  19.0 0.0 collective-permute-done.1.east_ref
  19.0 0.0 collective-permute-done.south_ref
  19.1 0.0 copy-start.3
  19.1 0.0 copy-start.4
  19.2 0.0 copy-start.12
  19.2 9.2 %attention_forward.1 = (f32[576,512]{1,0:T(8,128)S(1)}, bf16[576,512]{1,0:T(8,128)(2,1)S(1)}, bf16[576,32]{1,0:T(8,128)(2,1)S(1)}, f32[576,1024]{1,0:T(8,128)S(1...) custom-call(s32[2,1,2]{2,1,0:T(1,128)S(1)} %copy-done.1, f32[16]{0:T(128)S(1)} %copy-done.2, ...), custom_call_target="tpu_custom_call" | custom-call | flops 1811939328 | bytes 20000000 | tf_op jit(solution)/shard_map/attention_forward/pallas_call | solution.py:417
  28.4 0.0 collective-permute-done.5.corner_ref
  28.4 0.0 collective-permute-done.4.east_ref
  28.4 0.0 collective-permute-done.3.south_ref
  28.5 9.1 %feed_forward.1 = (f32[4,3,18,512]{3,2,1,0:T(8,128)S(1)}, bf16[4,3,18,512]{3,2,1,0:T(8,128)(2,1)S(1)}, bf16[4,3,6,512]{3,2,1,0:T(8,128)(2,1)S(1)}, bf16[4,3,6,51...) custom-call(f32[576,512]{1,0:T(8,128)S(1)} %get-tuple-element.16.hidden_ref, ...), custom_call_target="tpu_custom_call" | custom-call | flops 4831838208 | bytes 20000000 | tf_op jit(solution)/shard_map/feed_forward/pallas_call | solution.py:445
  37.6 10.3 %attention_backward.1 = bf16[128,8,128]{2,1,0:T(8,128)(2,1)S(1)} custom-call(s32[2,1,2]{2,1,0:T(1,128)S(1)} %copy-done.1, f32[16]{0:T(128)S(1)} %copy-done.2, bf16[576,512]{1,0:T(8,128)(2,1)S(1)} %get-tuple-element.21.normed_ref, bf16[576,32]{1,0:T(8,128)(2,1)S(1)} %get-tuple-element.22.low_ref, f32[576,1024]{1,0:T(8,128)S(1)} %get-tuple-element.23.qk_ref, ...), custom_call_target="tpu_custom_call" | custom-call | flops 1207959552 | bytes 12000000 | tf_op jit(solution)/shard_map/attention_backward/pallas_call | solution.py:467
  48.0 19.7 %all_to_all.10 = bf16[128,8,128]{2,1,0:T(8,128)(2,1)S(1)} all-to-all(bf16[128,8,128]{2,1,0:T(8,128)(2,1)S(1)} %attention_backward.1), channel_id=1, replica_groups=mesh['lat'=4,'lon'=32] {'lat','lon'}, dimensions={0} | all-to-all | bytes 524288 | tf_op jit(solution)/shard_map/all_to_all | solution.py:489
  67.7 0.4 sum_by_region.1
  68.1 14.7 %all_to_all.11 = bf16[64,1,32,128]{3,2,1,0:T(8,128)(2,1)S(1)} all-to-all(bf16[64,1,32,128]{3,2,1,0:T(8,128)(2,1)S(1)} %sum_by_region.1), channel_id=1, replica_groups={{0,1,2,3,4,5,6,7,8,9,10,11,12,13,14,15,16,17,18,19,20,21,22,23,24,25,26..., dimensions={0} | all-to-all | bytes 1048576 | tf_op jit(solution)/shard_map/all_to_all | solution.py:498
  82.8 3.0 %collective-permute-start.9 = (bf16[64,1,32,128]{3,2,1,0:T(8,128)(2,1)S(1)}, bf16[64,1,32,128]{3,2,1,0:T(8,128)(2,1)S(1)}, u32[]{:S(2)}, u32[]{:S(2)}) collective-permute-start(bf16[64,1,32,128]{3,2,1,0:T(8,128)(2,1)S(1)} %all_to_all.11), channel_id=1, source_target_pairs={{0,32},{32,0},{64,96},{96,64},{1,33},{33,1},{65,97},{97,65},{2,34}... | collective-permute-start | bytes 1572872 | tf_op jit(solution)/shard_map/ppermute | solution.py:499
  85.8 1.6 %collective-permute-start.7 = (bf16[4,3,18,512]{3,2,1,0:T(8,128)(2,1)S(1)}, bf16[4,3,18,512]{3,2,1,0:T(8,128)(2,1)S(1)}, u32[]{:S(2)}, u32[]{:S(2)}) collective-permute-start(bf16[4,3,18,512]{3,2,1,0:T(8,128)(2,1)S(1)} %get-tuple-element.18), channel_id=1, source_target_pairs={{0,32},{1,33},{2,34},{3,35},{4,36},{5,37},{6,38},{7,39},{8,40},{9,... | collective-permute-start | bytes 663560 | tf_op jit(solution)/shard_map/ppermute | solution.py:372
  87.5 0.0 collective-permute-start.8
  87.5 1.2 %collective-permute-start.6 = (bf16[4,3,6,512]{3,2,1,0:T(8,128)(2,1)S(1)}, bf16[4,3,6,512]{3,2,1,0:T(8,128)(2,1)S(1)}, u32[]{:S(2)}, u32[]{:S(2)}) collective-permute-start(bf16[4,3,6,512]{3,2,1,0:T(8,128)(2,1)S(1)} %get-tuple-element.17), channel_id=1, source_target_pairs={{0,33},{1,34},{2,35},{3,36},{4,37},{5,38},{6,39},{7,40},{8,41},{9,... | collective-permute-start | bytes 221192 | tf_op jit(solution)/shard_map/ppermute | solution.py:372
  88.6 7.5 %collective-permute-done.8 = bf16[4,3,6,512]{3,2,1,0:T(8,128)(2,1)S(1)} collective-permute-done((bf16[4,3,6,512]{3,2,1,0:T(8,128)(2,1)S(1)}, bf16[4,3,6,512]{3,2,1,0:T(8,128)(2,1)S(1)}, u32[]{:S(2)}, u32[]{:S(2)}) %collective-permute-start.8) | collective-permute-done | bytes 73760 | tf_op jit(solution)/shard_map/ppermute | solution.py:372
  96.2 1.1 %collective-permute-done.6 = bf16[4,3,6,512]{3,2,1,0:T(8,128)(2,1)S(1)} collective-permute-done((bf16[4,3,6,512]{3,2,1,0:T(8,128)(2,1)S(1)}, bf16[4,3,6,512]{3,2,1,0:T(8,128)(2,1)S(1)}, u32[]{:S(2)}, u32[]{:S(2)}) %collective-permute-start.6) | collective-permute-done | bytes 73760 | tf_op jit(solution)/shard_map/ppermute | solution.py:372
  97.3 0.0 collective-permute-done.7
  97.3 0.1 maximum_convert_fusion
  97.4 1.2 %maximum_maximum_fusion = f32[4,6,24,512]{3,2,1,0:T(8,128)} fusion(f32[4,3,18,512]{3,2,1,0:T(8,128)S(1)} %get-tuple-element.20, f32[4,3,6,512]{3,2,1,0:T(8,128)S(1)} %convert_element_type.13, f32[4,3,24,512]{3,2,1,0:T(8,128)S(1)} %maximum_convert_fusion), kind=kLoop, calls=%fused_computation | loop fusion | flops 589824 | bytes 2359296 | tf_op jit(solution)/shard_map/concatenate | solution.py:486
  98.6 0.0 collective-permute-done.9
  98.6 1.9 %scale_steps.1 = (f32[32,8,512]{2,1,0:T(8,128)}, f32[32,8,1536]{2,1,0:T(8,128)}) custom-call(bf16[2,2,16,32,128]{4,3,2,1,0:T(8,128)(2,1)S(1)} %bitcast.7, bf16[2,2,16,32,128]{4,3,2,1,0:T(8,128)(2,1)S(1)} %bitcast.9), custom_call_target="tpu_custom_call" | custom-call | tf_op jit(solution)/shard_map/scale_steps/pallas_call | solution.py:502
  (20 shorter events, 0.1 us)
Async XLA Ops:
  1.5 11.3 %copy-start.13 = (f32[4,6,24,512]{3,2,1,0:T(8,128)S(1)}, f32[4,6,24,512]{3,2,1,0:T(8,128)}, u32[]{:S(2)}) copy-start(f32[4,6,24,512]{3,2,1,0:T(8,128)} %param.31) | copy-start | bytes 3538948
  2.9 13.1 %collective-permute-start.2 = (bf16[4,3,6,512]{3,2,1,0:T(8,128)(2,1)S(1)}, bf16[4,3,6,512]{3,2,1,0:T(8,128)(2,1)S(1)}, u32[]{:S(2)}, u32[]{:S(2)}) collective-permute-start(bf16[4,3,6,512]{3,2,1,0:T(8,128)(2,1)S(1)} %get-tuple-element.33), channel_id=1, source_target_pairs={{0,127},{1,96},{2,97},{3,98},{4,99},{5,100},{6,101},{7,102},{8,103... | collective-permute-start | bytes 221192 | tf_op jit(solution)/shard_map/ppermute | solution.py:372
  10.6 8.4 %collective-permute-start.1 = (bf16[4,3,6,512]{3,2,1,0:T(8,128)(2,1)S(1)}, bf16[4,3,6,512]{3,2,1,0:T(8,128)(2,1)S(1)}, u32[]{:S(2)}, u32[]{:S(2)}) collective-permute-start(bf16[4,3,6,512]{3,2,1,0:T(8,128)(2,1)S(1)} %get-tuple-element.34), channel_id=1, source_target_pairs={{0,31},{1,0},{2,1},{3,2},{4,3},{5,4},{6,5},{7,6},{8,7},{9,8},{10,9... | collective-permute-start | bytes 221192 | tf_op jit(solution)/shard_map/ppermute | solution.py:372
  10.6 8.4 %copy-start.7 = (bf16[500,512]{1,0:T(8,128)(2,1)S(1)}, bf16[500,512]{1,0:T(8,128)(2,1)}, u32[]{:S(2)}) copy-start(bf16[500,512]{1,0:T(8,128)(2,1)} %wp_ref.1) | copy-start | bytes 1536004
  10.8 8.2 %collective-permute-start = (bf16[4,3,18,512]{3,2,1,0:T(8,128)(2,1)S(1)}, bf16[4,3,18,512]{3,2,1,0:T(8,128)(2,1)S(1)}, u32[]{:S(2)}, u32[]{:S(2)}) collective-permute-start(bf16[4,3,18,512]{3,2,1,0:T(8,128)(2,1)S(1)} %get-tuple-element.35), channel_id=1, source_target_pairs={{0,96},{1,97},{2,98},{3,99},{4,100},{5,101},{6,102},{7,103},{8,104... | collective-permute-start | bytes 663560 | tf_op jit(solution)/shard_map/ppermute | solution.py:372
  12.8 6.2 %copy-start.5 = (bf16[512,1536]{1,0:T(8,128)(2,1)S(1)}, bf16[512,1536]{1,0:T(8,128)(2,1)}, u32[]{:S(2)}) copy-start(bf16[512,1536]{1,0:T(8,128)(2,1)} %wqkv_ref.1) | copy-start | bytes 4718596
  12.9 6.1 %copy-start = (bf16[32,8,1536]{2,1,0:T(8,128)(2,1)S(1)}, bf16[32,8,1536]{2,1,0:T(8,128)(2,1)}, u32[]{:S(2)}) copy-start(bf16[32,8,1536]{2,1,0:T(8,128)(2,1)} %up_ref.3) | copy-start | bytes 2359300
  12.9 6.1 %copy-start.1 = (s32[2,1,2]{2,1,0:T(1,128)S(1)}, s32[2,1,2]{2,1,0:T(1,128)}, u32[]{:S(2)}) copy-start(s32[2,1,2]{2,1,0:T(1,128)} %region_ref.3) | copy-start | bytes 52
  12.9 6.1 %copy-start.2 = (f32[16]{0:T(128)S(1)}, f32[16]{0:T(128)}, u32[]{:S(2)}) copy-start(f32[16]{0:T(128)} %temper_ref.3) | copy-start | bytes 196
  12.9 6.1 %copy-start.6 = (bf16[512,512]{1,0:T(8,128)(2,1)S(1)}, bf16[512,512]{1,0:T(8,128)(2,1)}, u32[]{:S(2)}) copy-start(bf16[512,512]{1,0:T(8,128)(2,1)} %wo_ref.3) | copy-start | bytes 1572868
  13.0 6.1 %copy-start.8 = (bf16[32,8,512]{2,1,0:T(8,128)(2,1)S(1)}, bf16[32,8,512]{2,1,0:T(8,128)(2,1)}, u32[]{:S(2)}) copy-start(bf16[32,8,512]{2,1,0:T(8,128)(2,1)} %down_ref.1) | copy-start | bytes 786436
  13.0 6.1 %copy-start.9 = (f32[512]{0:T(512)S(1)}, f32[512]{0:T(512)}, u32[]{:S(2)}) copy-start(f32[512]{0:T(512)} %param.20) | copy-start | bytes 6148
  13.0 6.1 %copy-start.10 = (f32[512]{0:T(512)S(1)}, f32[512]{0:T(512)}, u32[]{:S(2)}) copy-start(f32[512]{0:T(512)} %param.21) | copy-start | bytes 6148
  13.0 6.1 %copy-start.11 = (f32[512]{0:T(512)S(1)}, f32[512]{0:T(512)}, u32[]{:S(2)}) copy-start(f32[512]{0:T(512)} %param.22) | copy-start | bytes 6148
  13.2 15.3 %collective-permute-start.3 = (bf16[4,3,18,512]{3,2,1,0:T(8,128)(2,1)S(1)}, bf16[4,3,18,512]{3,2,1,0:T(8,128)(2,1)S(1)}, u32[]{:S(2)}, u32[]{:S(2)}) collective-permute-start(bf16[4,3,18,512]{3,2,1,0:T(8,128)(2,1)S(1)} %get-tuple-element.31), channel_id=1, source_target_pairs={{0,96},{1,97},{2,98},{3,99},{4,100},{5,101},{6,102},{7,103},{8,104... | collective-permute-start | bytes 663560 | tf_op jit(solution)/shard_map/ppermute | solution.py:372
  15.1 13.3 %collective-permute-start.5 = (bf16[4,3,6,512]{3,2,1,0:T(8,128)(2,1)S(1)}, bf16[4,3,6,512]{3,2,1,0:T(8,128)(2,1)S(1)}, u32[]{:S(2)}, u32[]{:S(2)}) collective-permute-start(bf16[4,3,6,512]{3,2,1,0:T(8,128)(2,1)S(1)} %get-tuple-element.29), channel_id=1, source_target_pairs={{0,127},{1,96},{2,97},{3,98},{4,99},{5,100},{6,101},{7,102},{8,103... | collective-permute-start | bytes 221192 | tf_op jit(solution)/shard_map/ppermute | solution.py:372
  16.0 12.4 %collective-permute-start.4 = (bf16[4,3,6,512]{3,2,1,0:T(8,128)(2,1)S(1)}, bf16[4,3,6,512]{3,2,1,0:T(8,128)(2,1)S(1)}, u32[]{:S(2)}, u32[]{:S(2)}) collective-permute-start(bf16[4,3,6,512]{3,2,1,0:T(8,128)(2,1)S(1)} %get-tuple-element.30), channel_id=1, source_target_pairs={{0,31},{1,0},{2,1},{3,2},{4,3},{5,4},{6,5},{7,6},{8,7},{9,8},{10,9... | collective-permute-start | bytes 221192 | tf_op jit(solution)/shard_map/ppermute | solution.py:372
  19.1 9.3 %copy-start.3 = (bf16[512,2048]{1,0:T(8,128)(2,1)S(1)}, bf16[512,2048]{1,0:T(8,128)(2,1)}, u32[]{:S(2)}) copy-start(bf16[512,2048]{1,0:T(8,128)(2,1)} %wup_ref.1) | copy-start | bytes 6291460
  19.1 9.3 %copy-start.4 = (bf16[2048,512]{1,0:T(8,128)(2,1)S(1)}, bf16[2048,512]{1,0:T(8,128)(2,1)}, u32[]{:S(2)}) copy-start(bf16[2048,512]{1,0:T(8,128)(2,1)} %wdn_ref.1) | copy-start | bytes 6291460
  19.2 9.3 %copy-start.12 = (f32[512]{0:T(512)S(1)}, f32[512]{0:T(512)}, u32[]{:S(2)}) copy-start(f32[512]{0:T(512)} %param.28) | copy-start | bytes 6148
  82.8 15.8 %collective-permute-start.9 = (bf16[64,1,32,128]{3,2,1,0:T(8,128)(2,1)S(1)}, bf16[64,1,32,128]{3,2,1,0:T(8,128)(2,1)S(1)}, u32[]{:S(2)}, u32[]{:S(2)}) collective-permute-start(bf16[64,1,32,128]{3,2,1,0:T(8,128)(2,1)S(1)} %all_to_all.11), channel_id=1, source_target_pairs={{0,32},{32,0},{64,96},{96,64},{1,33},{33,1},{65,97},{97,65},{2,34}... | collective-permute-start | bytes 1572872 | tf_op jit(solution)/shard_map/ppermute | solution.py:499
  85.8 11.5 %collective-permute-start.7 = (bf16[4,3,18,512]{3,2,1,0:T(8,128)(2,1)S(1)}, bf16[4,3,18,512]{3,2,1,0:T(8,128)(2,1)S(1)}, u32[]{:S(2)}, u32[]{:S(2)}) collective-permute-start(bf16[4,3,18,512]{3,2,1,0:T(8,128)(2,1)S(1)} %get-tuple-element.18), channel_id=1, source_target_pairs={{0,32},{1,33},{2,34},{3,35},{4,36},{5,37},{6,38},{7,39},{8,40},{9,... | collective-permute-start | bytes 663560 | tf_op jit(solution)/shard_map/ppermute | solution.py:372
  87.5 8.7 %collective-permute-start.8 = (bf16[4,3,6,512]{3,2,1,0:T(8,128)(2,1)S(1)}, bf16[4,3,6,512]{3,2,1,0:T(8,128)(2,1)S(1)}, u32[]{:S(2)}, u32[]{:S(2)}) collective-permute-start(bf16[4,3,6,512]{3,2,1,0:T(8,128)(2,1)S(1)} %get-tuple-element.19), channel_id=1, source_target_pairs={{0,1},{1,2},{2,3},{3,4},{4,5},{5,6},{6,7},{7,8},{8,9},{9,10},{10,1... | collective-permute-start | bytes 221192 | tf_op jit(solution)/shard_map/ppermute | solution.py:372
  87.5 9.8 %collective-permute-start.6 = (bf16[4,3,6,512]{3,2,1,0:T(8,128)(2,1)S(1)}, bf16[4,3,6,512]{3,2,1,0:T(8,128)(2,1)S(1)}, u32[]{:S(2)}, u32[]{:S(2)}) collective-permute-start(bf16[4,3,6,512]{3,2,1,0:T(8,128)(2,1)S(1)} %get-tuple-element.17), channel_id=1, source_target_pairs={{0,33},{1,34},{2,35},{3,36},{4,37},{5,38},{6,39},{7,40},{8,41},{9,... | collective-permute-start | bytes 221192 | tf_op jit(solution)/shard_map/ppermute | solution.py:372

commit v3 on v2

--- a/solution.py
+++ b/solution.py
@@ -143,6 +143,23 @@
     tail = 0.5 * poly * t * e
     phi = jnp.where(u < 0, tail, 1.0 - tail)
     return u * phi, phi + u * (0.3989422804014327 * e)
+
+
+def pack_kernel(pixels_ref, land_ref, own_ref, south_ref, east_ref, corner_ref):
+    levels, rows, cols, patch_len = pixels_ref.shape
+    width = own_ref.shape[3]
+    eye = lax.broadcasted_iota(jnp.int32, (cols, cols), 0)
+    eye = jnp.where(eye == lax.broadcasted_iota(jnp.int32, (cols, cols), 1), 1.0, 0.0)
+    land = mm_nt(eye.astype(BF16), land_ref[...].astype(F32).astype(BF16))
+    lane = lax.broadcasted_iota(jnp.int32, (cols, width), 1)
+    blank = jnp.zeros((cols, width - patch_len), F32)
+    for level in range(levels):
+        for row in range(rows):
+            patch = jnp.concatenate((pixels_ref[level, row].astype(F32), blank), axis=1)
+            patch = jnp.where(lane == patch_len, land[:, row : row + 1], patch).astype(BF16)
+            half, at = divmod(row, HALF_LAT)
+            (own_ref if half else south_ref)[level, at] = patch[HALF_LON:]
+            (east_ref if half else corner_ref)[level, at] = patch[:HALF_LON]
 
 
 def attention_kernel(
@@ -372,11 +389,18 @@
     return lax.ppermute(array, ("lat", "lon"), pairs)
 
 
-def halves(field):
-    south = move(field[:, :HALF_LAT, HALF_LON:], (-1, 0))
-    east = move(field[:, HALF_LAT:, :HALF_LON], (0, -1))
-    corner = move(field[:, :HALF_LAT, :HALF_LON], (-1, -1))
-    return field[:, HALF_LAT:, HALF_LON:], south, east, corner
+def halos(field):
+    return (
+        field[:, :HALF_LAT, HALF_LON:],
+        field[:, HALF_LAT:, :HALF_LON],
+        field[:, :HALF_LAT, :HALF_LON],
+    )
+
+
+def move_halos(parts):
+    south, east, corner = parts
+    corner, east = move(corner, (-1, -1)), move(east, (0, -1))
+    return move(south, (-1, 0)), east, corner
 
 
 def local(
@@ -405,15 +429,21 @@
     tokens = count * TOKENS
     groups = width // LANES
     devices = lax.axis_size("lat") * lax.axis_size("lon")
-    spare = width - patch_len - 1
-
-    land = jnp.broadcast_to(land_patch_mask.astype(BF16)[None, :, :, None], (levels, rows, cols, 1))
-    blank = jnp.zeros((levels, rows, cols, spare), BF16)
-    pix = halves(jnp.concatenate((pixels, land, blank), axis=3))
-    cot = halves(cotangent.astype(BF16))
 
     wide = (levels, HALF_LAT, cols - HALF_LON, width)
     narrow = (levels, HALF_LAT, HALF_LON, width)
+    pix_own, *pix = call(
+        pack_kernel,
+        [VMEM] * 2,
+        tuple(shape(*dims, dtype=BF16) for dims in (wide, wide, narrow, narrow)),
+        moved=2_000_000,
+        name="pack_pixels",
+    )(pixels, land_patch_mask)
+    pix, cotangent = lax.optimization_barrier((pix, cotangent))
+    pix = move_halos(pix)
+    cot_own = cotangent[:, HALF_LAT:, HALF_LON:].astype(BF16)
+    cot = move_halos(tuple(part.astype(BF16) for part in halos(cotangent)))
+
     hidden, normed, low, qk, v, probs = call(
         attention_kernel,
         [SMEM] * 2 + [VMEM] * 12,
@@ -438,7 +468,7 @@
         moved=20_000_000,
         name="attention_forward",
     )(
-        region, head_logit_scale, *pix, patch_embed_weight, patch_embed_bias[None],
+        region, head_logit_scale, pix_own, *pix, patch_embed_weight, patch_embed_bias[None],
         land_embedding_vector[None], attention_norm_gain[None], query_key_value_weight,
         region_down_factor, region_up_factor, attention_output_weight,
     )
@@ -457,12 +487,10 @@
         moved=20_000_000,
         name="feed_forward",
     )(
-        hidden, *cot, feedforward_gain[None], feedforward_up_weight, feedforward_down_weight,
+        hidden, cot_own, *cot, feedforward_gain[None], feedforward_up_weight, feedforward_down_weight,
         attention_output_weight,
     )
-    north = move(north, (1, 0)).astype(F32)
-    west = move(west, (0, 1)).astype(F32)
-    diagonal = move(diagonal, (1, 1)).astype(F32)
+    diagonal, west, north = move(diagonal, (1, 1)), move(west, (0, 1)), move(north, (1, 0))
     pieces = rank * 4 * width // LANES
     terms = call(
         backward_kernel,
@@ -481,8 +509,9 @@
         moved=12_000_000,
         name="attention_backward",
     )(region, head_logit_scale, normed, low, qk, v, probs, d_att, region_up_factor)
-    upper = jnp.concatenate((diagonal, north), axis=2)
-    lower = jnp.concatenate((west, home), axis=2)
+    terms, north, west, diagonal = lax.optimization_barrier((terms, north, west, diagonal))
+    upper = jnp.concatenate((diagonal, north), axis=2).astype(F32)
+    lower = jnp.concatenate((west.astype(F32), home), axis=2)
     mixed_state = jnp.concatenate((upper, lower), axis=1)
 
     each = pieces // devices

time: 101 us -> 93.3 us (0.924)
  waiting for transfers between devices: 8.68 us -> 0.69 us
  local copies, waits for them, and re-layouts: 0.6 us -> 2 us
  blocking collectives: 34.4 us -> 33.3 us
    ppermute x9, waiting for transfers between devices: 8.68 us -> 0.46 us  [move(): return lax.ppermute(array, ('lat', 'lon'), pairs)]
    unnamed x28 -> x30, local copies, waits for them, and re-layouts: 0.08 us -> 1.82 us
    another operation x0 -> x1, other arithmetic: none -> 1.46 us
    concatenate x2 -> x0, other arithmetic: 1.44 us -> none  [the longest x1 1.35 us: local(): pix = halves(jnp.concatenate((pixels, land, blank), axis=3))]
    all_to_all x1, blocking collectives: 19.7 us -> 18.6 us  [local(): terms = lax.all_to_all(terms, AXES, 0, 0, tiled=True)]
  transfers between devices with their start and end apart: 10 -> 10, of which waited for: 2 -> 2; matrix products, arithmetic and copies ran while one was open for 2% -> 3% of each run, Pallas kernels for 9% -> 21%
where the time goes in v3:
time: 93.3 us; the launch traced here: 93.1 us
  blocking collectives  33.3 us (36%)
  Pallas kernels  31.2 us (33%)
  starting transfers between devices  22.2 us (24%)
  other arithmetic  2.76 us (3%)
  local copies, waits for them, and re-layouts  2 us (2%)
    ppermute x9, starting transfers between devices, move(): return lax.ppermute(array, ('lat', 'lon'), pairs)  19.1 us
    all_to_all x1, blocking collectives, local(): terms = lax.all_to_all(terms, AXES, 0, 0, tiled=True)  18.6 us
    all_to_all x1, blocking collectives, local(): near = lax.all_to_all(sums, AXES, 0, 0, axis_index_groups=cores, tiled=True)  14.7 us
    pallas_call x1, Pallas kernels, local(): call(backward_kernel, [SMEM] * 2 + [VMEM] * 7, shape(pieces, 2 * count, L...  10.3 us
    pallas_call x1, Pallas kernels, local(): call(attention_kernel, [SMEM] * 2 + [VMEM] * 12, (shape(tokens, width), s...  9.25 us
    pallas_call x1, Pallas kernels, local(): call(feed_kernel, [VMEM] * 9, (shape(*wide), shape(*wide, dtype=BF16), sh...  9.13 us
    ppermute x1, starting transfers between devices, local(): far = lax.ppermute(near, 'lat', [(a, a ^ 1) for a in range(lats)])  3.04 us
    pallas_call x1, Pallas kernels, local(): call(scale_kernel, [VMEM] * 2, (shape(regions, rank, width), shape(region...  1.91 us
  transfers between devices with their start and end apart: 10, of which 2 were waited for; matrix products, arithmetic and copies ran while one was open for 3% of the time, Pallas kernels for 21%

profile of v3, /device:TPU:1, one launch (start us, length us, event | category | flops | bytes accessed | tf_op | source)
XLA Modules:
  0.0 93.1 jit_solution(7729580802727357756)
XLA Ops:
  0.6 1.1 %copy-done.1 = bf16[4,6,24,500]{3,2,1,0:T(8,128)(2,1)S(1)} copy-done((bf16[4,6,24,500]{3,2,1,0:T(8,128)(2,1)S(1)}, bf16[4,6,24,500]{3,2,1,0:T(8,128)(2,1)}, u32[]{:S(2)}) %copy-start.1) | copy-done | bytes 576024
  1.7 0.7 copy-done.2
  2.4 0.3 pack_pixels.1
  2.6 7.2 %collective-permute-start.1 = (bf16[4,3,6,512]{3,2,1,0:T(8,128)(2,1)S(1)}, bf16[4,3,6,512]{3,2,1,0:T(8,128)(2,1)S(1)}, u32[]{:S(2)}, u32[]{:S(2)}) collective-permute-start(bf16[4,3,6,512]{3,2,1,0:T(8,128)(2,1)S(1)} %get-tuple-element.33), channel_id=1, source_target_pairs={{0,31},{1,0},{2,1},{3,2},{4,3},{5,4},{6,5},{7,6},{8,7},{9,8},{10,9... | collective-permute-start | bytes 221192 | tf_op jit(solution)/shard_map/ppermute | solution.py:389
  9.8 0.7 collective-permute-start.2
  10.5 2.0 %collective-permute-start = (bf16[4,3,18,512]{3,2,1,0:T(8,128)(2,1)S(1)}, bf16[4,3,18,512]{3,2,1,0:T(8,128)(2,1)S(1)}, u32[]{:S(2)}, u32[]{:S(2)}) collective-permute-start(bf16[4,3,18,512]{3,2,1,0:T(8,128)(2,1)S(1)} %get-tuple-element.32), channel_id=1, source_target_pairs={{0,96},{1,97},{2,98},{3,99},{4,100},{5,101},{6,102},{7,103},{8,104... | collective-permute-start | bytes 663560 | tf_op jit(solution)/shard_map/ppermute | solution.py:389
  12.5 1.5 %convert.6 = bf16[4,6,24,512]{3,2,1,0:T(8,128)(2,1)S(1)} convert(f32[4,6,24,512]{3,2,1,0:T(8,128)} %param.31) | non-fusion elementwise | flops 294912 | bytes 1769472 | tf_op jit(solution)/shard_map/convert.3
  13.9 0.0 copy-start
  13.9 0.0 copy-start.3
  14.0 0.0 copy-start.4
  14.0 0.0 copy-start.8
  14.0 0.0 copy-start.10
  14.0 0.0 copy-start.11
  14.0 0.0 copy-start.12
  14.0 0.0 copy-start.13
  14.0 0.2 fusion.1
  14.2 2.1 %collective-permute-start.3 = (bf16[4,3,18,512]{3,2,1,0:T(8,128)(2,1)S(1)}, bf16[4,3,18,512]{3,2,1,0:T(8,128)(2,1)S(1)}, u32[]{:S(2)}, u32[]{:S(2)}) collective-permute-start(bf16[4,3,18,512]{3,2,1,0:T(8,128)(2,1)S(1)} %get-tuple-element.55), channel_id=1, source_target_pairs={{0,96},{1,97},{2,98},{3,99},{4,100},{5,101},{6,102},{7,103},{8,104... | collective-permute-start | bytes 663560 | tf_op jit(solution)/shard_map/ppermute | solution.py:389
  16.3 0.9 collective-permute-start.5
  17.2 0.0 collective-permute-done.1.east_ref
  17.2 0.7 collective-permute-start.4
  17.9 0.0 collective-permute-done.2.corner_ref
  17.9 0.4 collective-permute-done.south_ref
  18.4 0.0 copy-done.9
  18.4 0.0 copy-done
  18.5 0.0 copy-start.5
  18.5 0.0 copy-start.6
  18.5 0.0 copy-start.14
  18.5 9.2 %attention_forward.1 = (f32[576,512]{1,0:T(8,128)S(1)}, bf16[576,512]{1,0:T(8,128)(2,1)S(1)}, bf16[576,32]{1,0:T(8,128)(2,1)S(1)}, f32[576,1024]{1,0:T(8,128)S(1...) custom-call(s32[2,1,2]{2,1,0:T(1,128)S(1)} %copy-done.3, f32[16]{0:T(128)S(1)} %copy-done.4, ...), custom_call_target="tpu_custom_call" | custom-call | flops 1811939328 | bytes 20000000 | tf_op jit(solution)/shard_map/attention_forward/pallas_call | solution.py:447
  27.7 0.0 collective-permute-done.5.corner_ref
  27.8 0.0 collective-permute-done.4.east_ref
  27.8 0.0 collective-permute-done.3.south_ref
  27.8 0.0 copy-done.5
  27.8 9.1 %feed_forward.1 = (f32[4,3,18,512]{3,2,1,0:T(8,128)S(1)}, bf16[4,3,18,512]{3,2,1,0:T(8,128)(2,1)S(1)}, bf16[4,3,6,512]{3,2,1,0:T(8,128)(2,1)S(1)}, bf16[4,3,6,51...) custom-call(f32[576,512]{1,0:T(8,128)S(1)} %get-tuple-element.40.hidden_ref, ...), custom_call_target="tpu_custom_call" | custom-call | flops 4831838208 | bytes 20000000 | tf_op jit(solution)/shard_map/feed_forward/pallas_call | solution.py:475
  36.9 5.6 %collective-permute-start.6 = (bf16[4,3,18,512]{3,2,1,0:T(8,128)(2,1)S(1)}, bf16[4,3,18,512]{3,2,1,0:T(8,128)(2,1)S(1)}, u32[]{:S(2)}, u32[]{:S(2)}) collective-permute-start(bf16[4,3,18,512]{3,2,1,0:T(8,128)(2,1)S(1)} %get-tuple-element.43), channel_id=1, source_target_pairs={{0,32},{1,33},{2,34},{3,35},{4,36},{5,37},{6,38},{7,39},{8,40},{9,... | collective-permute-start | bytes 663560 | tf_op jit(solution)/shard_map/ppermute | solution.py:389
  42.5 0.0 collective-permute-start.7
  42.5 0.0 collective-permute-start.8
  42.5 10.3 %attention_backward.1 = bf16[128,8,128]{2,1,0:T(8,128)(2,1)S(1)} custom-call(s32[2,1,2]{2,1,0:T(1,128)S(1)} %copy-done.3, f32[16]{0:T(128)S(1)} %copy-done.4, bf16[576,512]{1,0:T(8,128)(2,1)S(1)} %get-tuple-element.35.normed_ref, bf16[576,32]{1,0:T(8,128)(2,1)S(1)} %get-tuple-element.36.low_ref, f32[576,1024]{1,0:T(8,128)S(1)} %get-tuple-element.37.qk_ref, ...), custom_call_target="tpu_custom_call" | custom-call | flops 1207959552 | bytes 12000000 | tf_op jit(solution)/shard_map/attention_backward/pallas_call | solution.py:495
  52.9 0.0 collective-permute-done.7
  52.9 0.0 collective-permute-done.8
  52.9 0.0 collective-permute-done.6
  52.9 18.6 %all_to_all.10 = bf16[128,8,128]{2,1,0:T(8,128)(2,1)S(1)} all-to-all(bf16[128,8,128]{2,1,0:T(8,128)(2,1)S(1)} %attention_backward.1), channel_id=1, replica_groups=mesh['lat'=4,'lon'=32] {'lat','lon'}, dimensions={0} | all-to-all | bytes 524288 | tf_op jit(solution)/shard_map/all_to_all | solution.py:518
  71.5 0.4 sum_by_region.1
  71.9 14.7 %all_to_all.11 = bf16[64,1,32,128]{3,2,1,0:T(8,128)(2,1)S(1)} all-to-all(bf16[64,1,32,128]{3,2,1,0:T(8,128)(2,1)S(1)} %sum_by_region.1), channel_id=1, replica_groups={{0,1,2,3,4,5,6,7,8,9,10,11,12,13,14,15,16,17,18,19,20,21,22,23,24,25,26..., dimensions={0} | all-to-all | bytes 1048576 | tf_op jit(solution)/shard_map/all_to_all | solution.py:527
  86.6 3.0 %collective-permute-start.9 = (bf16[64,1,32,128]{3,2,1,0:T(8,128)(2,1)S(1)}, bf16[64,1,32,128]{3,2,1,0:T(8,128)(2,1)S(1)}, u32[]{:S(2)}, u32[]{:S(2)}) collective-permute-start(bf16[64,1,32,128]{3,2,1,0:T(8,128)(2,1)S(1)} %all_to_all.11), channel_id=1, source_target_pairs={{0,32},{32,0},{64,96},{96,64},{1,33},{33,1},{65,97},{97,65},{2,34}... | collective-permute-start | bytes 1572872 | tf_op jit(solution)/shard_map/ppermute | solution.py:528
  89.6 0.1 maximum_convert_fusion
  89.7 1.2 %maximum_maximum_fusion = f32[4,6,24,512]{3,2,1,0:T(8,128)} fusion(f32[4,3,18,512]{3,2,1,0:T(8,128)S(1)} %get-tuple-element.49, f32[4,3,6,512]{3,2,1,0:T(8,128)S(1)} %convert_element_type.5, f32[4,3,24,512]{3,2,1,0:T(8,128)S(1)} %maximum_convert_fusion), kind=kLoop, calls=%fused_computation | loop fusion | flops 589824 | bytes 2359296 | tf_op jit(solution)/shard_map/concatenate | solution.py:515
  90.9 0.2 collective-permute-done.9
  91.2 1.9 %scale_steps.1 = (f32[32,8,512]{2,1,0:T(8,128)}, f32[32,8,1536]{2,1,0:T(8,128)}) custom-call(bf16[2,2,16,32,128]{4,3,2,1,0:T(8,128)(2,1)S(1)} %bitcast.7, bf16[2,2,16,32,128]{4,3,2,1,0:T(8,128)(2,1)S(1)} %bitcast.9), custom_call_target="tpu_custom_call" | custom-call | tf_op jit(solution)/shard_map/scale_steps/pallas_call | solution.py:531
  (16 shorter events, 0.1 us)
Async XLA Ops:
  0.6 1.1 %copy-start.1 = (bf16[4,6,24,500]{3,2,1,0:T(8,128)(2,1)S(1)}, bf16[4,6,24,500]{3,2,1,0:T(8,128)(2,1)}, u32[]{:S(2)}) copy-start(bf16[4,6,24,500]{3,2,1,0:T(8,128)(2,1)} %pixels_ref.1) | copy-start | bytes 1728004
  1.7 0.7 copy-start.2
  2.4 16.0 %copy-start.9 = (bf16[500,512]{1,0:T(8,128)(2,1)S(1)}, bf16[500,512]{1,0:T(8,128)(2,1)}, u32[]{:S(2)}) copy-start(bf16[500,512]{1,0:T(8,128)(2,1)} %wp_ref.1) | copy-start | bytes 1536004
  2.6 14.6 %collective-permute-start.1 = (bf16[4,3,6,512]{3,2,1,0:T(8,128)(2,1)S(1)}, bf16[4,3,6,512]{3,2,1,0:T(8,128)(2,1)S(1)}, u32[]{:S(2)}, u32[]{:S(2)}) collective-permute-start(bf16[4,3,6,512]{3,2,1,0:T(8,128)(2,1)S(1)} %get-tuple-element.33), channel_id=1, source_target_pairs={{0,31},{1,0},{2,1},{3,2},{4,3},{5,4},{6,5},{7,6},{8,7},{9,8},{10,9... | collective-permute-start | bytes 221192 | tf_op jit(solution)/shard_map/ppermute | solution.py:389
  9.8 8.1 %collective-permute-start.2 = (bf16[4,3,6,512]{3,2,1,0:T(8,128)(2,1)S(1)}, bf16[4,3,6,512]{3,2,1,0:T(8,128)(2,1)S(1)}, u32[]{:S(2)}, u32[]{:S(2)}) collective-permute-start(bf16[4,3,6,512]{3,2,1,0:T(8,128)(2,1)S(1)} %get-tuple-element.34), channel_id=1, source_target_pairs={{0,127},{1,96},{2,97},{3,98},{4,99},{5,100},{6,101},{7,102},{8,103... | collective-permute-start | bytes 221192 | tf_op jit(solution)/shard_map/ppermute | solution.py:389
  10.5 7.9 %collective-permute-start = (bf16[4,3,18,512]{3,2,1,0:T(8,128)(2,1)S(1)}, bf16[4,3,18,512]{3,2,1,0:T(8,128)(2,1)S(1)}, u32[]{:S(2)}, u32[]{:S(2)}) collective-permute-start(bf16[4,3,18,512]{3,2,1,0:T(8,128)(2,1)S(1)} %get-tuple-element.32), channel_id=1, source_target_pairs={{0,96},{1,97},{2,98},{3,99},{4,100},{5,101},{6,102},{7,103},{8,104... | collective-permute-start | bytes 663560 | tf_op jit(solution)/shard_map/ppermute | solution.py:389
  12.5 5.9 %copy-start.7 = (bf16[512,1536]{1,0:T(8,128)(2,1)S(1)}, bf16[512,1536]{1,0:T(8,128)(2,1)}, u32[]{:S(2)}) copy-start(bf16[512,1536]{1,0:T(8,128)(2,1)} %wqkv_ref.1) | copy-start | bytes 4718596
  13.9 4.4 %copy-start = (bf16[32,8,1536]{2,1,0:T(8,128)(2,1)S(1)}, bf16[32,8,1536]{2,1,0:T(8,128)(2,1)}, u32[]{:S(2)}) copy-start(bf16[32,8,1536]{2,1,0:T(8,128)(2,1)} %up_ref.3) | copy-start | bytes 2359300
  13.9 4.4 %copy-start.3 = (s32[2,1,2]{2,1,0:T(1,128)S(1)}, s32[2,1,2]{2,1,0:T(1,128)}, u32[]{:S(2)}) copy-start(s32[2,1,2]{2,1,0:T(1,128)} %region_ref.3) | copy-start | bytes 52
  14.0 4.4 %copy-start.4 = (f32[16]{0:T(128)S(1)}, f32[16]{0:T(128)}, u32[]{:S(2)}) copy-start(f32[16]{0:T(128)} %temper_ref.3) | copy-start | bytes 196
  14.0 4.4 %copy-start.8 = (bf16[512,512]{1,0:T(8,128)(2,1)S(1)}, bf16[512,512]{1,0:T(8,128)(2,1)}, u32[]{:S(2)}) copy-start(bf16[512,512]{1,0:T(8,128)(2,1)} %wo_ref.3) | copy-start | bytes 1572868
  14.0 4.4 %copy-start.10 = (bf16[32,8,512]{2,1,0:T(8,128)(2,1)S(1)}, bf16[32,8,512]{2,1,0:T(8,128)(2,1)}, u32[]{:S(2)}) copy-start(bf16[32,8,512]{2,1,0:T(8,128)(2,1)} %down_ref.1) | copy-start | bytes 786436
  14.0 4.4 %copy-start.11 = (f32[512]{0:T(512)S(1)}, f32[512]{0:T(512)}, u32[]{:S(2)}) copy-start(f32[512]{0:T(512)} %param.20) | copy-start | bytes 6148
  14.0 4.4 %copy-start.12 = (f32[512]{0:T(512)S(1)}, f32[512]{0:T(512)}, u32[]{:S(2)}) copy-start(f32[512]{0:T(512)} %param.21) | copy-start | bytes 6148
  14.0 4.4 %copy-start.13 = (f32[512]{0:T(512)S(1)}, f32[512]{0:T(512)}, u32[]{:S(2)}) copy-start(f32[512]{0:T(512)} %param.22) | copy-start | bytes 6148
  14.2 13.6 %collective-permute-start.3 = (bf16[4,3,18,512]{3,2,1,0:T(8,128)(2,1)S(1)}, bf16[4,3,18,512]{3,2,1,0:T(8,128)(2,1)S(1)}, u32[]{:S(2)}, u32[]{:S(2)}) collective-permute-start(bf16[4,3,18,512]{3,2,1,0:T(8,128)(2,1)S(1)} %get-tuple-element.55), channel_id=1, source_target_pairs={{0,96},{1,97},{2,98},{3,99},{4,100},{5,101},{6,102},{7,103},{8,104... | collective-permute-start | bytes 663560 | tf_op jit(solution)/shard_map/ppermute | solution.py:389
  16.3 11.4 %collective-permute-start.5 = (bf16[4,3,6,512]{3,2,1,0:T(8,128)(2,1)S(1)}, bf16[4,3,6,512]{3,2,1,0:T(8,128)(2,1)S(1)}, u32[]{:S(2)}, u32[]{:S(2)}) collective-permute-start(bf16[4,3,6,512]{3,2,1,0:T(8,128)(2,1)S(1)} %get-tuple-element.53), channel_id=1, source_target_pairs={{0,127},{1,96},{2,97},{3,98},{4,99},{5,100},{6,101},{7,102},{8,103... | collective-permute-start | bytes 221192 | tf_op jit(solution)/shard_map/ppermute | solution.py:389
  17.2 10.6 %collective-permute-start.4 = (bf16[4,3,6,512]{3,2,1,0:T(8,128)(2,1)S(1)}, bf16[4,3,6,512]{3,2,1,0:T(8,128)(2,1)S(1)}, u32[]{:S(2)}, u32[]{:S(2)}) collective-permute-start(bf16[4,3,6,512]{3,2,1,0:T(8,128)(2,1)S(1)} %get-tuple-element.54), channel_id=1, source_target_pairs={{0,31},{1,0},{2,1},{3,2},{4,3},{5,4},{6,5},{7,6},{8,7},{9,8},{10,9... | collective-permute-start | bytes 221192 | tf_op jit(solution)/shard_map/ppermute | solution.py:389
  18.5 9.3 %copy-start.5 = (bf16[512,2048]{1,0:T(8,128)(2,1)S(1)}, bf16[512,2048]{1,0:T(8,128)(2,1)}, u32[]{:S(2)}) copy-start(bf16[512,2048]{1,0:T(8,128)(2,1)} %wup_ref.1) | copy-start | bytes 6291460
  18.5 9.3 %copy-start.6 = (bf16[2048,512]{1,0:T(8,128)(2,1)S(1)}, bf16[2048,512]{1,0:T(8,128)(2,1)}, u32[]{:S(2)}) copy-start(bf16[2048,512]{1,0:T(8,128)(2,1)} %wdn_ref.1) | copy-start | bytes 6291460
  18.5 9.3 %copy-start.14 = (f32[512]{0:T(512)S(1)}, f32[512]{0:T(512)}, u32[]{:S(2)}) copy-start(f32[512]{0:T(512)} %param.28) | copy-start | bytes 6148
  36.9 16.0 %collective-permute-start.6 = (bf16[4,3,18,512]{3,2,1,0:T(8,128)(2,1)S(1)}, bf16[4,3,18,512]{3,2,1,0:T(8,128)(2,1)S(1)}, u32[]{:S(2)}, u32[]{:S(2)}) collective-permute-start(bf16[4,3,18,512]{3,2,1,0:T(8,128)(2,1)S(1)} %get-tuple-element.43), channel_id=1, source_target_pairs={{0,32},{1,33},{2,34},{3,35},{4,36},{5,37},{6,38},{7,39},{8,40},{9,... | collective-permute-start | bytes 663560 | tf_op jit(solution)/shard_map/ppermute | solution.py:389
  42.5 10.4 %collective-permute-start.7 = (bf16[4,3,6,512]{3,2,1,0:T(8,128)(2,1)S(1)}, bf16[4,3,6,512]{3,2,1,0:T(8,128)(2,1)S(1)}, u32[]{:S(2)}, u32[]{:S(2)}) collective-permute-start(bf16[4,3,6,512]{3,2,1,0:T(8,128)(2,1)S(1)} %get-tuple-element.44), channel_id=1, source_target_pairs={{0,1},{1,2},{2,3},{3,4},{4,5},{5,6},{6,7},{7,8},{8,9},{9,10},{10,1... | collective-permute-start | bytes 221192 | tf_op jit(solution)/shard_map/ppermute | solution.py:389
  42.5 10.4 %collective-permute-start.8 = (bf16[4,3,6,512]{3,2,1,0:T(8,128)(2,1)S(1)}, bf16[4,3,6,512]{3,2,1,0:T(8,128)(2,1)S(1)}, u32[]{:S(2)}, u32[]{:S(2)}) collective-permute-start(bf16[4,3,6,512]{3,2,1,0:T(8,128)(2,1)S(1)} %get-tuple-element.45), channel_id=1, source_target_pairs={{0,33},{1,34},{2,35},{3,36},{4,37},{5,38},{6,39},{7,40},{8,41},{9,... | collective-permute-start | bytes 221192 | tf_op jit(solution)/shard_map/ppermute | solution.py:389
  86.6 4.6 %collective-permute-start.9 = (bf16[64,1,32,128]{3,2,1,0:T(8,128)(2,1)S(1)}, bf16[64,1,32,128]{3,2,1,0:T(8,128)(2,1)S(1)}, u32[]{:S(2)}, u32[]{:S(2)}) collective-permute-start(bf16[64,1,32,128]{3,2,1,0:T(8,128)(2,1)S(1)} %all_to_all.11), channel_id=1, source_target_pairs={{0,32},{32,0},{64,96},{96,64},{1,33},{33,1},{65,97},{97,65},{2,34}... | collective-permute-start | bytes 1572872 | tf_op jit(solution)/shard_map/ppermute | solution.py:528

commit v4 on v3

--- a/solution.py
+++ b/solution.py
@@ -16,6 +16,7 @@
 PER_GROUP = LANES // HEAD
 
 AXES = ("lat", "lon")
+LOG2_E = 1.4426950408889634
 F32 = jnp.float32
 BF16 = jnp.bfloat16
 
@@ -32,26 +33,27 @@
     return lax.dot_general(a, b, (((0,), (0,)), ((), ())), preferred_element_type=F32)
 
 
-def head_mean(squares):
-    rows = lax.broadcasted_iota(jnp.int32, (LANES, LANES), 0) // HEAD
-    cols = lax.broadcasted_iota(jnp.int32, (LANES, LANES), 1) // HEAD
+def head_mean(values):
+    wide = 2 * LANES
+    rows = lax.broadcasted_iota(jnp.int32, (wide, wide), 0) // HEAD
+    cols = lax.broadcasted_iota(jnp.int32, (wide, wide), 1) // HEAD
     block = jnp.where(rows == cols, 1.0 / HEAD, 0.0).astype(BF16)
     parts = []
-    for g in range(squares.shape[1] // LANES):
-        part = squares[:, g * LANES : (g + 1) * LANES]
+    for start in range(0, values.shape[1], wide):
+        part = values[:, start : start + wide]
         top = part.astype(BF16)
         rest = (part - top.astype(F32)).astype(BF16)
         parts.append(mm(top, block) + mm(rest, block))
     return jnp.concatenate(parts, axis=1)
 
 
-def head_masks():
+def head_masks(dtype):
     lane = lax.broadcasted_iota(jnp.int32, (1, LANES), 1) // HEAD
-    return [jnp.where(lane == h, 1.0, 0.0).astype(F32) for h in range(PER_GROUP)]
+    return [jnp.where(lane == h, 1.0, 0.0).astype(dtype) for h in range(PER_GROUP)]
 
 
 def stack_heads(x, masks):
-    return jnp.concatenate([(x * m).astype(BF16) for m in masks], axis=0)
+    return jnp.concatenate([x * m for m in masks], axis=0)
 
 
 def unstack_heads(x, masks):
@@ -134,15 +136,14 @@
 
 
 def gelu_and_slope(u):
-    x = jnp.abs(u) * 0.7071067811865476
-    t = 1.0 / (1.0 + 0.3275911 * x)
-    e = jnp.exp(-0.5 * u * u)
-    poly = 1.061405429
+    t = 1.0 / (1.0 + (0.3275911 * 0.5**0.5) * jnp.abs(u))
+    e = jnp.exp2((-0.5 * LOG2_E) * (u * u))
+    poly = 0.5 * 1.061405429
     for c in (-1.453152027, 1.421413741, -0.284496736, 0.254829592):
-        poly = poly * t + c
-    tail = 0.5 * poly * t * e
+        poly = poly * t + 0.5 * c
+    tail = poly * t * e
     phi = jnp.where(u < 0, tail, 1.0 - tail)
-    return u * phi, phi + u * (0.3989422804014327 * e)
+    return u * phi, phi + (0.3989422804014327 * u) * e
 
 
 def pack_kernel(pixels_ref, land_ref, own_ref, south_ref, east_ref, corner_ref):
@@ -165,13 +166,13 @@
 def attention_kernel(
     region_ref, temper_ref, own_ref, south_ref, east_ref, corner_ref, wp_ref, bias_ref, land_ref,
     gain_ref, wqkv_ref, down_ref, up_ref, wo_ref,
-    hidden_ref, normed_ref, low_ref, qk_ref, v_ref, probs_ref,
-    state_ref, qs_ref, kn_ref, att_ref, downs_ref, ups_ref, same_ref,
+    hidden_ref, normed_ref, low_ref, inv_ref, qs_ref, kn_ref, v_ref, probs_ref,
+    state_ref, att_ref, downs_ref, ups_ref, same_ref,
 ):
     tokens, width = state_ref.shape
     count = tokens // TOKENS
     groups = width // LANES
-    masks = head_masks()
+    masks, narrow_masks = head_masks(F32), head_masks(BF16)
     patch_len = wp_ref.shape[0]
     into_windows(state_ref, own_ref, south_ref, east_ref, corner_ref)
     pix = state_ref[:, :patch_len].astype(BF16)
@@ -192,12 +193,12 @@
         if part == 2:
             v_ref[...] = qkv.astype(BF16)
         else:
-            qk_ref[:, cols] = qkv
-            unit = qkv * lax.rsqrt(head_mean(qkv * qkv) + 1e-06)
+            inv = lax.rsqrt(head_mean(qkv * qkv) + 1e-06)
+            inv_ref[:, cols] = inv
             if part == 0:
-                qs_ref[...] = unit * scale
+                qs_ref[...] = (qkv * inv * (scale * LOG2_E)).astype(BF16)
             else:
-                kn_ref[...] = unit.astype(BF16)
+                kn_ref[...] = (qkv * inv).astype(BF16)
     last_band = lax.axis_index("lat") == lax.axis_size("lat") - 1
     south = jnp.where(last_band, 1, 0).astype(jnp.int32)
     parts = same_ref.shape[0]
@@ -209,8 +210,8 @@
         same = same_ref[w // (count // parts)]
         for g in range(groups):
             cols = slice(g * LANES, (g + 1) * LANES)
-            stack = stack_heads(qs_ref[rows, cols], masks)
-            weights = jnp.exp(mm_nt(kn_ref[rows, cols], stack)) * same
+            stack = stack_heads(qs_ref[rows, cols], narrow_masks)
+            weights = jnp.exp2(mm_nt(kn_ref[rows, cols], stack)) * same
             total = jnp.sum(weights, axis=0, keepdims=True)
             probs = (weights * (1.0 / total)).astype(BF16)
             probs_ref[w * groups + g] = probs
@@ -218,7 +219,7 @@
             att_ref[rows, cols] = unstack_heads(mixed, masks).astype(BF16)
         return carry
 
-    lax.fori_loop(0, count, window, 0)
+    lax.fori_loop(0, count, window, 0, unroll=True)
     z = mm(att_ref[...], wo_ref[...]).astype(BF16)
     hidden_ref[...] = state_ref[...] + z.astype(F32)
 
@@ -238,7 +239,7 @@
     mixed_ref[...] = hidden
     unit_ref[...] = unit
     d_normed = jnp.zeros((tokens, width), F32)
-    chunk = 512
+    chunk = 2048
     for c in range(wup_ref.shape[1] // chunk):
         cols = slice(c * chunk, (c + 1) * chunk)
         act, slope = gelu_and_slope(mm(normed, wup_ref[:, cols]))
@@ -255,30 +256,23 @@
 
 
 def backward_kernel(
-    region_ref, temper_ref, normed_ref, low_ref, qk_ref, v_ref, probs_ref, datt_ref, up_ref,
+    region_ref, temper_ref, normed_ref, low_ref, inv_ref, qs_ref, kn_ref, v_ref, probs_ref, datt_ref,
+    up_ref,
     terms_ref,
-    qs_ref, kn_ref, dq_ref, dk_ref, dqkv_ref, ups_ref, grads_ref,
+    dq_ref, dk_ref, dqkv_ref, ups_ref, grads_ref,
 ):
     tokens, width = normed_ref.shape
     count = tokens // TOKENS
     groups = width // LANES
-    masks = head_masks()
+    masks, narrow_masks = head_masks(F32), head_masks(BF16)
     scale = scale_row(temper_ref, width)
-    inv = []
-    for part in range(2):
-        raw = qk_ref[:, part * width : (part + 1) * width]
-        inv.append(lax.rsqrt(head_mean(raw * raw) + 1e-06))
-        if part == 0:
-            qs_ref[...] = raw * inv[0] * scale
-        else:
-            kn_ref[...] = (raw * inv[1]).astype(BF16)
 
     def window(w, carry):
         rows = pl.ds(pl.multiple_of(w * TOKENS, TOKENS), TOKENS)
         for g in range(groups):
             cols = slice(g * LANES, (g + 1) * LANES)
-            d_stack = stack_heads(datt_ref[rows, cols].astype(F32), masks)
-            q_stack = stack_heads(qs_ref[rows, cols], masks)
+            d_stack = stack_heads(datt_ref[rows, cols], narrow_masks)
+            q_stack = stack_heads(qs_ref[rows, cols], narrow_masks)
             probs = probs_ref[w * groups + g]
             d_probs = mm_nt(v_ref[rows, cols], d_stack)
             wide = probs.astype(F32)
@@ -291,12 +285,14 @@
             dq_ref[rows, cols] = unstack_heads(mm_tn(d_scores, kn_ref[rows, cols]), masks)
         return carry
 
-    lax.fori_loop(0, count, window, 0)
-    for part, grad_ref in enumerate((dq_ref, dk_ref)):
+    lax.fori_loop(0, count, window, 0, unroll=True)
+    scales = ((scale, 1.0 / (scale * (LOG2_E * LOG2_E))), (1.0 / LOG2_E, 1.0 / LOG2_E))
+    for part, (unit_ref, grad_ref) in enumerate(((qs_ref, dq_ref), (kn_ref, dk_ref))):
         cols = slice(part * width, (part + 1) * width)
-        unit = qk_ref[:, cols] * inv[part]
-        grad = grad_ref[...] * scale if part == 0 else grad_ref[...]
-        dqkv_ref[:, cols] = (inv[part] * (grad - unit * head_mean(grad * unit))).astype(BF16)
+        unit, grad = unit_ref[...].astype(F32), grad_ref[...]
+        along = unit * head_mean(grad * unit)
+        first, second = scales[part]
+        dqkv_ref[:, cols] = (inv_ref[:, cols] * (grad * first - along * second)).astype(BF16)
     ups = factors(region_ref, up_ref, ups_ref)
     d_qkv = dqkv_ref[...]
     back = (mm_nt(d_qkv, ups) * adapter_columns(tokens, ups.shape[0])).astype(BF16)
@@ -444,7 +440,7 @@
     cot_own = cotangent[:, HALF_LAT:, HALF_LON:].astype(BF16)
     cot = move_halos(tuple(part.astype(BF16) for part in halos(cotangent)))
 
-    hidden, normed, low, qk, v, probs = call(
+    hidden, normed, low, inv, qs, kn, v, probs = call(
         attention_kernel,
         [SMEM] * 2 + [VMEM] * 12,
         (
@@ -453,12 +449,12 @@
             shape(tokens, rank * count, dtype=BF16),
             shape(tokens, 2 * width),
             shape(tokens, width, dtype=BF16),
+            shape(tokens, width, dtype=BF16),
+            shape(tokens, width, dtype=BF16),
             shape(count * groups, TOKENS, PER_GROUP * TOKENS, dtype=BF16),
         ),
         (
             ((tokens, width), F32),
-            ((tokens, width), F32),
-            ((tokens, width), BF16),
             ((tokens, width), BF16),
             ((rank * count, width), F32),
             ((rank * count, 3 * width), F32),
@@ -490,15 +486,12 @@
         hidden, cot_own, *cot, feedforward_gain[None], feedforward_up_weight, feedforward_down_weight,
         attention_output_weight,
     )
-    diagonal, west, north = move(diagonal, (1, 1)), move(west, (0, 1)), move(north, (1, 0))
     pieces = rank * 4 * width // LANES
     terms = call(
         backward_kernel,
-        [SMEM] * 2 + [VMEM] * 7,
+        [SMEM] * 2 + [VMEM] * 9,
         shape(pieces, 2 * count, LANES, dtype=BF16),
         (
-            ((tokens, width), F32),
-            ((tokens, width), BF16),
             ((tokens, width), F32),
             ((tokens, width), F32),
             ((tokens, 3 * width), BF16),
@@ -508,12 +501,9 @@
         flops=2 * tokens * width * 4 * width,
         moved=12_000_000,
         name="attention_backward",
-    )(region, head_logit_scale, normed, low, qk, v, probs, d_att, region_up_factor)
-    terms, north, west, diagonal = lax.optimization_barrier((terms, north, west, diagonal))
-    upper = jnp.concatenate((diagonal, north), axis=2).astype(F32)
-    lower = jnp.concatenate((west.astype(F32), home), axis=2)
-    mixed_state = jnp.concatenate((upper, lower), axis=1)
-
+    )(
+        region, head_logit_scale, normed, low, inv, qs, kn, v, probs, d_att, region_up_factor
+    )
     each = pieces // devices
     terms = lax.all_to_all(terms, AXES, 0, 0, tiled=True)
     sums = call(
@@ -524,7 +514,13 @@
     )(terms.reshape(devices, each, 2 * count, LANES))
     lats, lons = lax.axis_size("lat"), lax.axis_size("lon")
     cores = [[a * lons + b for a in range(c, lats, 2) for b in range(lons)] for c in range(2)]
+    sums, diagonal, west, north = lax.optimization_barrier((sums, diagonal, west, north))
     near = lax.all_to_all(sums, AXES, 0, 0, axis_index_groups=cores, tiled=True)
+    diagonal, west, north = move(diagonal, (1, 1)), move(west, (0, 1)), move(north, (1, 0))
+    near, diagonal, west, north = lax.optimization_barrier((near, diagonal, west, north))
+    upper = jnp.concatenate((diagonal, north), axis=2).astype(F32)
+    lower = jnp.concatenate((west.astype(F32), home), axis=2)
+    mixed_state = jnp.concatenate((upper, lower), axis=1)
     far = lax.ppermute(near, "lat", [(a, a ^ 1) for a in range(lats)])
     blocks = 4 * width // LANES
     order = (lats // 2, rank // lats, blocks, regions, LANES)

time: 93.3 us -> 87.4 us (0.937)
  blocking collectives: 33.3 us -> 18.3 us
  waiting for transfers between devices: 0.69 us -> 11.5 us
  Pallas kernels: 31.2 us -> 27.6 us
  starting transfers between devices: 22.2 us -> 24 us
    all_to_all x1 -> x0, blocking collectives: 14.7 us -> none  [local(): near = lax.all_to_all(sums, AXES, 0, 0, axis_index_groups=cores, tiled=True)]
    ppermute x9, waiting for transfers between devices: 0.46 us -> 11.3 us  [move(): return lax.ppermute(array, ('lat', 'lon'), pairs)]
    all_to_all x0 -> x1, starting transfers between devices: none -> 4.63 us  [local(): near = lax.all_to_all(sums, AXES, 0, 0, axis_index_groups=cores, tiled=True)]
    pallas_call x1, Pallas kernels: 10.3 us -> 8.11 us  [local(): call(backward_kernel, [SMEM] * 2 + [VMEM] * 9, shape(pieces, 2 * count, L...]
    ppermute x1, starting transfers between devices: 3.04 us -> 1.3 us  [local(): far = lax.ppermute(near, 'lat', [(a, a ^ 1) for a in range(lats)])]
    pallas_call x1, Pallas kernels: 9.25 us -> 7.92 us  [local(): call(attention_kernel, [SMEM] * 2 + [VMEM] * 12, (shape(tokens, width), s...]
    ppermute x9, starting transfers between devices: 19.1 us -> 18.1 us  [move(): return lax.ppermute(array, ('lat', 'lon'), pairs)]
  transfers between devices with their start and end apart: 10 -> 11, of which waited for: 2 -> 4; matrix products, arithmetic and copies ran while one was open for 3% -> 3% of each run, Pallas kernels for 21% -> 9%
where the time goes in v4:
time: 87.4 us; the launch traced here: 87.1 us
  Pallas kernels  27.6 us (32%)
  starting transfers between devices  24 us (27%)
  blocking collectives  18.3 us (21%)
  waiting for transfers between devices  11.5 us (13%)
  other arithmetic  2.76 us (3%)
  local copies, waits for them, and re-layouts  2 us (2%)
  between operations  0.91 us (1%)
    all_to_all x1, blocking collectives, local(): terms = lax.all_to_all(terms, AXES, 0, 0, tiled=True)  18.3 us
    ppermute x9, starting transfers between devices, move(): return lax.ppermute(array, ('lat', 'lon'), pairs)  18.1 us
    ppermute x9, waiting for transfers between devices, move(): return lax.ppermute(array, ('lat', 'lon'), pairs)  11.3 us
    pallas_call x1, Pallas kernels, local(): call(feed_kernel, [VMEM] * 9, (shape(*wide), shape(*wide, dtype=BF16), sh...  8.28 us
    pallas_call x1, Pallas kernels, local(): call(backward_kernel, [SMEM] * 2 + [VMEM] * 9, shape(pieces, 2 * count, L...  8.11 us
    pallas_call x1, Pallas kernels, local(): call(attention_kernel, [SMEM] * 2 + [VMEM] * 12, (shape(tokens, width), s...  7.92 us
    all_to_all x1, starting transfers between devices, local(): near = lax.all_to_all(sums, AXES, 0, 0, axis_index_groups=cores, tiled=True)  4.63 us
    pallas_call x1, Pallas kernels, local(): call(scale_kernel, [VMEM] * 2, (shape(regions, rank, width), shape(region...  1.91 us
  transfers between devices with their start and end apart: 11, of which 4 were waited for; matrix products, arithmetic and copies ran while one was open for 3% of the time, Pallas kernels for 9%

profile of v4, /device:TPU:1, one launch (start us, length us, event | category | flops | bytes accessed | tf_op | source)
XLA Modules:
  0.0 87.1 jit_solution(11205072739138446803)
XLA Ops:
  0.6 0.0 copy-start.1
  0.6 1.1 %copy-done.1 = bf16[4,6,24,500]{3,2,1,0:T(8,128)(2,1)S(1)} copy-done((bf16[4,6,24,500]{3,2,1,0:T(8,128)(2,1)S(1)}, bf16[4,6,24,500]{3,2,1,0:T(8,128)(2,1)}, u32[]{:S(2)}) %copy-start.1) | copy-done | bytes 576024
  1.7 0.7 copy-done.2
  2.4 0.3 pack_pixels.1
  2.6 7.2 %collective-permute-start.1 = (bf16[4,3,6,512]{3,2,1,0:T(8,128)(2,1)S(1)}, bf16[4,3,6,512]{3,2,1,0:T(8,128)(2,1)S(1)}, u32[]{:S(2)}, u32[]{:S(2)}) collective-permute-start(bf16[4,3,6,512]{3,2,1,0:T(8,128)(2,1)S(1)} %get-tuple-element.39), channel_id=1, source_target_pairs={{0,31},{1,0},{2,1},{3,2},{4,3},{5,4},{6,5},{7,6},{8,7},{9,8},{10,9... | collective-permute-start | bytes 221192 | tf_op jit(solution)/shard_map/ppermute | solution.py:385
  9.8 0.7 collective-permute-start.2
  10.5 2.0 %collective-permute-start = (bf16[4,3,18,512]{3,2,1,0:T(8,128)(2,1)S(1)}, bf16[4,3,18,512]{3,2,1,0:T(8,128)(2,1)S(1)}, u32[]{:S(2)}, u32[]{:S(2)}) collective-permute-start(bf16[4,3,18,512]{3,2,1,0:T(8,128)(2,1)S(1)} %get-tuple-element.38), channel_id=1, source_target_pairs={{0,96},{1,97},{2,98},{3,99},{4,100},{5,101},{6,102},{7,103},{8,104... | collective-permute-start | bytes 663560 | tf_op jit(solution)/shard_map/ppermute | solution.py:385
  12.5 1.5 %convert.6 = bf16[4,6,24,512]{3,2,1,0:T(8,128)(2,1)S(1)} convert(f32[4,6,24,512]{3,2,1,0:T(8,128)} %param.31) | non-fusion elementwise | flops 294912 | bytes 1769472 | tf_op jit(solution)/shard_map/convert.3
  13.9 0.0 copy-start
  13.9 0.0 copy-start.3
  14.0 0.0 copy-start.4
  14.0 0.0 copy-start.8
  14.0 0.0 copy-start.10
  14.0 0.0 copy-start.11
  14.0 0.0 copy-start.12
  14.0 0.0 copy-start.13
  14.0 0.2 fusion.1
  14.2 2.1 %collective-permute-start.3 = (bf16[4,3,18,512]{3,2,1,0:T(8,128)(2,1)S(1)}, bf16[4,3,18,512]{3,2,1,0:T(8,128)(2,1)S(1)}, u32[]{:S(2)}, u32[]{:S(2)}) collective-permute-start(bf16[4,3,18,512]{3,2,1,0:T(8,128)(2,1)S(1)} %get-tuple-element.67), channel_id=1, source_target_pairs={{0,96},{1,97},{2,98},{3,99},{4,100},{5,101},{6,102},{7,103},{8,104... | collective-permute-start | bytes 663560 | tf_op jit(solution)/shard_map/ppermute | solution.py:385
  16.3 0.9 %collective-permute-start.5 = (bf16[4,3,6,512]{3,2,1,0:T(8,128)(2,1)S(1)}, bf16[4,3,6,512]{3,2,1,0:T(8,128)(2,1)S(1)}, u32[]{:S(2)}, u32[]{:S(2)}) collective-permute-start(bf16[4,3,6,512]{3,2,1,0:T(8,128)(2,1)S(1)} %get-tuple-element.65), channel_id=1, source_target_pairs={{0,127},{1,96},{2,97},{3,98},{4,99},{5,100},{6,101},{7,102},{8,103... | collective-permute-start | bytes 221192 | tf_op jit(solution)/shard_map/ppermute | solution.py:385
  17.2 0.0 collective-permute-done.1.east_ref
  17.2 0.7 collective-permute-start.4
  17.9 0.0 collective-permute-done.2.corner_ref
  17.9 0.4 collective-permute-done.south_ref
  18.4 0.0 copy-done.7
  18.5 0.0 copy-start.5
  18.5 0.0 copy-start.6
  18.5 0.0 copy-start.14
  18.5 7.9 %attention_forward.1 = (f32[576,512]{1,0:T(8,128)S(1)}, bf16[576,512]{1,0:T(8,128)(2,1)S(1)}, bf16[576,32]{1,0:T(8,128)(2,1)S(1)}, f32[576,1024]{1,0:T(8,128)S(1...) custom-call(s32[2,1,2]{2,1,0:T(1,128)S(1)} %copy-done.3, ...), custom_call_target="tpu_custom_call" | custom-call | flops 1811939328 | bytes 20000000 | tf_op jit(solution)/shard_map/attention_forward/pallas_call | solution.py:443
  26.4 0.0 collective-permute-done.5.corner_ref
  26.4 0.0 collective-permute-done.4.east_ref
  26.4 0.0 collective-permute-done.3.south_ref
  26.5 8.3 %feed_forward.1 = (f32[4,3,18,512]{3,2,1,0:T(8,128)S(1)}, bf16[4,3,18,512]{3,2,1,0:T(8,128)(2,1)S(1)}, bf16[4,3,6,512]{3,2,1,0:T(8,128)(2,1)S(1)}, bf16[4,3,6,51...) custom-call(f32[576,512]{1,0:T(8,128)S(1)} %get-tuple-element.48.hidden_ref, ...), custom_call_target="tpu_custom_call" | custom-call | flops 4831838208 | bytes 20000000 | tf_op jit(solution)/shard_map/feed_forward/pallas_call | solution.py:471
  34.8 8.1 %attention_backward.1 = bf16[128,8,128]{2,1,0:T(8,128)(2,1)S(1)} custom-call(s32[2,1,2]{2,1,0:T(1,128)S(1)} %copy-done.3, f32[16]{0:T(128)S(1)} %copy-done.4, bf16[576,512]{1,0:T(8,128)(2,1)S(1)} %get-tuple-element.41.normed_ref, bf16[576,32]{1,0:T(8,128)(2,1)S(1)} %get-tuple-element.42.low_ref, f32[576,1024]{1,0:T(8,128)S(1)} %get-tuple-element.43.inv_ref, ...), custom_call_target="tpu_custom_call" | custom-call | flops 1207959552 | bytes 12000000 | tf_op jit(solution)/shard_map/attention_backward/pallas_call | solution.py:490
  42.9 18.3 %all_to_all.10 = bf16[128,8,128]{2,1,0:T(8,128)(2,1)S(1)} all-to-all(bf16[128,8,128]{2,1,0:T(8,128)(2,1)S(1)} %attention_backward.1), channel_id=1, replica_groups=mesh['lat'=4,'lon'=32] {'lat','lon'}, dimensions={0} | all-to-all | bytes 524288 | tf_op jit(solution)/shard_map/all_to_all | solution.py:508
  61.2 1.2 %sum_by_region.1 = bf16[64,1,32,128]{3,2,1,0:T(8,128)(2,1)} custom-call(bf16[128,1,8,128]{3,2,1,0:T(8,128)(2,1)S(1)} %bitcast.8), custom_call_target="tpu_custom_call" | custom-call | tf_op jit(solution)/shard_map/sum_by_region/pallas_call | solution.py:509
  62.3 4.6 %all-to-all-start.1 = ((bf16[64,1,32,128]{3,2,1,0:T(8,128)(2,1)}), bf16[64,1,32,128]{3,2,1,0:T(8,128)(2,1)S(1)}, u32[]{:S(2)}, u32[]{:S(2)}) async-start(bf16[64,1,32,128]{3,2,1,0:T(8,128)(2,1)} %sum_by_region.1), calls=%async_computation.1 | async-start | bytes 1048576 | tf_op jit(solution)/shard_map/all_to_all | solution.py:518
  67.0 3.8 %collective-permute-start.8 = (bf16[4,3,18,512]{3,2,1,0:T(8,128)(2,1)S(1)}, bf16[4,3,18,512]{3,2,1,0:T(8,128)(2,1)S(1)}, u32[]{:S(2)}, u32[]{:S(2)}) collective-permute-start(bf16[4,3,18,512]{3,2,1,0:T(8,128)(2,1)S(1)} %get-tuple-element.57), channel_id=1, source_target_pairs={{0,32},{1,33},{2,34},{3,35},{4,36},{5,37},{6,38},{7,39},{8,40},{9,... | collective-permute-start | bytes 663560 | tf_op jit(solution)/shard_map/ppermute | solution.py:385
  70.8 0.0 collective-permute-start.6
  70.8 0.7 collective-permute-start.7
  71.5 10.2 %collective-permute-done.6 = bf16[4,3,6,512]{3,2,1,0:T(8,128)(2,1)S(1)} collective-permute-done((bf16[4,3,6,512]{3,2,1,0:T(8,128)(2,1)S(1)}, bf16[4,3,6,512]{3,2,1,0:T(8,128)(2,1)S(1)}, u32[]{:S(2)}, u32[]{:S(2)}) %collective-permute-start.6) | collective-permute-done | bytes 73760 | tf_op jit(solution)/shard_map/ppermute | solution.py:385
  81.7 0.6 collective-permute-done.7
  82.3 0.0 collective-permute-done.8
  82.3 0.0 all-to-all-done.1
  82.3 1.3 %collective-permute-start.9 = (bf16[64,1,32,128]{3,2,1,0:T(8,128)(2,1)S(1)}, bf16[64,1,32,128]{3,2,1,0:T(8,128)(2,1)S(1)}, u32[]{:S(2)}, u32[]{:S(2)}) collective-permute-start(bf16[64,1,32,128]{3,2,1,0:T(8,128)(2,1)S(1)} %all-to-all-done.1), channel_id=1, source_target_pairs={{0,32},{32,0},{64,96},{96,64},{1,33},{33,1},{65,97},{97,65},{2,34}... | collective-permute-start | bytes 1572872 | tf_op jit(solution)/shard_map/ppermute | solution.py:524
  83.6 0.1 maximum_convert_fusion
  83.7 1.2 %maximum_maximum_fusion = f32[4,6,24,512]{3,2,1,0:T(8,128)} fusion(f32[4,3,18,512]{3,2,1,0:T(8,128)S(1)} %get-tuple-element.61, f32[4,3,6,512]{3,2,1,0:T(8,128)S(1)} %convert_element_type.5, f32[4,3,24,512]{3,2,1,0:T(8,128)S(1)} %maximum_convert_fusion), kind=kLoop, calls=%fused_computation | loop fusion | flops 589824 | bytes 2359296 | tf_op jit(solution)/shard_map/concatenate | solution.py:523
  84.9 0.2 collective-permute-done.9
  85.2 1.9 %scale_steps.1 = (f32[32,8,512]{2,1,0:T(8,128)}, f32[32,8,1536]{2,1,0:T(8,128)}) custom-call(bf16[2,2,16,32,128]{4,3,2,1,0:T(8,128)(2,1)S(1)} %bitcast.7, bf16[2,2,16,32,128]{4,3,2,1,0:T(8,128)(2,1)S(1)} %bitcast.9), custom_call_target="tpu_custom_call" | custom-call | tf_op jit(solution)/shard_map/scale_steps/pallas_call | solution.py:527
  (17 shorter events, 0.1 us)
Async XLA Ops:
  0.6 1.1 %copy-start.1 = (bf16[4,6,24,500]{3,2,1,0:T(8,128)(2,1)S(1)}, bf16[4,6,24,500]{3,2,1,0:T(8,128)(2,1)}, u32[]{:S(2)}) copy-start(bf16[4,6,24,500]{3,2,1,0:T(8,128)(2,1)} %pixels_ref.1) | copy-start | bytes 1728004
  1.7 0.7 copy-start.2
  2.4 16.0 %copy-start.9 = (bf16[500,512]{1,0:T(8,128)(2,1)S(1)}, bf16[500,512]{1,0:T(8,128)(2,1)}, u32[]{:S(2)}) copy-start(bf16[500,512]{1,0:T(8,128)(2,1)} %wp_ref.1) | copy-start | bytes 1536004
  2.6 14.6 %collective-permute-start.1 = (bf16[4,3,6,512]{3,2,1,0:T(8,128)(2,1)S(1)}, bf16[4,3,6,512]{3,2,1,0:T(8,128)(2,1)S(1)}, u32[]{:S(2)}, u32[]{:S(2)}) collective-permute-start(bf16[4,3,6,512]{3,2,1,0:T(8,128)(2,1)S(1)} %get-tuple-element.39), channel_id=1, source_target_pairs={{0,31},{1,0},{2,1},{3,2},{4,3},{5,4},{6,5},{7,6},{8,7},{9,8},{10,9... | collective-permute-start | bytes 221192 | tf_op jit(solution)/shard_map/ppermute | solution.py:385
  9.8 8.1 %collective-permute-start.2 = (bf16[4,3,6,512]{3,2,1,0:T(8,128)(2,1)S(1)}, bf16[4,3,6,512]{3,2,1,0:T(8,128)(2,1)S(1)}, u32[]{:S(2)}, u32[]{:S(2)}) collective-permute-start(bf16[4,3,6,512]{3,2,1,0:T(8,128)(2,1)S(1)} %get-tuple-element.40), channel_id=1, source_target_pairs={{0,127},{1,96},{2,97},{3,98},{4,99},{5,100},{6,101},{7,102},{8,103... | collective-permute-start | bytes 221192 | tf_op jit(solution)/shard_map/ppermute | solution.py:385
  10.5 7.9 %collective-permute-start = (bf16[4,3,18,512]{3,2,1,0:T(8,128)(2,1)S(1)}, bf16[4,3,18,512]{3,2,1,0:T(8,128)(2,1)S(1)}, u32[]{:S(2)}, u32[]{:S(2)}) collective-permute-start(bf16[4,3,18,512]{3,2,1,0:T(8,128)(2,1)S(1)} %get-tuple-element.38), channel_id=1, source_target_pairs={{0,96},{1,97},{2,98},{3,99},{4,100},{5,101},{6,102},{7,103},{8,104... | collective-permute-start | bytes 663560 | tf_op jit(solution)/shard_map/ppermute | solution.py:385
  12.5 5.9 %copy-start.7 = (bf16[512,1536]{1,0:T(8,128)(2,1)S(1)}, bf16[512,1536]{1,0:T(8,128)(2,1)}, u32[]{:S(2)}) copy-start(bf16[512,1536]{1,0:T(8,128)(2,1)} %wqkv_ref.1) | copy-start | bytes 4718596
  13.9 4.4 %copy-start = (bf16[32,8,1536]{2,1,0:T(8,128)(2,1)S(1)}, bf16[32,8,1536]{2,1,0:T(8,128)(2,1)}, u32[]{:S(2)}) copy-start(bf16[32,8,1536]{2,1,0:T(8,128)(2,1)} %up_ref.3) | copy-start | bytes 2359300
  13.9 4.4 %copy-start.3 = (s32[2,1,2]{2,1,0:T(1,128)S(1)}, s32[2,1,2]{2,1,0:T(1,128)}, u32[]{:S(2)}) copy-start(s32[2,1,2]{2,1,0:T(1,128)} %region_ref.3) | copy-start | bytes 52
  14.0 4.4 %copy-start.4 = (f32[16]{0:T(128)S(1)}, f32[16]{0:T(128)}, u32[]{:S(2)}) copy-start(f32[16]{0:T(128)} %temper_ref.3) | copy-start | bytes 196
  14.0 4.4 %copy-start.8 = (bf16[512,512]{1,0:T(8,128)(2,1)S(1)}, bf16[512,512]{1,0:T(8,128)(2,1)}, u32[]{:S(2)}) copy-start(bf16[512,512]{1,0:T(8,128)(2,1)} %wo_ref.3) | copy-start | bytes 1572868
  14.0 4.4 %copy-start.10 = (bf16[32,8,512]{2,1,0:T(8,128)(2,1)S(1)}, bf16[32,8,512]{2,1,0:T(8,128)(2,1)}, u32[]{:S(2)}) copy-start(bf16[32,8,512]{2,1,0:T(8,128)(2,1)} %down_ref.1) | copy-start | bytes 786436
  14.0 4.4 %copy-start.11 = (f32[512]{0:T(512)S(1)}, f32[512]{0:T(512)}, u32[]{:S(2)}) copy-start(f32[512]{0:T(512)} %param.20) | copy-start | bytes 6148
  14.0 4.4 %copy-start.12 = (f32[512]{0:T(512)S(1)}, f32[512]{0:T(512)}, u32[]{:S(2)}) copy-start(f32[512]{0:T(512)} %param.21) | copy-start | bytes 6148
  14.0 4.4 %copy-start.13 = (f32[512]{0:T(512)S(1)}, f32[512]{0:T(512)}, u32[]{:S(2)}) copy-start(f32[512]{0:T(512)} %param.22) | copy-start | bytes 6148
  14.2 12.2 %collective-permute-start.3 = (bf16[4,3,18,512]{3,2,1,0:T(8,128)(2,1)S(1)}, bf16[4,3,18,512]{3,2,1,0:T(8,128)(2,1)S(1)}, u32[]{:S(2)}, u32[]{:S(2)}) collective-permute-start(bf16[4,3,18,512]{3,2,1,0:T(8,128)(2,1)S(1)} %get-tuple-element.67), channel_id=1, source_target_pairs={{0,96},{1,97},{2,98},{3,99},{4,100},{5,101},{6,102},{7,103},{8,104... | collective-permute-start | bytes 663560 | tf_op jit(solution)/shard_map/ppermute | solution.py:385
  16.3 10.1 %collective-permute-start.5 = (bf16[4,3,6,512]{3,2,1,0:T(8,128)(2,1)S(1)}, bf16[4,3,6,512]{3,2,1,0:T(8,128)(2,1)S(1)}, u32[]{:S(2)}, u32[]{:S(2)}) collective-permute-start(bf16[4,3,6,512]{3,2,1,0:T(8,128)(2,1)S(1)} %get-tuple-element.65), channel_id=1, source_target_pairs={{0,127},{1,96},{2,97},{3,98},{4,99},{5,100},{6,101},{7,102},{8,103... | collective-permute-start | bytes 221192 | tf_op jit(solution)/shard_map/ppermute | solution.py:385
  17.2 9.2 %collective-permute-start.4 = (bf16[4,3,6,512]{3,2,1,0:T(8,128)(2,1)S(1)}, bf16[4,3,6,512]{3,2,1,0:T(8,128)(2,1)S(1)}, u32[]{:S(2)}, u32[]{:S(2)}) collective-permute-start(bf16[4,3,6,512]{3,2,1,0:T(8,128)(2,1)S(1)} %get-tuple-element.66), channel_id=1, source_target_pairs={{0,31},{1,0},{2,1},{3,2},{4,3},{5,4},{6,5},{7,6},{8,7},{9,8},{10,9... | collective-permute-start | bytes 221192 | tf_op jit(solution)/shard_map/ppermute | solution.py:385
  18.5 8.0 %copy-start.5 = (bf16[512,2048]{1,0:T(8,128)(2,1)S(1)}, bf16[512,2048]{1,0:T(8,128)(2,1)}, u32[]{:S(2)}) copy-start(bf16[512,2048]{1,0:T(8,128)(2,1)} %wup_ref.1) | copy-start | bytes 6291460
  18.5 8.0 %copy-start.6 = (bf16[2048,512]{1,0:T(8,128)(2,1)S(1)}, bf16[2048,512]{1,0:T(8,128)(2,1)}, u32[]{:S(2)}) copy-start(bf16[2048,512]{1,0:T(8,128)(2,1)} %wdn_ref.1) | copy-start | bytes 6291460
  18.5 8.0 %copy-start.14 = (f32[512]{0:T(512)S(1)}, f32[512]{0:T(512)}, u32[]{:S(2)}) copy-start(f32[512]{0:T(512)} %param.28) | copy-start | bytes 6148
  62.3 20.0 %all-to-all-start.1 = ((bf16[64,1,32,128]{3,2,1,0:T(8,128)(2,1)}), bf16[64,1,32,128]{3,2,1,0:T(8,128)(2,1)S(1)}, u32[]{:S(2)}, u32[]{:S(2)}) async-start(bf16[64,1,32,128]{3,2,1,0:T(8,128)(2,1)} %sum_by_region.1), calls=%async_computation.1 | async-start | bytes 1048576 | tf_op jit(solution)/shard_map/all_to_all | solution.py:518
  67.0 15.3 %collective-permute-start.8 = (bf16[4,3,18,512]{3,2,1,0:T(8,128)(2,1)S(1)}, bf16[4,3,18,512]{3,2,1,0:T(8,128)(2,1)S(1)}, u32[]{:S(2)}, u32[]{:S(2)}) collective-permute-start(bf16[4,3,18,512]{3,2,1,0:T(8,128)(2,1)S(1)} %get-tuple-element.57), channel_id=1, source_target_pairs={{0,32},{1,33},{2,34},{3,35},{4,36},{5,37},{6,38},{7,39},{8,40},{9,... | collective-permute-start | bytes 663560 | tf_op jit(solution)/shard_map/ppermute | solution.py:385
  70.8 10.9 %collective-permute-start.6 = (bf16[4,3,6,512]{3,2,1,0:T(8,128)(2,1)S(1)}, bf16[4,3,6,512]{3,2,1,0:T(8,128)(2,1)S(1)}, u32[]{:S(2)}, u32[]{:S(2)}) collective-permute-start(bf16[4,3,6,512]{3,2,1,0:T(8,128)(2,1)S(1)} %get-tuple-element.55), channel_id=1, source_target_pairs={{0,33},{1,34},{2,35},{3,36},{4,37},{5,38},{6,39},{7,40},{8,41},{9,... | collective-permute-start | bytes 221192 | tf_op jit(solution)/shard_map/ppermute | solution.py:385
  70.8 11.5 %collective-permute-start.7 = (bf16[4,3,6,512]{3,2,1,0:T(8,128)(2,1)S(1)}, bf16[4,3,6,512]{3,2,1,0:T(8,128)(2,1)S(1)}, u32[]{:S(2)}, u32[]{:S(2)}) collective-permute-start(bf16[4,3,6,512]{3,2,1,0:T(8,128)(2,1)S(1)} %get-tuple-element.56), channel_id=1, source_target_pairs={{0,1},{1,2},{2,3},{3,4},{4,5},{5,6},{6,7},{7,8},{8,9},{9,10},{10,1... | collective-permute-start | bytes 221192 | tf_op jit(solution)/shard_map/ppermute | solution.py:385
  82.3 2.8 %collective-permute-start.9 = (bf16[64,1,32,128]{3,2,1,0:T(8,128)(2,1)S(1)}, bf16[64,1,32,128]{3,2,1,0:T(8,128)(2,1)S(1)}, u32[]{:S(2)}, u32[]{:S(2)}) collective-permute-start(bf16[64,1,32,128]{3,2,1,0:T(8,128)(2,1)S(1)} %all-to-all-done.1), channel_id=1, source_target_pairs={{0,32},{32,0},{64,96},{96,64},{1,33},{33,1},{65,97},{97,65},{2,34}... | collective-permute-start | bytes 1572872 | tf_op jit(solution)/shard_map/ppermute | solution.py:524

commit v5 on v4

--- a/solution.py
+++ b/solution.py
@@ -136,14 +136,8 @@
 
 
 def gelu_and_slope(u):
-    t = 1.0 / (1.0 + (0.3275911 * 0.5**0.5) * jnp.abs(u))
-    e = jnp.exp2((-0.5 * LOG2_E) * (u * u))
-    poly = 0.5 * 1.061405429
-    for c in (-1.453152027, 1.421413741, -0.284496736, 0.254829592):
-        poly = poly * t + 0.5 * c
-    tail = poly * t * e
-    phi = jnp.where(u < 0, tail, 1.0 - tail)
-    return u * phi, phi + (0.3989422804014327 * u) * e
+    phi = 0.5 + 0.5 * lax.erf(u * 0.5**0.5)
+    return u * phi, phi + (0.3989422804014327 * u) * jnp.exp2((-0.5 * LOG2_E) * (u * u))
 
 
 def pack_kernel(pixels_ref, land_ref, own_ref, south_ref, east_ref, corner_ref):
@@ -151,7 +145,7 @@
     width = own_ref.shape[3]
     eye = lax.broadcasted_iota(jnp.int32, (cols, cols), 0)
     eye = jnp.where(eye == lax.broadcasted_iota(jnp.int32, (cols, cols), 1), 1.0, 0.0)
-    land = mm_nt(eye.astype(BF16), land_ref[...].astype(F32).astype(BF16))
+    land = mm_nt(eye.astype(BF16), land_ref[...])
     lane = lax.broadcasted_iota(jnp.int32, (cols, width), 1)
     blank = jnp.zeros((cols, width - patch_len), F32)
     for level in range(levels):
@@ -434,7 +428,7 @@
         tuple(shape(*dims, dtype=BF16) for dims in (wide, wide, narrow, narrow)),
         moved=2_000_000,
         name="pack_pixels",
-    )(pixels, land_patch_mask)
+    )(pixels, land_patch_mask.astype(BF16))
     pix, cotangent = lax.optimization_barrier((pix, cotangent))
     pix = move_halos(pix)
     cot_own = cotangent[:, HALF_LAT:, HALF_LON:].astype(BF16)
@@ -514,7 +508,6 @@
     )(terms.reshape(devices, each, 2 * count, LANES))
     lats, lons = lax.axis_size("lat"), lax.axis_size("lon")
     cores = [[a * lons + b for a in range(c, lats, 2) for b in range(lons)] for c in range(2)]
-    sums, diagonal, west, north = lax.optimization_barrier((sums, diagonal, west, north))
     near = lax.all_to_all(sums, AXES, 0, 0, axis_index_groups=cores, tiled=True)
     diagonal, west, north = move(diagonal, (1, 1)), move(west, (0, 1)), move(north, (1, 0))
     near, diagonal, west, north = lax.optimization_barrier((near, diagonal, west, north))

time: 87.4 us -> 85.9 us (0.983)
  Pallas kernels: 27.6 us -> 26.2 us
    pallas_call x1, Pallas kernels: 8.28 us -> 6.84 us  [local(): call(feed_kernel, [VMEM] * 9, (shape(*wide), shape(*wide, dtype=BF16), sh...]
    unnamed x30 -> x28, local copies, waits for them, and re-layouts: 1.82 us -> 1.14 us
where the time goes in v5:
time: 85.9 us; the launch traced here: 85.6 us
  Pallas kernels  26.2 us (31%)
  starting transfers between devices  24 us (28%)
  blocking collectives  18.3 us (21%)
  waiting for transfers between devices  11.5 us (13%)
  other arithmetic  3.45 us (4%)
  local copies, waits for them, and re-layouts  1.32 us (2%)
  between operations  0.9 us (1%)
    all_to_all x1, blocking collectives, local(): terms = lax.all_to_all(terms, AXES, 0, 0, tiled=True)  18.3 us
    ppermute x9, starting transfers between devices, move(): return lax.ppermute(array, ('lat', 'lon'), pairs)  18.1 us
    ppermute x9, waiting for transfers between devices, move(): return lax.ppermute(array, ('lat', 'lon'), pairs)  11.3 us
    pallas_call x1, Pallas kernels, local(): call(backward_kernel, [SMEM] * 2 + [VMEM] * 9, shape(pieces, 2 * count, L...  8.11 us
    pallas_call x1, Pallas kernels, local(): call(attention_kernel, [SMEM] * 2 + [VMEM] * 12, (shape(tokens, width), s...  7.91 us
    pallas_call x1, Pallas kernels, local(): call(feed_kernel, [VMEM] * 9, (shape(*wide), shape(*wide, dtype=BF16), sh...  6.84 us
    all_to_all x1, starting transfers between devices, local(): near = lax.all_to_all(sums, AXES, 0, 0, axis_index_groups=cores, tiled=True)  4.63 us
    pallas_call x1, Pallas kernels, local(): call(scale_kernel, [VMEM] * 2, (shape(regions, rank, width), shape(region...  1.91 us
  transfers between devices with their start and end apart: 11, of which 4 were waited for; matrix products, arithmetic and copies ran while one was open for 3% of the time, Pallas kernels for 9%

profile of v5, /device:TPU:1, one launch (start us, length us, event | category | flops | bytes accessed | tf_op | source)
XLA Modules:
  0.0 85.6 jit_solution(16099250105941703676)
XLA Ops:
  0.6 0.7 convert_element_type.6.land_ref
  1.3 1.1 %copy-done.1 = bf16[4,6,24,500]{3,2,1,0:T(8,128)(2,1)S(1)} copy-done((bf16[4,6,24,500]{3,2,1,0:T(8,128)(2,1)S(1)}, bf16[4,6,24,500]{3,2,1,0:T(8,128)(2,1)}, u32[]{:S(2)}) %copy-start.1) | copy-done | bytes 576024
  2.4 0.3 pack_pixels.1
  2.6 7.2 %collective-permute-start.1 = (bf16[4,3,6,512]{3,2,1,0:T(8,128)(2,1)S(1)}, bf16[4,3,6,512]{3,2,1,0:T(8,128)(2,1)S(1)}, u32[]{:S(2)}, u32[]{:S(2)}) collective-permute-start(bf16[4,3,6,512]{3,2,1,0:T(8,128)(2,1)S(1)} %get-tuple-element.35), channel_id=1, source_target_pairs={{0,31},{1,0},{2,1},{3,2},{4,3},{5,4},{6,5},{7,6},{8,7},{9,8},{10,9... | collective-permute-start | bytes 221192 | tf_op jit(solution)/shard_map/ppermute | solution.py:379
  9.8 0.7 collective-permute-start.2
  10.5 2.0 %collective-permute-start = (bf16[4,3,18,512]{3,2,1,0:T(8,128)(2,1)S(1)}, bf16[4,3,18,512]{3,2,1,0:T(8,128)(2,1)S(1)}, u32[]{:S(2)}, u32[]{:S(2)}) collective-permute-start(bf16[4,3,18,512]{3,2,1,0:T(8,128)(2,1)S(1)} %get-tuple-element.34), channel_id=1, source_target_pairs={{0,96},{1,97},{2,98},{3,99},{4,100},{5,101},{6,102},{7,103},{8,104... | collective-permute-start | bytes 663560 | tf_op jit(solution)/shard_map/ppermute | solution.py:379
  12.5 1.5 %convert.6 = bf16[4,6,24,512]{3,2,1,0:T(8,128)(2,1)S(1)} convert(f32[4,6,24,512]{3,2,1,0:T(8,128)} %param.31) | non-fusion elementwise | flops 294912 | bytes 1769472 | tf_op jit(solution)/shard_map/convert.3
  13.9 0.0 copy-start
  13.9 0.0 copy-start.2
  14.0 0.0 copy-start.3
  14.0 0.0 copy-start.7
  14.0 0.0 copy-start.9
  14.0 0.0 copy-start.10
  14.0 0.0 copy-start.11
  14.0 0.0 copy-start.12
  14.0 0.2 fusion.1
  14.2 2.1 %collective-permute-start.3 = (bf16[4,3,18,512]{3,2,1,0:T(8,128)(2,1)S(1)}, bf16[4,3,18,512]{3,2,1,0:T(8,128)(2,1)S(1)}, u32[]{:S(2)}, u32[]{:S(2)}) collective-permute-start(bf16[4,3,18,512]{3,2,1,0:T(8,128)(2,1)S(1)} %get-tuple-element.59), channel_id=1, source_target_pairs={{0,96},{1,97},{2,98},{3,99},{4,100},{5,101},{6,102},{7,103},{8,104... | collective-permute-start | bytes 663560 | tf_op jit(solution)/shard_map/ppermute | solution.py:379
  16.3 0.9 %collective-permute-start.5 = (bf16[4,3,6,512]{3,2,1,0:T(8,128)(2,1)S(1)}, bf16[4,3,6,512]{3,2,1,0:T(8,128)(2,1)S(1)}, u32[]{:S(2)}, u32[]{:S(2)}) collective-permute-start(bf16[4,3,6,512]{3,2,1,0:T(8,128)(2,1)S(1)} %get-tuple-element.57), channel_id=1, source_target_pairs={{0,127},{1,96},{2,97},{3,98},{4,99},{5,100},{6,101},{7,102},{8,103... | collective-permute-start | bytes 221192 | tf_op jit(solution)/shard_map/ppermute | solution.py:379
  17.2 0.0 collective-permute-done.1.east_ref
  17.2 0.7 collective-permute-start.4
  17.9 0.0 collective-permute-done.2.corner_ref
  17.9 0.4 collective-permute-done.south_ref
  18.4 0.0 copy-done.8
  18.4 0.0 copy-done.6
  18.5 0.0 copy-start.4
  18.5 0.0 copy-start.5
  18.5 0.0 copy-start.13
  18.5 7.9 %attention_forward.1 = (f32[576,512]{1,0:T(8,128)S(1)}, bf16[576,512]{1,0:T(8,128)(2,1)S(1)}, bf16[576,32]{1,0:T(8,128)(2,1)S(1)}, f32[576,1024]{1,0:T(8,128)S(1...) custom-call(s32[2,1,2]{2,1,0:T(1,128)S(1)} %copy-done.2, ...), custom_call_target="tpu_custom_call" | custom-call | flops 1811939328 | bytes 20000000 | tf_op jit(solution)/shard_map/attention_forward/pallas_call | solution.py:437
  26.4 0.0 collective-permute-done.5.corner_ref
  26.4 0.0 collective-permute-done.4.east_ref
  26.4 0.0 collective-permute-done.3.south_ref
  26.5 6.8 %feed_forward.1 = (f32[4,3,18,512]{3,2,1,0:T(8,128)S(1)}, bf16[4,3,18,512]{3,2,1,0:T(8,128)(2,1)S(1)}, bf16[4,3,6,512]{3,2,1,0:T(8,128)(2,1)S(1)}, bf16[4,3,6,51...) custom-call(f32[576,512]{1,0:T(8,128)S(1)} %get-tuple-element.44.hidden_ref, ...), custom_call_target="tpu_custom_call" | custom-call | flops 4831838208 | bytes 20000000 | tf_op jit(solution)/shard_map/feed_forward/pallas_call | solution.py:465
  33.3 8.1 %attention_backward.1 = bf16[128,8,128]{2,1,0:T(8,128)(2,1)S(1)} custom-call(s32[2,1,2]{2,1,0:T(1,128)S(1)} %copy-done.2, f32[16]{0:T(128)S(1)} %copy-done.3, bf16[576,512]{1,0:T(8,128)(2,1)S(1)} %get-tuple-element.37.normed_ref, bf16[576,32]{1,0:T(8,128)(2,1)S(1)} %get-tuple-element.38.low_ref, f32[576,1024]{1,0:T(8,128)S(1)} %get-tuple-element.39.inv_ref, ...), custom_call_target="tpu_custom_call" | custom-call | flops 1207959552 | bytes 12000000 | tf_op jit(solution)/shard_map/attention_backward/pallas_call | solution.py:484
  41.4 18.3 %all_to_all.10 = bf16[128,8,128]{2,1,0:T(8,128)(2,1)S(1)} all-to-all(bf16[128,8,128]{2,1,0:T(8,128)(2,1)S(1)} %attention_backward.1), channel_id=1, replica_groups=mesh['lat'=4,'lon'=32] {'lat','lon'}, dimensions={0} | all-to-all | bytes 524288 | tf_op jit(solution)/shard_map/all_to_all | solution.py:502
  59.7 1.2 %sum_by_region.1 = bf16[64,1,32,128]{3,2,1,0:T(8,128)(2,1)} custom-call(bf16[128,1,8,128]{3,2,1,0:T(8,128)(2,1)S(1)} %bitcast.8), custom_call_target="tpu_custom_call" | custom-call | tf_op jit(solution)/shard_map/sum_by_region/pallas_call | solution.py:503
  60.9 4.6 %all-to-all-start.1 = ((bf16[64,1,32,128]{3,2,1,0:T(8,128)(2,1)}), bf16[64,1,32,128]{3,2,1,0:T(8,128)(2,1)S(1)}, u32[]{:S(2)}, u32[]{:S(2)}) async-start(bf16[64,1,32,128]{3,2,1,0:T(8,128)(2,1)} %sum_by_region.1), calls=%async_computation.1 | async-start | bytes 1048576 | tf_op jit(solution)/shard_map/all_to_all | solution.py:511
  65.5 3.8 %collective-permute-start.8 = (bf16[4,3,18,512]{3,2,1,0:T(8,128)(2,1)S(1)}, bf16[4,3,18,512]{3,2,1,0:T(8,128)(2,1)S(1)}, u32[]{:S(2)}, u32[]{:S(2)}) collective-permute-start(bf16[4,3,18,512]{3,2,1,0:T(8,128)(2,1)S(1)} %get-tuple-element.49), channel_id=1, source_target_pairs={{0,32},{1,33},{2,34},{3,35},{4,36},{5,37},{6,38},{7,39},{8,40},{9,... | collective-permute-start | bytes 663560 | tf_op jit(solution)/shard_map/ppermute | solution.py:379
  69.4 0.0 collective-permute-start.6
  69.4 0.7 collective-permute-start.7
  70.1 10.2 %collective-permute-done.6 = bf16[4,3,6,512]{3,2,1,0:T(8,128)(2,1)S(1)} collective-permute-done((bf16[4,3,6,512]{3,2,1,0:T(8,128)(2,1)S(1)}, bf16[4,3,6,512]{3,2,1,0:T(8,128)(2,1)S(1)}, u32[]{:S(2)}, u32[]{:S(2)}) %collective-permute-start.6) | collective-permute-done | bytes 73760 | tf_op jit(solution)/shard_map/ppermute | solution.py:379
  80.3 0.6 collective-permute-done.7
  80.9 0.0 collective-permute-done.8
  80.9 0.0 all-to-all-done.1
  80.9 1.3 %collective-permute-start.9 = (bf16[64,1,32,128]{3,2,1,0:T(8,128)(2,1)S(1)}, bf16[64,1,32,128]{3,2,1,0:T(8,128)(2,1)S(1)}, u32[]{:S(2)}, u32[]{:S(2)}) collective-permute-start(bf16[64,1,32,128]{3,2,1,0:T(8,128)(2,1)S(1)} %all-to-all-done.1), channel_id=1, source_target_pairs={{0,32},{32,0},{64,96},{96,64},{1,33},{33,1},{65,97},{97,65},{2,34}... | collective-permute-start | bytes 1572872 | tf_op jit(solution)/shard_map/ppermute | solution.py:517
  82.2 0.1 maximum_convert_fusion
  82.3 1.2 %maximum_maximum_fusion = f32[4,6,24,512]{3,2,1,0:T(8,128)} fusion(f32[4,3,18,512]{3,2,1,0:T(8,128)S(1)} %get-tuple-element.53, f32[4,3,6,512]{3,2,1,0:T(8,128)S(1)} %convert_element_type.15, f32[4,3,24,512]{3,2,1,0:T(8,128)S(1)} %maximum_convert_fusion), kind=kLoop, calls=%fused_computation | loop fusion | flops 589824 | bytes 2359296 | tf_op jit(solution)/shard_map/concatenate | solution.py:516
  83.5 0.2 collective-permute-done.9
  83.7 1.9 %scale_steps.1 = (f32[32,8,512]{2,1,0:T(8,128)}, f32[32,8,1536]{2,1,0:T(8,128)}) custom-call(bf16[2,2,16,32,128]{4,3,2,1,0:T(8,128)(2,1)S(1)} %bitcast.7, bf16[2,2,16,32,128]{4,3,2,1,0:T(8,128)(2,1)S(1)} %bitcast.9), custom_call_target="tpu_custom_call" | custom-call | tf_op jit(solution)/shard_map/scale_steps/pallas_call | solution.py:520
  (16 shorter events, 0.1 us)
Async XLA Ops:
  1.3 1.1 %copy-start.1 = (bf16[4,6,24,500]{3,2,1,0:T(8,128)(2,1)S(1)}, bf16[4,6,24,500]{3,2,1,0:T(8,128)(2,1)}, u32[]{:S(2)}) copy-start(bf16[4,6,24,500]{3,2,1,0:T(8,128)(2,1)} %pixels_ref.1) | copy-start | bytes 1728004
  2.4 16.0 %copy-start.8 = (bf16[500,512]{1,0:T(8,128)(2,1)S(1)}, bf16[500,512]{1,0:T(8,128)(2,1)}, u32[]{:S(2)}) copy-start(bf16[500,512]{1,0:T(8,128)(2,1)} %wp_ref.1) | copy-start | bytes 1536004
  2.6 14.6 %collective-permute-start.1 = (bf16[4,3,6,512]{3,2,1,0:T(8,128)(2,1)S(1)}, bf16[4,3,6,512]{3,2,1,0:T(8,128)(2,1)S(1)}, u32[]{:S(2)}, u32[]{:S(2)}) collective-permute-start(bf16[4,3,6,512]{3,2,1,0:T(8,128)(2,1)S(1)} %get-tuple-element.35), channel_id=1, source_target_pairs={{0,31},{1,0},{2,1},{3,2},{4,3},{5,4},{6,5},{7,6},{8,7},{9,8},{10,9... | collective-permute-start | bytes 221192 | tf_op jit(solution)/shard_map/ppermute | solution.py:379
  9.8 8.1 %collective-permute-start.2 = (bf16[4,3,6,512]{3,2,1,0:T(8,128)(2,1)S(1)}, bf16[4,3,6,512]{3,2,1,0:T(8,128)(2,1)S(1)}, u32[]{:S(2)}, u32[]{:S(2)}) collective-permute-start(bf16[4,3,6,512]{3,2,1,0:T(8,128)(2,1)S(1)} %get-tuple-element.36), channel_id=1, source_target_pairs={{0,127},{1,96},{2,97},{3,98},{4,99},{5,100},{6,101},{7,102},{8,103... | collective-permute-start | bytes 221192 | tf_op jit(solution)/shard_map/ppermute | solution.py:379
  10.5 7.9 %collective-permute-start = (bf16[4,3,18,512]{3,2,1,0:T(8,128)(2,1)S(1)}, bf16[4,3,18,512]{3,2,1,0:T(8,128)(2,1)S(1)}, u32[]{:S(2)}, u32[]{:S(2)}) collective-permute-start(bf16[4,3,18,512]{3,2,1,0:T(8,128)(2,1)S(1)} %get-tuple-element.34), channel_id=1, source_target_pairs={{0,96},{1,97},{2,98},{3,99},{4,100},{5,101},{6,102},{7,103},{8,104... | collective-permute-start | bytes 663560 | tf_op jit(solution)/shard_map/ppermute | solution.py:379
  12.5 5.9 %copy-start.6 = (bf16[512,1536]{1,0:T(8,128)(2,1)S(1)}, bf16[512,1536]{1,0:T(8,128)(2,1)}, u32[]{:S(2)}) copy-start(bf16[512,1536]{1,0:T(8,128)(2,1)} %wqkv_ref.1) | copy-start | bytes 4718596
  13.9 4.4 %copy-start = (bf16[32,8,1536]{2,1,0:T(8,128)(2,1)S(1)}, bf16[32,8,1536]{2,1,0:T(8,128)(2,1)}, u32[]{:S(2)}) copy-start(bf16[32,8,1536]{2,1,0:T(8,128)(2,1)} %up_ref.3) | copy-start | bytes 2359300
  13.9 4.4 %copy-start.2 = (s32[2,1,2]{2,1,0:T(1,128)S(1)}, s32[2,1,2]{2,1,0:T(1,128)}, u32[]{:S(2)}) copy-start(s32[2,1,2]{2,1,0:T(1,128)} %region_ref.3) | copy-start | bytes 52
  14.0 4.4 %copy-start.3 = (f32[16]{0:T(128)S(1)}, f32[16]{0:T(128)}, u32[]{:S(2)}) copy-start(f32[16]{0:T(128)} %temper_ref.3) | copy-start | bytes 196
  14.0 4.4 %copy-start.7 = (bf16[512,512]{1,0:T(8,128)(2,1)S(1)}, bf16[512,512]{1,0:T(8,128)(2,1)}, u32[]{:S(2)}) copy-start(bf16[512,512]{1,0:T(8,128)(2,1)} %wo_ref.3) | copy-start | bytes 1572868
  14.0 4.4 %copy-start.9 = (bf16[32,8,512]{2,1,0:T(8,128)(2,1)S(1)}, bf16[32,8,512]{2,1,0:T(8,128)(2,1)}, u32[]{:S(2)}) copy-start(bf16[32,8,512]{2,1,0:T(8,128)(2,1)} %down_ref.1) | copy-start | bytes 786436
  14.0 4.4 %copy-start.10 = (f32[512]{0:T(512)S(1)}, f32[512]{0:T(512)}, u32[]{:S(2)}) copy-start(f32[512]{0:T(512)} %param.20) | copy-start | bytes 6148
  14.0 4.4 %copy-start.11 = (f32[512]{0:T(512)S(1)}, f32[512]{0:T(512)}, u32[]{:S(2)}) copy-start(f32[512]{0:T(512)} %param.21) | copy-start | bytes 6148
  14.0 4.4 %copy-start.12 = (f32[512]{0:T(512)S(1)}, f32[512]{0:T(512)}, u32[]{:S(2)}) copy-start(f32[512]{0:T(512)} %param.22) | copy-start | bytes 6148
  14.2 12.2 %collective-permute-start.3 = (bf16[4,3,18,512]{3,2,1,0:T(8,128)(2,1)S(1)}, bf16[4,3,18,512]{3,2,1,0:T(8,128)(2,1)S(1)}, u32[]{:S(2)}, u32[]{:S(2)}) collective-permute-start(bf16[4,3,18,512]{3,2,1,0:T(8,128)(2,1)S(1)} %get-tuple-element.59), channel_id=1, source_target_pairs={{0,96},{1,97},{2,98},{3,99},{4,100},{5,101},{6,102},{7,103},{8,104... | collective-permute-start | bytes 663560 | tf_op jit(solution)/shard_map/ppermute | solution.py:379
  16.3 10.1 %collective-permute-start.5 = (bf16[4,3,6,512]{3,2,1,0:T(8,128)(2,1)S(1)}, bf16[4,3,6,512]{3,2,1,0:T(8,128)(2,1)S(1)}, u32[]{:S(2)}, u32[]{:S(2)}) collective-permute-start(bf16[4,3,6,512]{3,2,1,0:T(8,128)(2,1)S(1)} %get-tuple-element.57), channel_id=1, source_target_pairs={{0,127},{1,96},{2,97},{3,98},{4,99},{5,100},{6,101},{7,102},{8,103... | collective-permute-start | bytes 221192 | tf_op jit(solution)/shard_map/ppermute | solution.py:379
  17.2 9.2 %collective-permute-start.4 = (bf16[4,3,6,512]{3,2,1,0:T(8,128)(2,1)S(1)}, bf16[4,3,6,512]{3,2,1,0:T(8,128)(2,1)S(1)}, u32[]{:S(2)}, u32[]{:S(2)}) collective-permute-start(bf16[4,3,6,512]{3,2,1,0:T(8,128)(2,1)S(1)} %get-tuple-element.58), channel_id=1, source_target_pairs={{0,31},{1,0},{2,1},{3,2},{4,3},{5,4},{6,5},{7,6},{8,7},{9,8},{10,9... | collective-permute-start | bytes 221192 | tf_op jit(solution)/shard_map/ppermute | solution.py:379
  18.5 8.0 %copy-start.4 = (bf16[512,2048]{1,0:T(8,128)(2,1)S(1)}, bf16[512,2048]{1,0:T(8,128)(2,1)}, u32[]{:S(2)}) copy-start(bf16[512,2048]{1,0:T(8,128)(2,1)} %wup_ref.1) | copy-start | bytes 6291460
  18.5 8.0 %copy-start.5 = (bf16[2048,512]{1,0:T(8,128)(2,1)S(1)}, bf16[2048,512]{1,0:T(8,128)(2,1)}, u32[]{:S(2)}) copy-start(bf16[2048,512]{1,0:T(8,128)(2,1)} %wdn_ref.1) | copy-start | bytes 6291460
  18.5 8.0 %copy-start.13 = (f32[512]{0:T(512)S(1)}, f32[512]{0:T(512)}, u32[]{:S(2)}) copy-start(f32[512]{0:T(512)} %param.28) | copy-start | bytes 6148
  60.9 20.0 %all-to-all-start.1 = ((bf16[64,1,32,128]{3,2,1,0:T(8,128)(2,1)}), bf16[64,1,32,128]{3,2,1,0:T(8,128)(2,1)S(1)}, u32[]{:S(2)}, u32[]{:S(2)}) async-start(bf16[64,1,32,128]{3,2,1,0:T(8,128)(2,1)} %sum_by_region.1), calls=%async_computation.1 | async-start | bytes 1048576 | tf_op jit(solution)/shard_map/all_to_all | solution.py:511
  65.5 15.3 %collective-permute-start.8 = (bf16[4,3,18,512]{3,2,1,0:T(8,128)(2,1)S(1)}, bf16[4,3,18,512]{3,2,1,0:T(8,128)(2,1)S(1)}, u32[]{:S(2)}, u32[]{:S(2)}) collective-permute-start(bf16[4,3,18,512]{3,2,1,0:T(8,128)(2,1)S(1)} %get-tuple-element.49), channel_id=1, source_target_pairs={{0,32},{1,33},{2,34},{3,35},{4,36},{5,37},{6,38},{7,39},{8,40},{9,... | collective-permute-start | bytes 663560 | tf_op jit(solution)/shard_map/ppermute | solution.py:379
  69.4 10.9 %collective-permute-start.6 = (bf16[4,3,6,512]{3,2,1,0:T(8,128)(2,1)S(1)}, bf16[4,3,6,512]{3,2,1,0:T(8,128)(2,1)S(1)}, u32[]{:S(2)}, u32[]{:S(2)}) collective-permute-start(bf16[4,3,6,512]{3,2,1,0:T(8,128)(2,1)S(1)} %get-tuple-element.47), channel_id=1, source_target_pairs={{0,33},{1,34},{2,35},{3,36},{4,37},{5,38},{6,39},{7,40},{8,41},{9,... | collective-permute-start | bytes 221192 | tf_op jit(solution)/shard_map/ppermute | solution.py:379
  69.4 11.5 %collective-permute-start.7 = (bf16[4,3,6,512]{3,2,1,0:T(8,128)(2,1)S(1)}, bf16[4,3,6,512]{3,2,1,0:T(8,128)(2,1)S(1)}, u32[]{:S(2)}, u32[]{:S(2)}) collective-permute-start(bf16[4,3,6,512]{3,2,1,0:T(8,128)(2,1)S(1)} %get-tuple-element.48), channel_id=1, source_target_pairs={{0,1},{1,2},{2,3},{3,4},{4,5},{5,6},{6,7},{7,8},{8,9},{9,10},{10,1... | collective-permute-start | bytes 221192 | tf_op jit(solution)/shard_map/ppermute | solution.py:379
  80.9 2.8 %collective-permute-start.9 = (bf16[64,1,32,128]{3,2,1,0:T(8,128)(2,1)S(1)}, bf16[64,1,32,128]{3,2,1,0:T(8,128)(2,1)S(1)}, u32[]{:S(2)}, u32[]{:S(2)}) collective-permute-start(bf16[64,1,32,128]{3,2,1,0:T(8,128)(2,1)S(1)} %all-to-all-done.1), channel_id=1, source_target_pairs={{0,32},{32,0},{64,96},{96,64},{1,33},{33,1},{65,97},{97,65},{2,34}... | collective-permute-start | bytes 1572872 | tf_op jit(solution)/shard_map/ppermute | solution.py:517

commit v6 on v5

--- a/solution.py
+++ b/solution.py
@@ -33,7 +33,7 @@
     return lax.dot_general(a, b, (((0,), (0,)), ((), ())), preferred_element_type=F32)
 
 
-def head_mean(values):
+def head_mean(values, exact=True):
     wide = 2 * LANES
     rows = lax.broadcasted_iota(jnp.int32, (wide, wide), 0) // HEAD
     cols = lax.broadcasted_iota(jnp.int32, (wide, wide), 1) // HEAD
@@ -42,8 +42,10 @@
     for start in range(0, values.shape[1], wide):
         part = values[:, start : start + wide]
         top = part.astype(BF16)
-        rest = (part - top.astype(F32)).astype(BF16)
-        parts.append(mm(top, block) + mm(rest, block))
+        mean = mm(top, block)
+        if exact:
+            mean += mm((part - top.astype(F32)).astype(BF16), block)
+        parts.append(mean)
     return jnp.concatenate(parts, axis=1)
 
 
@@ -233,7 +235,7 @@
     mixed_ref[...] = hidden
     unit_ref[...] = unit
     d_normed = jnp.zeros((tokens, width), F32)
-    chunk = 2048
+    chunk = 1024
     for c in range(wup_ref.shape[1] // chunk):
         cols = slice(c * chunk, (c + 1) * chunk)
         act, slope = gelu_and_slope(mm(normed, wup_ref[:, cols]))
@@ -284,7 +286,7 @@
     for part, (unit_ref, grad_ref) in enumerate(((qs_ref, dq_ref), (kn_ref, dk_ref))):
         cols = slice(part * width, (part + 1) * width)
         unit, grad = unit_ref[...].astype(F32), grad_ref[...]
-        along = unit * head_mean(grad * unit)
+        along = unit * head_mean(grad * unit, exact=False)
         first, second = scales[part]
         dqkv_ref[:, cols] = (inv_ref[:, cols] * (grad * first - along * second)).astype(BF16)
     ups = factors(region_ref, up_ref, ups_ref)

time: 85.9 us -> 85.7 us (level)
  no operation moved by 1% of the time
where the time goes in v6:
time: 85.7 us; the launch traced here: 85.4 us
  Pallas kernels  25.9 us (30%)
  starting transfers between devices  24 us (28%)
  blocking collectives  18.3 us (21%)
  waiting for transfers between devices  11.5 us (13%)
  other arithmetic  3.45 us (4%)
  local copies, waits for them, and re-layouts  1.32 us (2%)
  between operations  0.9 us (1%)
    all_to_all x1, blocking collectives, local(): terms = lax.all_to_all(terms, AXES, 0, 0, tiled=True)  18.3 us
    ppermute x9, starting transfers between devices, move(): return lax.ppermute(array, ('lat', 'lon'), pairs)  18.1 us
    ppermute x9, waiting for transfers between devices, move(): return lax.ppermute(array, ('lat', 'lon'), pairs)  11.3 us
    pallas_call x1, Pallas kernels, local(): call(attention_kernel, [SMEM] * 2 + [VMEM] * 12, (shape(tokens, width), s...  7.92 us
    pallas_call x1, Pallas kernels, local(): call(backward_kernel, [SMEM] * 2 + [VMEM] * 9, shape(pieces, 2 * count, L...  7.88 us
    pallas_call x1, Pallas kernels, local(): call(feed_kernel, [VMEM] * 9, (shape(*wide), shape(*wide, dtype=BF16), sh...  6.82 us
    all_to_all x1, starting transfers between devices, local(): near = lax.all_to_all(sums, AXES, 0, 0, axis_index_groups=cores, tiled=True)  4.63 us
    pallas_call x1, Pallas kernels, local(): call(scale_kernel, [VMEM] * 2, (shape(regions, rank, width), shape(region...  1.91 us
  transfers between devices with their start and end apart: 11, of which 4 were waited for; matrix products, arithmetic and copies ran while one was open for 3% of the time, Pallas kernels for 9%

profile of v6, /device:TPU:1, one launch (start us, length us, event | category | flops | bytes accessed | tf_op | source)
XLA Modules:
  0.0 85.4 jit_solution(1670150902603917370)
XLA Ops:
  0.6 0.7 convert_element_type.6.land_ref
  1.3 1.1 %copy-done.1 = bf16[4,6,24,500]{3,2,1,0:T(8,128)(2,1)S(1)} copy-done((bf16[4,6,24,500]{3,2,1,0:T(8,128)(2,1)S(1)}, bf16[4,6,24,500]{3,2,1,0:T(8,128)(2,1)}, u32[]{:S(2)}) %copy-start.1) | copy-done | bytes 576024
  2.4 0.3 pack_pixels.1
  2.6 7.2 %collective-permute-start.1 = (bf16[4,3,6,512]{3,2,1,0:T(8,128)(2,1)S(1)}, bf16[4,3,6,512]{3,2,1,0:T(8,128)(2,1)S(1)}, u32[]{:S(2)}, u32[]{:S(2)}) collective-permute-start(bf16[4,3,6,512]{3,2,1,0:T(8,128)(2,1)S(1)} %get-tuple-element.35), channel_id=1, source_target_pairs={{0,31},{1,0},{2,1},{3,2},{4,3},{5,4},{6,5},{7,6},{8,7},{9,8},{10,9... | collective-permute-start | bytes 221192 | tf_op jit(solution)/shard_map/ppermute | solution.py:381
  9.8 0.7 collective-permute-start.2
  10.5 2.0 %collective-permute-start = (bf16[4,3,18,512]{3,2,1,0:T(8,128)(2,1)S(1)}, bf16[4,3,18,512]{3,2,1,0:T(8,128)(2,1)S(1)}, u32[]{:S(2)}, u32[]{:S(2)}) collective-permute-start(bf16[4,3,18,512]{3,2,1,0:T(8,128)(2,1)S(1)} %get-tuple-element.34), channel_id=1, source_target_pairs={{0,96},{1,97},{2,98},{3,99},{4,100},{5,101},{6,102},{7,103},{8,104... | collective-permute-start | bytes 663560 | tf_op jit(solution)/shard_map/ppermute | solution.py:381
  12.5 1.5 %convert.6 = bf16[4,6,24,512]{3,2,1,0:T(8,128)(2,1)S(1)} convert(f32[4,6,24,512]{3,2,1,0:T(8,128)} %param.31) | non-fusion elementwise | flops 294912 | bytes 1769472 | tf_op jit(solution)/shard_map/convert.3
  13.9 0.0 copy-start
  13.9 0.0 copy-start.2
  14.0 0.0 copy-start.3
  14.0 0.0 copy-start.7
  14.0 0.0 copy-start.9
  14.0 0.0 copy-start.10
  14.0 0.0 copy-start.11
  14.0 0.0 copy-start.12
  14.0 0.2 fusion.1
  14.2 2.1 %collective-permute-start.3 = (bf16[4,3,18,512]{3,2,1,0:T(8,128)(2,1)S(1)}, bf16[4,3,18,512]{3,2,1,0:T(8,128)(2,1)S(1)}, u32[]{:S(2)}, u32[]{:S(2)}) collective-permute-start(bf16[4,3,18,512]{3,2,1,0:T(8,128)(2,1)S(1)} %get-tuple-element.59), channel_id=1, source_target_pairs={{0,96},{1,97},{2,98},{3,99},{4,100},{5,101},{6,102},{7,103},{8,104... | collective-permute-start | bytes 663560 | tf_op jit(solution)/shard_map/ppermute | solution.py:381
  16.3 0.9 %collective-permute-start.5 = (bf16[4,3,6,512]{3,2,1,0:T(8,128)(2,1)S(1)}, bf16[4,3,6,512]{3,2,1,0:T(8,128)(2,1)S(1)}, u32[]{:S(2)}, u32[]{:S(2)}) collective-permute-start(bf16[4,3,6,512]{3,2,1,0:T(8,128)(2,1)S(1)} %get-tuple-element.57), channel_id=1, source_target_pairs={{0,127},{1,96},{2,97},{3,98},{4,99},{5,100},{6,101},{7,102},{8,103... | collective-permute-start | bytes 221192 | tf_op jit(solution)/shard_map/ppermute | solution.py:381
  17.2 0.0 collective-permute-done.1.east_ref
  17.2 0.7 collective-permute-start.4
  17.9 0.0 collective-permute-done.2.corner_ref
  17.9 0.4 collective-permute-done.south_ref
  18.4 0.0 copy-done.8
  18.4 0.0 copy-done.6
  18.5 0.0 copy-start.4
  18.5 0.0 copy-start.5
  18.5 0.0 copy-start.13
  18.5 7.9 %attention_forward.1 = (f32[576,512]{1,0:T(8,128)S(1)}, bf16[576,512]{1,0:T(8,128)(2,1)S(1)}, bf16[576,32]{1,0:T(8,128)(2,1)S(1)}, f32[576,1024]{1,0:T(8,128)S(1...) custom-call(s32[2,1,2]{2,1,0:T(1,128)S(1)} %copy-done.2, ...), custom_call_target="tpu_custom_call" | custom-call | flops 1811939328 | bytes 20000000 | tf_op jit(solution)/shard_map/attention_forward/pallas_call | solution.py:439
  26.4 0.0 collective-permute-done.5.corner_ref
  26.4 0.0 collective-permute-done.4.east_ref
  26.4 0.0 collective-permute-done.3.south_ref
  26.5 6.8 %feed_forward.1 = (f32[4,3,18,512]{3,2,1,0:T(8,128)S(1)}, bf16[4,3,18,512]{3,2,1,0:T(8,128)(2,1)S(1)}, bf16[4,3,6,512]{3,2,1,0:T(8,128)(2,1)S(1)}, bf16[4,3,6,51...) custom-call(f32[576,512]{1,0:T(8,128)S(1)} %get-tuple-element.44.hidden_ref, ...), custom_call_target="tpu_custom_call" | custom-call | flops 4831838208 | bytes 20000000 | tf_op jit(solution)/shard_map/feed_forward/pallas_call | solution.py:467
  33.3 7.9 %attention_backward.1 = bf16[128,8,128]{2,1,0:T(8,128)(2,1)S(1)} custom-call(s32[2,1,2]{2,1,0:T(1,128)S(1)} %copy-done.2, f32[16]{0:T(128)S(1)} %copy-done.3, bf16[576,512]{1,0:T(8,128)(2,1)S(1)} %get-tuple-element.37.normed_ref, bf16[576,32]{1,0:T(8,128)(2,1)S(1)} %get-tuple-element.38.low_ref, f32[576,1024]{1,0:T(8,128)S(1)} %get-tuple-element.39.inv_ref, ...), custom_call_target="tpu_custom_call" | custom-call | flops 1207959552 | bytes 12000000 | tf_op jit(solution)/shard_map/attention_backward/pallas_call | solution.py:486
  41.2 18.3 %all_to_all.10 = bf16[128,8,128]{2,1,0:T(8,128)(2,1)S(1)} all-to-all(bf16[128,8,128]{2,1,0:T(8,128)(2,1)S(1)} %attention_backward.1), channel_id=1, replica_groups=mesh['lat'=4,'lon'=32] {'lat','lon'}, dimensions={0} | all-to-all | bytes 524288 | tf_op jit(solution)/shard_map/all_to_all | solution.py:504
  59.5 1.2 %sum_by_region.1 = bf16[64,1,32,128]{3,2,1,0:T(8,128)(2,1)} custom-call(bf16[128,1,8,128]{3,2,1,0:T(8,128)(2,1)S(1)} %bitcast.8), custom_call_target="tpu_custom_call" | custom-call | tf_op jit(solution)/shard_map/sum_by_region/pallas_call | solution.py:505
  60.7 4.6 %all-to-all-start.1 = ((bf16[64,1,32,128]{3,2,1,0:T(8,128)(2,1)}), bf16[64,1,32,128]{3,2,1,0:T(8,128)(2,1)S(1)}, u32[]{:S(2)}, u32[]{:S(2)}) async-start(bf16[64,1,32,128]{3,2,1,0:T(8,128)(2,1)} %sum_by_region.1), calls=%async_computation.1 | async-start | bytes 1048576 | tf_op jit(solution)/shard_map/all_to_all | solution.py:513
  65.3 3.9 %collective-permute-start.8 = (bf16[4,3,18,512]{3,2,1,0:T(8,128)(2,1)S(1)}, bf16[4,3,18,512]{3,2,1,0:T(8,128)(2,1)S(1)}, u32[]{:S(2)}, u32[]{:S(2)}) collective-permute-start(bf16[4,3,18,512]{3,2,1,0:T(8,128)(2,1)S(1)} %get-tuple-element.49), channel_id=1, source_target_pairs={{0,32},{1,33},{2,34},{3,35},{4,36},{5,37},{6,38},{7,39},{8,40},{9,... | collective-permute-start | bytes 663560 | tf_op jit(solution)/shard_map/ppermute | solution.py:381
  69.1 0.0 collective-permute-start.6
  69.2 0.7 collective-permute-start.7
  69.8 10.2 %collective-permute-done.6 = bf16[4,3,6,512]{3,2,1,0:T(8,128)(2,1)S(1)} collective-permute-done((bf16[4,3,6,512]{3,2,1,0:T(8,128)(2,1)S(1)}, bf16[4,3,6,512]{3,2,1,0:T(8,128)(2,1)S(1)}, u32[]{:S(2)}, u32[]{:S(2)}) %collective-permute-start.6) | collective-permute-done | bytes 73760 | tf_op jit(solution)/shard_map/ppermute | solution.py:381
  80.0 0.6 collective-permute-done.7
  80.6 0.0 collective-permute-done.8
  80.6 0.0 all-to-all-done.1
  80.6 1.3 %collective-permute-start.9 = (bf16[64,1,32,128]{3,2,1,0:T(8,128)(2,1)S(1)}, bf16[64,1,32,128]{3,2,1,0:T(8,128)(2,1)S(1)}, u32[]{:S(2)}, u32[]{:S(2)}) collective-permute-start(bf16[64,1,32,128]{3,2,1,0:T(8,128)(2,1)S(1)} %all-to-all-done.1), channel_id=1, source_target_pairs={{0,32},{32,0},{64,96},{96,64},{1,33},{33,1},{65,97},{97,65},{2,34}... | collective-permute-start | bytes 1572872 | tf_op jit(solution)/shard_map/ppermute | solution.py:519
  82.0 0.1 maximum_convert_fusion
  82.1 1.2 %maximum_maximum_fusion = f32[4,6,24,512]{3,2,1,0:T(8,128)} fusion(f32[4,3,18,512]{3,2,1,0:T(8,128)S(1)} %get-tuple-element.53, f32[4,3,6,512]{3,2,1,0:T(8,128)S(1)} %convert_element_type.15, f32[4,3,24,512]{3,2,1,0:T(8,128)S(1)} %maximum_convert_fusion), kind=kLoop, calls=%fused_computation | loop fusion | flops 589824 | bytes 2359296 | tf_op jit(solution)/shard_map/concatenate | solution.py:518
  83.2 0.2 collective-permute-done.9
  83.5 1.9 %scale_steps.1 = (f32[32,8,512]{2,1,0:T(8,128)}, f32[32,8,1536]{2,1,0:T(8,128)}) custom-call(bf16[2,2,16,32,128]{4,3,2,1,0:T(8,128)(2,1)S(1)} %bitcast.7, bf16[2,2,16,32,128]{4,3,2,1,0:T(8,128)(2,1)S(1)} %bitcast.9), custom_call_target="tpu_custom_call" | custom-call | tf_op jit(solution)/shard_map/scale_steps/pallas_call | solution.py:522
  (16 shorter events, 0.1 us)
Async XLA Ops:
  1.3 1.1 %copy-start.1 = (bf16[4,6,24,500]{3,2,1,0:T(8,128)(2,1)S(1)}, bf16[4,6,24,500]{3,2,1,0:T(8,128)(2,1)}, u32[]{:S(2)}) copy-start(bf16[4,6,24,500]{3,2,1,0:T(8,128)(2,1)} %pixels_ref.1) | copy-start | bytes 1728004
  2.4 16.0 %copy-start.8 = (bf16[500,512]{1,0:T(8,128)(2,1)S(1)}, bf16[500,512]{1,0:T(8,128)(2,1)}, u32[]{:S(2)}) copy-start(bf16[500,512]{1,0:T(8,128)(2,1)} %wp_ref.1) | copy-start | bytes 1536004
  2.6 14.6 %collective-permute-start.1 = (bf16[4,3,6,512]{3,2,1,0:T(8,128)(2,1)S(1)}, bf16[4,3,6,512]{3,2,1,0:T(8,128)(2,1)S(1)}, u32[]{:S(2)}, u32[]{:S(2)}) collective-permute-start(bf16[4,3,6,512]{3,2,1,0:T(8,128)(2,1)S(1)} %get-tuple-element.35), channel_id=1, source_target_pairs={{0,31},{1,0},{2,1},{3,2},{4,3},{5,4},{6,5},{7,6},{8,7},{9,8},{10,9... | collective-permute-start | bytes 221192 | tf_op jit(solution)/shard_map/ppermute | solution.py:381
  9.8 8.1 %collective-permute-start.2 = (bf16[4,3,6,512]{3,2,1,0:T(8,128)(2,1)S(1)}, bf16[4,3,6,512]{3,2,1,0:T(8,128)(2,1)S(1)}, u32[]{:S(2)}, u32[]{:S(2)}) collective-permute-start(bf16[4,3,6,512]{3,2,1,0:T(8,128)(2,1)S(1)} %get-tuple-element.36), channel_id=1, source_target_pairs={{0,127},{1,96},{2,97},{3,98},{4,99},{5,100},{6,101},{7,102},{8,103... | collective-permute-start | bytes 221192 | tf_op jit(solution)/shard_map/ppermute | solution.py:381
  10.5 7.9 %collective-permute-start = (bf16[4,3,18,512]{3,2,1,0:T(8,128)(2,1)S(1)}, bf16[4,3,18,512]{3,2,1,0:T(8,128)(2,1)S(1)}, u32[]{:S(2)}, u32[]{:S(2)}) collective-permute-start(bf16[4,3,18,512]{3,2,1,0:T(8,128)(2,1)S(1)} %get-tuple-element.34), channel_id=1, source_target_pairs={{0,96},{1,97},{2,98},{3,99},{4,100},{5,101},{6,102},{7,103},{8,104... | collective-permute-start | bytes 663560 | tf_op jit(solution)/shard_map/ppermute | solution.py:381
  12.5 5.9 %copy-start.6 = (bf16[512,1536]{1,0:T(8,128)(2,1)S(1)}, bf16[512,1536]{1,0:T(8,128)(2,1)}, u32[]{:S(2)}) copy-start(bf16[512,1536]{1,0:T(8,128)(2,1)} %wqkv_ref.1) | copy-start | bytes 4718596
  13.9 4.4 %copy-start = (bf16[32,8,1536]{2,1,0:T(8,128)(2,1)S(1)}, bf16[32,8,1536]{2,1,0:T(8,128)(2,1)}, u32[]{:S(2)}) copy-start(bf16[32,8,1536]{2,1,0:T(8,128)(2,1)} %up_ref.3) | copy-start | bytes 2359300
  13.9 4.4 %copy-start.2 = (s32[2,1,2]{2,1,0:T(1,128)S(1)}, s32[2,1,2]{2,1,0:T(1,128)}, u32[]{:S(2)}) copy-start(s32[2,1,2]{2,1,0:T(1,128)} %region_ref.3) | copy-start | bytes 52
  14.0 4.4 %copy-start.3 = (f32[16]{0:T(128)S(1)}, f32[16]{0:T(128)}, u32[]{:S(2)}) copy-start(f32[16]{0:T(128)} %temper_ref.3) | copy-start | bytes 196
  14.0 4.4 %copy-start.7 = (bf16[512,512]{1,0:T(8,128)(2,1)S(1)}, bf16[512,512]{1,0:T(8,128)(2,1)}, u32[]{:S(2)}) copy-start(bf16[512,512]{1,0:T(8,128)(2,1)} %wo_ref.3) | copy-start | bytes 1572868
  14.0 4.4 %copy-start.9 = (bf16[32,8,512]{2,1,0:T(8,128)(2,1)S(1)}, bf16[32,8,512]{2,1,0:T(8,128)(2,1)}, u32[]{:S(2)}) copy-start(bf16[32,8,512]{2,1,0:T(8,128)(2,1)} %down_ref.1) | copy-start | bytes 786436
  14.0 4.4 %copy-start.10 = (f32[512]{0:T(512)S(1)}, f32[512]{0:T(512)}, u32[]{:S(2)}) copy-start(f32[512]{0:T(512)} %param.20) | copy-start | bytes 6148
  14.0 4.4 %copy-start.11 = (f32[512]{0:T(512)S(1)}, f32[512]{0:T(512)}, u32[]{:S(2)}) copy-start(f32[512]{0:T(512)} %param.21) | copy-start | bytes 6148
  14.0 4.4 %copy-start.12 = (f32[512]{0:T(512)S(1)}, f32[512]{0:T(512)}, u32[]{:S(2)}) copy-start(f32[512]{0:T(512)} %param.22) | copy-start | bytes 6148
  14.2 12.2 %collective-permute-start.3 = (bf16[4,3,18,512]{3,2,1,0:T(8,128)(2,1)S(1)}, bf16[4,3,18,512]{3,2,1,0:T(8,128)(2,1)S(1)}, u32[]{:S(2)}, u32[]{:S(2)}) collective-permute-start(bf16[4,3,18,512]{3,2,1,0:T(8,128)(2,1)S(1)} %get-tuple-element.59), channel_id=1, source_target_pairs={{0,96},{1,97},{2,98},{3,99},{4,100},{5,101},{6,102},{7,103},{8,104... | collective-permute-start | bytes 663560 | tf_op jit(solution)/shard_map/ppermute | solution.py:381
  16.3 10.1 %collective-permute-start.5 = (bf16[4,3,6,512]{3,2,1,0:T(8,128)(2,1)S(1)}, bf16[4,3,6,512]{3,2,1,0:T(8,128)(2,1)S(1)}, u32[]{:S(2)}, u32[]{:S(2)}) collective-permute-start(bf16[4,3,6,512]{3,2,1,0:T(8,128)(2,1)S(1)} %get-tuple-element.57), channel_id=1, source_target_pairs={{0,127},{1,96},{2,97},{3,98},{4,99},{5,100},{6,101},{7,102},{8,103... | collective-permute-start | bytes 221192 | tf_op jit(solution)/shard_map/ppermute | solution.py:381
  17.2 9.2 %collective-permute-start.4 = (bf16[4,3,6,512]{3,2,1,0:T(8,128)(2,1)S(1)}, bf16[4,3,6,512]{3,2,1,0:T(8,128)(2,1)S(1)}, u32[]{:S(2)}, u32[]{:S(2)}) collective-permute-start(bf16[4,3,6,512]{3,2,1,0:T(8,128)(2,1)S(1)} %get-tuple-element.58), channel_id=1, source_target_pairs={{0,31},{1,0},{2,1},{3,2},{4,3},{5,4},{6,5},{7,6},{8,7},{9,8},{10,9... | collective-permute-start | bytes 221192 | tf_op jit(solution)/shard_map/ppermute | solution.py:381
  18.5 8.0 %copy-start.4 = (bf16[512,2048]{1,0:T(8,128)(2,1)S(1)}, bf16[512,2048]{1,0:T(8,128)(2,1)}, u32[]{:S(2)}) copy-start(bf16[512,2048]{1,0:T(8,128)(2,1)} %wup_ref.1) | copy-start | bytes 6291460
  18.5 8.0 %copy-start.5 = (bf16[2048,512]{1,0:T(8,128)(2,1)S(1)}, bf16[2048,512]{1,0:T(8,128)(2,1)}, u32[]{:S(2)}) copy-start(bf16[2048,512]{1,0:T(8,128)(2,1)} %wdn_ref.1) | copy-start | bytes 6291460
  18.5 8.0 %copy-start.13 = (f32[512]{0:T(512)S(1)}, f32[512]{0:T(512)}, u32[]{:S(2)}) copy-start(f32[512]{0:T(512)} %param.28) | copy-start | bytes 6148
  60.7 20.0 %all-to-all-start.1 = ((bf16[64,1,32,128]{3,2,1,0:T(8,128)(2,1)}), bf16[64,1,32,128]{3,2,1,0:T(8,128)(2,1)S(1)}, u32[]{:S(2)}, u32[]{:S(2)}) async-start(bf16[64,1,32,128]{3,2,1,0:T(8,128)(2,1)} %sum_by_region.1), calls=%async_computation.1 | async-start | bytes 1048576 | tf_op jit(solution)/shard_map/all_to_all | solution.py:513
  65.3 15.3 %collective-permute-start.8 = (bf16[4,3,18,512]{3,2,1,0:T(8,128)(2,1)S(1)}, bf16[4,3,18,512]{3,2,1,0:T(8,128)(2,1)S(1)}, u32[]{:S(2)}, u32[]{:S(2)}) collective-permute-start(bf16[4,3,18,512]{3,2,1,0:T(8,128)(2,1)S(1)} %get-tuple-element.49), channel_id=1, source_target_pairs={{0,32},{1,33},{2,34},{3,35},{4,36},{5,37},{6,38},{7,39},{8,40},{9,... | collective-permute-start | bytes 663560 | tf_op jit(solution)/shard_map/ppermute | solution.py:381
  69.1 10.9 %collective-permute-start.6 = (bf16[4,3,6,512]{3,2,1,0:T(8,128)(2,1)S(1)}, bf16[4,3,6,512]{3,2,1,0:T(8,128)(2,1)S(1)}, u32[]{:S(2)}, u32[]{:S(2)}) collective-permute-start(bf16[4,3,6,512]{3,2,1,0:T(8,128)(2,1)S(1)} %get-tuple-element.47), channel_id=1, source_target_pairs={{0,33},{1,34},{2,35},{3,36},{4,37},{5,38},{6,39},{7,40},{8,41},{9,... | collective-permute-start | bytes 221192 | tf_op jit(solution)/shard_map/ppermute | solution.py:381
  69.2 11.5 %collective-permute-start.7 = (bf16[4,3,6,512]{3,2,1,0:T(8,128)(2,1)S(1)}, bf16[4,3,6,512]{3,2,1,0:T(8,128)(2,1)S(1)}, u32[]{:S(2)}, u32[]{:S(2)}) collective-permute-start(bf16[4,3,6,512]{3,2,1,0:T(8,128)(2,1)S(1)} %get-tuple-element.48), channel_id=1, source_target_pairs={{0,1},{1,2},{2,3},{3,4},{4,5},{5,6},{6,7},{7,8},{8,9},{9,10},{10,1... | collective-permute-start | bytes 221192 | tf_op jit(solution)/shard_map/ppermute | solution.py:381
  80.6 2.8 %collective-permute-start.9 = (bf16[64,1,32,128]{3,2,1,0:T(8,128)(2,1)S(1)}, bf16[64,1,32,128]{3,2,1,0:T(8,128)(2,1)S(1)}, u32[]{:S(2)}, u32[]{:S(2)}) collective-permute-start(bf16[64,1,32,128]{3,2,1,0:T(8,128)(2,1)S(1)} %all-to-all-done.1), channel_id=1, source_target_pairs={{0,32},{32,0},{64,96},{96,64},{1,33},{33,1},{65,97},{97,65},{2,34}... | collective-permute-start | bytes 1572872 | tf_op jit(solution)/shard_map/ppermute | solution.py:519
